TPU v7x, 512 devices: a whole 4x8x8 slice. The times are simulated.
512 devices in a mesh: dp: 64 (over x, y_hi, z), tensor: 8 (over y_lo, core).
Axes of the slice: x: 4, y: 8 (y_hi: 2, y_lo: 4; y = y_hi * 4 + y_lo), z: 8, core: 2. Of those that a mesh axis runs over, the one named last changes fastest.
Arguments:
- query_inputs: bfloat16 [4, 256, 32, 8192], P(None, 'dp', None, 'tensor'), may hold values from -6 to 6
- query_output_grads: bfloat16 [4, 256, 32, 8192], P(None, 'dp', None, 'tensor'), may hold values from -6 to 6
- in_projection: bfloat16 [4, 64, 8192], P(None, None, 'tensor'), may hold values from -0.0625 to 0.0625
- out_projection: bfloat16 [4, 64, 8192], P(None, None, 'tensor'), may hold values from -0.0625 to 0.0625
- train_grads: bfloat16 [16384, 16384], P(('dp', 'tensor')), may hold values from -0.01171875 to 0.01171875
- lengths: int32 [256], P('dp'), may hold values from 1 to 32
- loss_mask: int32 [256, 32], P('dp'), may hold values 0 or 1
- domains: int32 [256, 1], replicated, may hold values from 0 to 7
Outputs:
- scores: float32 [16384, 256], P(('dp', 'tensor'))
- domain_influence: float32 [16384, 8], P(('dp', 'tensor'))
Inputs may be any that keep to these rules, and one draw needn't show every extreme that they name: `domains`: every domain has at least one query example.
All inputs are finite; a program needn't handle non-finite values. No bound on the sum of `loss_mask` on one device may be relied on, other than what follows from the above.
Results may differ from a plain program's by a relative error of at most 0.0029.
Values may be sent and summed in bfloat16 or wider, within the bound.
No kernel may reach another device: no remote copies, remote signals or barrier semaphores. Data moves between devices by JAX's collectives and lax.ppermute only.
A program may use at most 64 MiB of HBM per device.

v0:
```python
import jax
import jax.numpy as jnp
from jax import lax
from jax.sharding import PartitionSpec as P

DOMAINS = 8


def row_products(rows, shard_rows):
    return lax.dot_general(
        rows, shard_rows, (((1,), (1,)), ((), ())), preferred_element_type=jnp.float32
    )


def body(
    query_inputs,
    query_output_grads,
    in_projection,
    out_projection,
    train_grads,
    lengths,
    loss_mask,
    domains,
):
    highest = lax.Precision.HIGHEST
    positions = lax.broadcasted_iota(jnp.int32, loss_mask.shape, 1)
    token_weight = jnp.where(positions < lengths[:, None], loss_mask, 0).astype(jnp.float32)
    in_part = jnp.einsum(
        "lqsd,lkd->lqsk", query_inputs, in_projection, preferred_element_type=jnp.float32
    )
    out_part = jnp.einsum(
        "lqsd,lkd->lqsk", query_output_grads, out_projection, preferred_element_type=jnp.float32
    )
    in_factor, out_factor = lax.psum((in_part, out_part), "tensor")
    weighted = out_factor * token_weight[None, :, :, None]
    outer = jnp.einsum("lqso,lqsi->qloi", weighted, in_factor, precision=highest)
    query_grads = outer.reshape(outer.shape[0], -1).astype(jnp.bfloat16)
    scores = row_products(train_grads, lax.all_gather(query_grads, "dp", axis=0, tiled=True))
    onehot = (domains == lax.broadcasted_iota(jnp.int32, (1, DOMAINS), 1)).astype(jnp.float32)
    counts = jnp.sum(onehot, axis=0)
    domain_influence = jnp.dot(scores, onehot, precision=highest) / counts[None, :]
    return (scores, domain_influence)


def solution(mesh):
    return jax.shard_map(
        body,
        mesh=mesh,
        in_specs=(
            P(None, "dp", None, "tensor"),
            P(None, "dp", None, "tensor"),
            P(None, None, "tensor"),
            P(None, None, "tensor"),
            P(("dp", "tensor"), None),
            P("dp"),
            P("dp", None),
            P(),
        ),
        out_specs=(P(("dp", "tensor"), None), P(("dp", "tensor"), None)),
        check_vma=False,
    )
```

profile of v0, /device:TPU:1, one launch (start us, length us, event | category | flops | bytes accessed | tf_op | source)
XLA Modules:
  0.0 314.1 jit_solution(12278639232750141473)
XLA Ops:
  7.2 0.0 copy-start
  7.2 0.0 all-reduce.3.cloned.1.call-start
  7.2 2.5 fusion
  9.8 2.5 fusion.2
  12.3 0.0 all-reduce.3.cloned.1.call-update
  12.3 0.0 all-gather.3.cloned.1.call-start
  12.3 0.8 select_convert_fusion
  13.1 79.8 %all-reduce.3.cloned.1.call-done = (f32[4,4,32,64]{3,2,0,1:T(8,128)}, f32[4,4,32,64]{3,2,0,1:T(8,128)}) async-done(((f32[4,4,32,64]{3,2,0,1:T(8,128)}, f32[4,4,32,64]{3,2,0,1:T(8,128)}), (f32[4,4,32,64]{3,2,0,1:T(8,128)}, f32[4,4,32,64]{3,2,0,1:T(8,128)})) %all-reduce.3.cloned.1.call-update) | async-done | bytes 262160 | tf_op jit(solution)/shard_map/psum | solution.py:34
  92.9 2.1 convolution_convert_fusion
  95.0 0.8 reshape.9
  95.9 0.0 all-gather.3.cloned.1.call-update
  95.9 0.8 convert_reduce_fusion
  96.7 191.3 %all-gather.3.cloned.1.call-done = bf16[64,4,16384]{2,1,0:T(4,128)(2,1)} async-done(((bf16[1,4,16384]{2,1,0:T(4,128)(2,1)}), bf16[64,4,16384]{2,1,0:T(4,128)(2,1)}) %all-gather.3.cloned.1.call-update) | async-done | bytes 8388624 | tf_op jit(solution)/shard_map/all_gather | solution.py:38
  287.9 12.5 %reshape.10 = bf16[256,16384]{1,0:T(8,128)(2,1)} reshape(bf16[64,4,16384]{2,1,0:T(4,128)(2,1)} %all-gather.3.cloned.1.call-done) | data formatting | bytes 16777216
  300.5 0.0 copy-done
  300.5 0.0 copy-start.2
  300.5 6.0 %fusion.9 = f32[256,32]{0,1:T(8,128)S(1)} fusion(bf16[256,16384]{1,0:T(8,128)(2,1)} %reshape.10, bf16[32,16384]{1,0:T(8,128)(2,1)S(1)} %copy-done), kind=kOutput, calls=%fused_computation.15 | convolution fusion | flops 268435456 | bytes 9469952 | tf_op jit(solution)/shard_map/dot_general | solution.py:10
  306.5 0.0 copy-done.2
  306.5 0.0 copy-start.1
  306.5 0.7 convolution_divide_fusion
  307.2 0.0 copy-done.1
Async XLA Ops:
  7.2 293.3 %copy-start = (bf16[32,16384]{1,0:T(8,128)(2,1)S(1)}, bf16[32,16384]{1,0:T(8,128)(2,1)}, u32[]{:S(2)}) copy-start(bf16[32,16384]{1,0:T(8,128)(2,1)} %param.12) | copy-start | bytes 3145732
  7.2 85.7 %all-reduce.3.cloned.1.call-start = ((), (), s32[]{:S(2)}) async-start(), calls=%async_computation.1 | async-start | bytes 1048576 | tf_op jit(solution)/shard_map/psum | solution.py:34
  12.3 275.7 %all-gather.3.cloned.1.call-start = ((), (), s32[]{:S(2)}) async-start(), calls=%async_computation | async-start | bytes 8519680 | tf_op jit(solution)/shard_map/all_gather | solution.py:38
  300.5 6.0 %copy-start.2 = (s32[256,1]{0,1:T(1,128)S(1)}, s32[256,1]{0,1:T(1,128)}, u32[]{:S(2)}) copy-start(s32[256,1]{0,1:T(1,128)} %param.15) | copy-start | bytes 3076
  306.5 0.7 copy-start.1
Sparse Core Ops, SparseCore 0:
  12.4 80.4 all-reduce.2
  98.2 189.6 all-gather.2
where the time goes:
time: 316 us; the launch traced here: 314 us
  waiting for transfers between devices  271 us (86%)
  between operations  14.1 us (4%)
  matrix products  13.9 us (4%)
  local copies, waits for them, and re-layouts  13.4 us (4%)
    all_gather x1, waiting for transfers between devices, body(): lax.all_gather(query_grads, 'dp', axis=0, tiled=True)  191 us
    psum x1, waiting for transfers between devices, body(): in_factor, out_factor = lax.psum((in_part, out_part), 'tensor')  79.8 us
    unnamed x8, local copies, waits for them, and re-layouts  13.4 us
  transfers between devices with their start and end apart: 2, of which 2 were waited for; matrix products, arithmetic and copies ran while one was open for 0% of the time, Pallas kernels for 0%

commit v1 on v0

v1 whole, which is shorter than its diff:
```python
import functools

import jax
import jax.numpy as jnp
from jax import lax
from jax.experimental import pallas as pl
from jax.experimental.pallas import tpu as pltpu
from jax.sharding import PartitionSpec as P

LAYERS = 4
SEQ = 32
WIDTH = 64
DOMAINS = 8
AXES = ("dp", "tensor")
NX, NY, NZ, NC = 4, 8, 8, 2
LANES = 128
PAIRS = WIDTH * WIDTH // LANES


def flat(x, y, z, c):
    return (x * 16 + (y // 4) * 8 + z) * 8 + (y % 4) * 2 + c


def places():
    return [(x, y, z, c) for x in range(NX) for y in range(NY) for z in range(NZ) for c in range(NC)]


def partition(members):
    groups, seen = [], set()
    for place in places():
        group = [flat(*m) for m in members(*place)]
        if group[0] not in seen:
            seen.update(group)
            groups.append(group)
    return groups


def along_x(x, y, z, c):
    return [(i, y, z, c) for i in range(NX)]


def far_members(x, y, z, c):
    return [
        ((x & 1) | (xh << 1), (h << 2) | ((y & 3) ^ (((x >> 1) ^ xh) << 1)), (z & 1) | (zz << 1), c)
        for xh in range(2)
        for h in range(2)
        for zz in range(4)
    ]


def near_members(x, y, z, c):
    return [
        ((x & 2) | xl, y ^ ((x & 1) ^ xl), (z & 6) | zl, c)
        for xl in range(2)
        for zl in range(2)
    ]


def project_kernel(place_ref, in_ref, grad_ref, in_proj_ref, out_proj_ref, out_ref):
    def side(rows_ref, proj_ref):
        rows = rows_ref[0].reshape(-1, rows_ref.shape[-1])
        return lax.dot_general(
            rows, proj_ref[0], (((1,), (1,)), ((), ())), preferred_element_type=jnp.float32
        )

    out_ref[0] = jnp.concatenate([side(in_ref, in_proj_ref), side(grad_ref, out_proj_ref)], axis=1)


def project(place, query_inputs, query_output_grads, in_projection, out_projection):
    _, queries, seq, depth = query_inputs.shape
    rows = pl.BlockSpec((1, queries, seq, depth), lambda j, place: (place[0] ^ j, 0, 0, 0))
    proj = pl.BlockSpec((1, WIDTH, depth), lambda j, place: (place[0] ^ j, 0, 0))
    return pl.pallas_call(
        project_kernel,
        out_shape=jax.ShapeDtypeStruct((LAYERS, queries * seq, 2 * WIDTH), jnp.float32),
        grid_spec=pltpu.PrefetchScalarGridSpec(
            num_scalar_prefetch=1,
            grid=(LAYERS,),
            in_specs=[rows, rows, proj, proj],
            out_specs=pl.BlockSpec((1, queries * seq, 2 * WIDTH), lambda j, place: (j, 0, 0)),
        ),
        compiler_params=pltpu.CompilerParams(vmem_limit_bytes=16 * 1024 * 1024),
        name="project",
    )(place, query_inputs, query_output_grads, in_projection, out_projection)


def outer_kernel(place_ref, lengths_ref, mask_ref, parts_ref, out_ref, rows_ref):
    core = place_ref[1]
    total = parts_ref[0]
    for part in range(1, parts_ref.shape[0]):
        total = total + parts_ref[part]
    row = lax.broadcasted_iota(jnp.int32, (SEQ, SEQ), 0)
    col = lax.broadcasted_iota(jnp.int32, (SEQ, SEQ), 1)
    first = lax.broadcasted_iota(jnp.int32, (SEQ, LANES), 1) < WIDTH
    for k in range(2):
        mask = jnp.where(core == 0, mask_ref[k : k + 1, :], mask_ref[2 + k : 3 + k, :])
        kept = (row == col) & (col < lengths_ref[2 * core + k])
        weight = jnp.sum(jnp.where(kept, mask, 0).astype(jnp.float32), axis=1, keepdims=True)
        factors = total[k * SEQ : (k + 1) * SEQ]
        inner = factors[:, :WIDTH]
        inner = jnp.concatenate([inner, inner], axis=1)
        weighted = factors[:, WIDTH:] * weight
        for p in range(PAIRS):
            low = jnp.broadcast_to(weighted[:, 2 * p : 2 * p + 1], (SEQ, LANES))
            high = jnp.broadcast_to(weighted[:, 2 * p + 1 : 2 * p + 2], (SEQ, LANES))
            product = jnp.where(first, low, high) * inner
            rows_ref[2 * p + k : 2 * p + k + 1, :] = jnp.sum(product, axis=0, keepdims=True)
    out_ref[...] = rows_ref[...].astype(jnp.bfloat16)


def outer(place, lengths, loss_mask, parts):
    smem = pl.BlockSpec(memory_space=pltpu.SMEM)
    vmem = pl.BlockSpec(memory_space=pltpu.VMEM)
    return pl.pallas_call(
        outer_kernel,
        out_shape=jax.ShapeDtypeStruct((2 * PAIRS, LANES), jnp.bfloat16),
        in_specs=[smem, smem, vmem, vmem],
        out_specs=vmem,
        scratch_shapes=[pltpu.VMEM((2 * PAIRS, LANES), jnp.float32)],
        compiler_params=pltpu.CompilerParams(vmem_limit_bytes=16 * 1024 * 1024),
        name="outer",
    )(place, lengths, loss_mask, parts)


def finish_kernel(parts_ref, domains_ref, scores_ref, influence_ref):
    total = parts_ref[0]
    for part in range(1, parts_ref.shape[0]):
        total = total + parts_ref[part]
    queries = total.shape[1]
    here = lax.broadcasted_iota(jnp.int32, (queries, queries), 0)
    there = lax.broadcasted_iota(jnp.int32, (queries, queries), 1)

    def bit(value, at, to, bits=1):
        return ((value >> at) & ((1 << bits) - 1)) << to

    target = (
        bit(here, 7, 1) + bit(here, 6, 6) + bit(here, 5, 2) + bit(here, 4, 0) + bit(here, 3, 7)
        + bit(here, 2, 5) + bit(here, 0, 3, 2)
    )
    place = (target == there).astype(jnp.float32)
    scores = jnp.dot(total, place, precision=lax.Precision.HIGHEST, preferred_element_type=jnp.float32)
    scores_ref[...] = scores
    lane = lax.broadcasted_iota(jnp.int32, (queries, DOMAINS), 1)
    onehot = (domains_ref[...] == lane).astype(jnp.float32)
    counts = jnp.sum(onehot, axis=0, keepdims=True)
    sums = jnp.dot(scores, onehot, precision=lax.Precision.HIGHEST, preferred_element_type=jnp.float32)
    influence_ref[...] = sums / counts


def finish(parts, domains):
    _, rows, queries = parts.shape
    return pl.pallas_call(
        finish_kernel,
        out_shape=(
            jax.ShapeDtypeStruct((rows, queries), jnp.float32),
            jax.ShapeDtypeStruct((rows, DOMAINS), jnp.float32),
        ),
        compiler_params=pltpu.CompilerParams(vmem_limit_bytes=16 * 1024 * 1024),
        name="finish",
    )(parts, domains)


def score_kernel(place_ref, own_ref, first_ref, second_ref, third_ref, near_ref, mate_ref, out_ref, queries_ref):
    x, core = place_ref[0], place_ref[1]
    near, pairs, rows, lanes = near_ref.shape
    half = near * rows
    for block_ref, side in ((near_ref, core), (mate_ref, 1 - core)):
        for n in range(near):
            at = pl.ds(pl.multiple_of(side * half + n * rows, rows), rows)
            for p in range(pairs):
                queries_ref[at, p * lanes : (p + 1) * lanes] = block_ref[n, p]
    for step, rows_ref in enumerate((own_ref, first_ref, second_ref, third_ref)):
        out_ref[pl.ds(x ^ step, 1)] = lax.dot_general(
            rows_ref[...], queries_ref[...], (((1,), (1,)), ((), ())), preferred_element_type=jnp.float32
        )[None]


def score(place, blocks, near, mate):
    smem = pl.BlockSpec(memory_space=pltpu.SMEM)
    vmem = pl.BlockSpec(memory_space=pltpu.VMEM)
    rows, width = blocks[0].shape
    queries = 2 * near.shape[0] * near.shape[2]
    return pl.pallas_call(
        score_kernel,
        out_shape=jax.ShapeDtypeStruct((NX, rows, queries), jnp.float32),
        in_specs=[smem] + [vmem] * 6,
        out_specs=vmem,
        scratch_shapes=[pltpu.VMEM((queries, width), jnp.bfloat16)],
        compiler_params=pltpu.CompilerParams(vmem_limit_bytes=24 * 1024 * 1024),
        name="score",
    )(place, *blocks, near, mate)


def spread(block, members):
    groups = partition(members)
    copies = jnp.broadcast_to(block[None], (len(groups[0]),) + block.shape)
    return lax.all_to_all(copies, AXES, 0, 0, axis_index_groups=groups)


def body(
    query_inputs,
    query_output_grads,
    in_projection,
    out_projection,
    train_grads,
    lengths,
    loss_mask,
    domains,
):
    dp, tensor = lax.axis_index("dp"), lax.axis_index("tensor")
    x, core = dp >> 4, tensor & 1
    layer = x ^ (tensor >> 1)
    place = jnp.stack([x, core]).astype(jnp.int32)

    width = train_grads.shape[1] // LAYERS

    def columns(step):
        return lax.dynamic_slice_in_dim(train_grads, (layer ^ step) * width, width, axis=1)

    blocks = [columns(0)]
    for step in range(1, NX):
        partners = [(flat(a, y, z, c), flat(a ^ step, y, z, c)) for a, y, z, c in places()]
        blocks.append(lax.ppermute(columns(step), AXES, partners))

    parts = project(place, query_inputs, query_output_grads, in_projection, out_projection)
    parts = parts.reshape(2 * LAYERS, -1, 2 * WIDTH)
    parts = lax.all_to_all(parts, "tensor", 0, 0)
    gradient = outer(place, lengths, loss_mask, parts)

    far = spread(gradient, far_members)
    blocks, far = lax.optimization_barrier((blocks, far))
    far = far.transpose(1, 0, 2).reshape(PAIRS, -1, LANES)
    near = spread(far, near_members)
    mates = [(flat(a, y, z, c), flat(a, y, z, 1 - c)) for a, y, z, c in places()]
    mate = lax.ppermute(near, AXES, mates)

    parts = score(place, blocks, near, mate)
    parts = lax.all_to_all(parts, AXES, 0, 0, axis_index_groups=partition(along_x))
    return finish(parts, domains)


def solution(mesh):
    return jax.shard_map(
        body,
        mesh=mesh,
        in_specs=(
            P(None, "dp", None, "tensor"),
            P(None, "dp", None, "tensor"),
            P(None, None, "tensor"),
            P(None, None, "tensor"),
            P(("dp", "tensor"), None),
            P("dp"),
            P("dp", None),
            P(),
        ),
        out_specs=(P(("dp", "tensor"), None), P(("dp", "tensor"), None)),
        check_vma=False,
    )
```

time: 316 us -> 103 us (0.33)
  waiting for transfers between devices: 271 us -> 29.6 us
  starting transfers between devices: 0.08 us -> 40.5 us
  blocking collectives: 0 us -> 15.6 us
  matrix products: 13.9 us -> 0 us
  between operations: 14.1 us -> 0.75 us
  Pallas kernels: 0 us -> 9.61 us
  local copies, waits for them, and re-layouts: 13.4 us -> 6.5 us
    all_gather x1 -> x0, waiting for transfers between devices: 191 us -> none  [body(): lax.all_gather(query_grads, 'dp', axis=0, tiled=True)]
    psum x1 -> x0, waiting for transfers between devices: 79.8 us -> none  [body(): in_factor, out_factor = lax.psum((in_part, out_part), 'tensor')]
    all_to_all x0 -> x3, starting transfers between devices: none -> 23.7 us  [the longest x1 10.2 us: body(): parts = lax.all_to_all(parts, 'tensor', 0, 0)]
    ppermute x0 -> x4, starting transfers between devices: none -> 16.8 us  [the longest x3 12 us: body(): blocks.append(lax.ppermute(columns(step), AXES, partners))]
    ppermute x0 -> x4, waiting for transfers between devices: none -> 16.2 us  [the longest x3 13.9 us: body(): blocks.append(lax.ppermute(columns(step), AXES, partners))]
    all_to_all x0 -> x1, blocking collectives: none -> 15.6 us  [spread(): return lax.all_to_all(copies, AXES, 0, 0, axis_index_groups=groups)]
    dot_general x5 -> x0, matrix products: 13.9 us -> none  [the longest x1 5.99 us: row_products(): lax.dot_general(rows, shard_rows, (((1,), (1,)), ((), ())), preferred_ele...]
    all_to_all x0 -> x3, waiting for transfers between devices: none -> 13.4 us  [the longest x1 8.72 us: body(): parts = lax.all_to_all(parts, 'tensor', 0, 0)]
  transfers between devices with their start and end apart: 2 -> 7, of which waited for: 2 -> 5; matrix products, arithmetic and copies ran while one was open for 0% -> 0% of each run, Pallas kernels for 0% -> 0%
where the time goes in v1:
time: 103 us
  starting transfers between devices  40.5 us (39%)
  waiting for transfers between devices  29.6 us (29%)
  blocking collectives  15.6 us (15%)
  Pallas kernels  9.61 us (9%)
  local copies, waits for them, and re-layouts  6.5 us (6%)
    all_to_all x1, blocking collectives, spread(): return lax.all_to_all(copies, AXES, 0, 0, axis_index_groups=groups)  15.6 us
    ppermute x3, waiting for transfers between devices, body(): blocks.append(lax.ppermute(columns(step), AXES, partners))  13.9 us
    ppermute x3, starting transfers between devices, body(): blocks.append(lax.ppermute(columns(step), AXES, partners))  12 us
    all_to_all x1, starting transfers between devices, body(): parts = lax.all_to_all(parts, 'tensor', 0, 0)  10.2 us
    all_to_all x1, starting transfers between devices, spread(): return lax.all_to_all(copies, AXES, 0, 0, axis_index_groups=groups)  10 us
    all_to_all x1, waiting for transfers between devices, body(): parts = lax.all_to_all(parts, 'tensor', 0, 0)  8.72 us
    ppermute x1, starting transfers between devices, body(): mate = lax.ppermute(near, AXES, mates)  4.85 us
    unnamed x17, local copies, waits for them, and re-layouts  4.68 us
  transfers between devices with their start and end apart: 7, of which 5 were waited for; matrix products, arithmetic and copies ran while one was open for 0% of the time, Pallas kernels for 0%

profile of v1, /device:TPU:1, one launch (start us, length us, event | category | flops | bytes accessed | tf_op | source)
XLA Modules:
  0.0 102.6 jit_solution(2686097871433939559)
XLA Ops:
  0.6 0.1 pad_add_fusion.place_ref
  0.7 1.2 %copy-done = bf16[4,4,32,1024]{3,2,1,0:T(8,128)(2,1)S(1)} copy-done((bf16[4,4,32,1024]{3,2,1,0:T(8,128)(2,1)S(1)}, bf16[4,4,32,1024]{3,2,1,0:T(8,128)(2,1)}, u32[]{:S(2)}) %copy-start) | copy-done | bytes 1048600
  1.9 1.2 %copy-done.1 = bf16[4,4,32,1024]{3,2,1,0:T(8,128)(2,1)S(1)} copy-done((bf16[4,4,32,1024]{3,2,1,0:T(8,128)(2,1)S(1)}, bf16[4,4,32,1024]{3,2,1,0:T(8,128)(2,1)}, u32[]{:S(2)}) %copy-start.1) | copy-done | bytes 1048600
  3.2 1.0 %copy-done.2 = bf16[4,64,1024]{2,1,0:T(8,128)(2,1)S(1)} copy-done((bf16[4,64,1024]{2,1,0:T(8,128)(2,1)S(1)}, bf16[4,64,1024]{2,1,0:T(8,128)(2,1)}, u32[]{:S(2)}) %copy-start.2) | copy-done | bytes 524312
  4.2 1.0 %copy-done.3 = bf16[4,64,1024]{2,1,0:T(8,128)(2,1)S(1)} copy-done((bf16[4,64,1024]{2,1,0:T(8,128)(2,1)S(1)}, bf16[4,64,1024]{2,1,0:T(8,128)(2,1)}, u32[]{:S(2)}) %copy-start.3) | copy-done | bytes 524312
  5.2 2.9 %project.1 = f32[4,128,128]{2,1,0:T(8,128)} custom-call(s32[2]{0:T(128)S(1)} %pad_add_fusion.place_ref, bf16[4,4,32,1024]{3,2,1,0:T(8,128)(2,1)S(1)} %copy-done, bf16[4,4,32,1024]{3,2,1,0:T(8,128)(2,1)S(1)} %copy-done.1, bf16[4,64,1024]{2,1,0:T(8,128)(2,1)S(1)} %copy-done.2, bf16[4,64,1024]{2,1,0:T(8,128)(2,1)S(1)} %copy-done.3), custom_call_target="tpu_custom_call" | custom-call | tf_op jit(solution)/shard_map/project/pallas_call | solution.py:73
  8.1 10.2 %all-to-all-start = ((f32[8,64,128]{2,1,0:T(8,128)}), f32[8,64,128]{2,1,0:T(8,128)S(1)}, u32[]{:S(2)}, u32[]{:S(2)}) async-start(f32[8,64,128]{2,1,0:T(8,128)} %bitcast.2), calls=%async_computation | async-start | bytes 524288 | tf_op jit(solution)/shard_map/all_to_all | solution.py:227
  18.3 8.7 %all-to-all-done.parts_ref = f32[8,64,128]{2,1,0:T(8,128)S(1)} async-done(((f32[8,64,128]{2,1,0:T(8,128)}), f32[8,64,128]{2,1,0:T(8,128)S(1)}, u32[]{:S(2)}, u32[]{:S(2)}) %all-to-all-start) | async-done | bytes 262176 | tf_op jit(solution)/shard_map/all_to_all | solution.py:227
  27.0 0.0 copy-done.4
  27.0 0.0 copy-done.5
  27.0 1.6 %outer.1 = bf16[64,128]{1,0:T(8,128)(2,1)S(1)} custom-call(s32[2]{0:T(128)S(1)} %pad_add_fusion.place_ref, s32[4]{0:T(128)S(1)} %copy-done.5, s32[4,32]{1,0:T(4,128)S(1)} %copy-done.4, f32[8,64,128]{2,1,0:T(8,128)S(1)} %all-to-all-done.parts_ref), custom_call_target="tpu_custom_call" | custom-call | tf_op jit(solution)/shard_map/outer/pallas_call | solution.py:114
  28.6 0.7 broadcast_in_dim.6
  29.4 10.0 %all-to-all-start.1 = ((bf16[16,64,128]{2,1,0:T(8,128)(2,1)}), bf16[16,64,128]{2,1,0:T(8,128)(2,1)S(1)}, u32[]{:S(2)}, u32[]{:S(2)}) async-start(bf16[16,64,128]{2,1,0:T(8,128)(2,1)} %broadcast_in_dim.6), calls=%async_computation.1 | async-start | bytes 524288 | tf_op jit(solution)/shard_map/all_to_all | solution.py:197
  39.4 0.1 constant_dynamic-slice_fusion
  39.5 3.1 %collective-permute-start = (bf16[32,4096]{1,0:T(8,128)(2,1)S(1)}, bf16[32,4096]{1,0:T(8,128)(2,1)S(1)}, u32[]{:S(2)}, u32[]{:S(2)}) collective-permute-start(bf16[32,4096]{1,0:T(8,128)(2,1)S(1)} %get-tuple-element.19), channel_id=1, source_target_pairs={{0,128},{1,129},{8,136},{9,137},{16,144},{17,145},{24,152},{25,153... | collective-permute-start | bytes 786440 | tf_op jit(solution)/shard_map/ppermute | solution.py:223
  42.6 6.9 %collective-permute-start.1 = (bf16[32,4096]{1,0:T(8,128)(2,1)S(1)}, bf16[32,4096]{1,0:T(8,128)(2,1)S(1)}, u32[]{:S(2)}, u32[]{:S(2)}) collective-permute-start(bf16[32,4096]{1,0:T(8,128)(2,1)S(1)} %get-tuple-element.21), channel_id=1, source_target_pairs={{0,256},{1,257},{8,264},{9,265},{16,272},{17,273},{24,280},{25,281... | collective-permute-start | bytes 786440 | tf_op jit(solution)/shard_map/ppermute | solution.py:223
  49.6 1.9 %collective-permute-start.2 = (bf16[32,4096]{1,0:T(8,128)(2,1)S(1)}, bf16[32,4096]{1,0:T(8,128)(2,1)S(1)}, u32[]{:S(2)}, u32[]{:S(2)}) collective-permute-start(bf16[32,4096]{1,0:T(8,128)(2,1)S(1)} %get-tuple-element.18), channel_id=1, source_target_pairs={{0,384},{1,385},{8,392},{9,393},{16,400},{17,401},{24,408},{25,409... | collective-permute-start | bytes 786440 | tf_op jit(solution)/shard_map/ppermute | solution.py:223
  51.5 0.0 collective-permute-done.first_ref
  51.5 9.4 %collective-permute-done.1.second_ref = bf16[32,4096]{1,0:T(8,128)(2,1)S(1)} collective-permute-done((bf16[32,4096]{1,0:T(8,128)(2,1)S(1)}, bf16[32,4096]{1,0:T(8,128)(2,1)S(1)}, u32[]{:S(2)}, u32[]{:S(2)}) %collective-permute-start.1) | collective-permute-done | bytes 262176 | tf_op jit(solution)/shard_map/ppermute | solution.py:223
  60.9 4.5 %collective-permute-done.2.third_ref = bf16[32,4096]{1,0:T(8,128)(2,1)S(1)} collective-permute-done((bf16[32,4096]{1,0:T(8,128)(2,1)S(1)}, bf16[32,4096]{1,0:T(8,128)(2,1)S(1)}, u32[]{:S(2)}, u32[]{:S(2)}) %collective-permute-start.2) | collective-permute-done | bytes 262176 | tf_op jit(solution)/shard_map/ppermute | solution.py:223
  65.4 0.0 all-to-all-done.1
  65.4 0.2 copy.14
  65.6 0.2 broadcast_in_dim.15
  65.8 15.6 %all_to_all.20.near_ref = bf16[4,32,32,128]{3,2,1,0:T(8,128)(2,1)S(1)} all-to-all(bf16[4,32,32,128]{3,2,1,0:T(8,128)(2,1)S(1)} %broadcast_in_dim.15), channel_id=1, replica_groups={{0,8,130,138},{1,9,131,139},{16,24,146,154},{17,25,147,155},{32,40,162,..., dimensions={0} | all-to-all | bytes 2097152 | tf_op jit(solution)/shard_map/all_to_all | solution.py:197
  81.4 4.8 %collective-permute-start.3 = (bf16[4,32,32,128]{3,2,1,0:T(8,128)(2,1)S(1)}, bf16[4,32,32,128]{3,2,1,0:T(8,128)(2,1)S(1)}, u32[]{:S(2)}, u32[]{:S(2)}) collective-permute-start(bf16[4,32,32,128]{3,2,1,0:T(8,128)(2,1)S(1)} %all_to_all.20.near_ref), channel_id=1, source_target_pairs={{0,1},{1,0},{8,9},{9,8},{16,17},{17,16},{24,25},{25,24},{32,33},{3... | collective-permute-start | bytes 3145736 | tf_op jit(solution)/shard_map/ppermute | solution.py:235
  86.3 2.3 %collective-permute-done.3.mate_ref = bf16[4,32,32,128]{3,2,1,0:T(8,128)(2,1)S(1)} collective-permute-done((bf16[4,32,32,128]{3,2,1,0:T(8,128)(2,1)S(1)}, bf16[4,32,32,128]{3,2,1,0:T(8,128)(2,1)S(1)}, u32[]{:S(2)}, u32[]{:S(2)}) %collective-permute-start.3) | collective-permute-done | bytes 1048608 | tf_op jit(solution)/shard_map/ppermute | solution.py:235
  88.5 4.1 %score.1 = f32[4,32,256]{2,1,0:T(8,128)} custom-call(s32[2]{0:T(128)S(1)} %pad_add_fusion.place_ref, bf16[32,4096]{1,0:T(8,128)(2,1)S(1)} %get-tuple-element.7.own_ref, bf16[32,4096]{1,0:T(8,128)(2,1)S(1)} %collective-permute-done.first_ref, bf16[32,4096]{1,0:T(8,128)(2,1)S(1)} %collective-permute-done.1.second_ref, ...), custom_call_target="tpu_custom_call" | custom-call | tf_op jit(solution)/shard_map/score/pallas_call | solution.py:183
  92.6 3.5 %all-to-all-start.3 = ((f32[4,32,256]{2,1,0:T(8,128)}), f32[4,32,256]{2,1,0:T(8,128)S(1)}, u32[]{:S(2)}, u32[]{:S(2)}) async-start(f32[4,32,256]{2,1,0:T(8,128)} %score.1), calls=%async_computation.3 | async-start | bytes 262144 | tf_op jit(solution)/shard_map/all_to_all | solution.py:238
  96.1 0.1 copy.15.domains_ref
  96.2 4.7 %all-to-all-done.3.parts_ref = f32[4,32,256]{2,1,0:T(8,128)S(1)} async-done(((f32[4,32,256]{2,1,0:T(8,128)}), f32[4,32,256]{2,1,0:T(8,128)S(1)}, u32[]{:S(2)}, u32[]{:S(2)}) %all-to-all-start.3) | async-done | bytes 131104 | tf_op jit(solution)/shard_map/all_to_all | solution.py:238
  100.9 1.1 %finish.1 = (f32[32,256]{1,0:T(8,128)}, f32[32,8]{1,0:T(8,128)S(1)}) custom-call(f32[4,32,256]{2,1,0:T(8,128)S(1)} %all-to-all-done.3.parts_ref, s32[256,1]{1,0:T(8,128)S(1)} %copy.15.domains_ref), custom_call_target="tpu_custom_call" | custom-call | tf_op jit(solution)/shard_map/finish/pallas_call | solution.py:152
  101.9 0.7 copy.16
  (10 shorter events, 0.0 us)
Async XLA Ops:
  0.7 1.2 %copy-start = (bf16[4,4,32,1024]{3,2,1,0:T(8,128)(2,1)S(1)}, bf16[4,4,32,1024]{3,2,1,0:T(8,128)(2,1)}, u32[]{:S(2)}) copy-start(bf16[4,4,32,1024]{3,2,1,0:T(8,128)(2,1)} %in_ref.1) | copy-start | bytes 3145732
  1.9 1.2 %copy-start.1 = (bf16[4,4,32,1024]{3,2,1,0:T(8,128)(2,1)S(1)}, bf16[4,4,32,1024]{3,2,1,0:T(8,128)(2,1)}, u32[]{:S(2)}) copy-start(bf16[4,4,32,1024]{3,2,1,0:T(8,128)(2,1)} %grad_ref.1) | copy-start | bytes 3145732
  3.2 1.0 %copy-start.2 = (bf16[4,64,1024]{2,1,0:T(8,128)(2,1)S(1)}, bf16[4,64,1024]{2,1,0:T(8,128)(2,1)}, u32[]{:S(2)}) copy-start(bf16[4,64,1024]{2,1,0:T(8,128)(2,1)} %in_proj_ref.1) | copy-start | bytes 1572868
  4.2 1.0 %copy-start.3 = (bf16[4,64,1024]{2,1,0:T(8,128)(2,1)S(1)}, bf16[4,64,1024]{2,1,0:T(8,128)(2,1)}, u32[]{:S(2)}) copy-start(bf16[4,64,1024]{2,1,0:T(8,128)(2,1)} %out_proj_ref.1) | copy-start | bytes 1572868
  5.2 34.2 %copy-start.6 = (bf16[32,16384]{1,0:T(8,128)(2,1)S(1)}, bf16[32,16384]{1,0:T(8,128)(2,1)}, u32[]{:S(2)}) copy-start(bf16[32,16384]{1,0:T(8,128)(2,1)} %param.12) | copy-start | bytes 3145732
  8.1 18.9 %all-to-all-start = ((f32[8,64,128]{2,1,0:T(8,128)}), f32[8,64,128]{2,1,0:T(8,128)S(1)}, u32[]{:S(2)}, u32[]{:S(2)}) async-start(f32[8,64,128]{2,1,0:T(8,128)} %bitcast.2), calls=%async_computation | async-start | bytes 524288 | tf_op jit(solution)/shard_map/all_to_all | solution.py:227
  18.3 8.7 %copy-start.4 = (s32[4,32]{1,0:T(4,128)S(1)}, s32[4,32]{1,0:T(4,128)}, u32[]{:S(2)}) copy-start(s32[4,32]{1,0:T(4,128)} %mask_ref.1) | copy-start | bytes 1540
  18.3 8.7 %copy-start.5 = (s32[4]{0:T(128)S(1)}, s32[4]{0:T(128)}, u32[]{:S(2)}) copy-start(s32[4]{0:T(128)} %lengths_ref.1) | copy-start | bytes 52
  29.4 36.1 %all-to-all-start.1 = ((bf16[16,64,128]{2,1,0:T(8,128)(2,1)}), bf16[16,64,128]{2,1,0:T(8,128)(2,1)S(1)}, u32[]{:S(2)}, u32[]{:S(2)}) async-start(bf16[16,64,128]{2,1,0:T(8,128)(2,1)} %broadcast_in_dim.6), calls=%async_computation.1 | async-start | bytes 524288 | tf_op jit(solution)/shard_map/all_to_all | solution.py:197
  39.5 12.0 %collective-permute-start = (bf16[32,4096]{1,0:T(8,128)(2,1)S(1)}, bf16[32,4096]{1,0:T(8,128)(2,1)S(1)}, u32[]{:S(2)}, u32[]{:S(2)}) collective-permute-start(bf16[32,4096]{1,0:T(8,128)(2,1)S(1)} %get-tuple-element.19), channel_id=1, source_target_pairs={{0,128},{1,129},{8,136},{9,137},{16,144},{17,145},{24,152},{25,153... | collective-permute-start | bytes 786440 | tf_op jit(solution)/shard_map/ppermute | solution.py:223
  42.6 18.2 %collective-permute-start.1 = (bf16[32,4096]{1,0:T(8,128)(2,1)S(1)}, bf16[32,4096]{1,0:T(8,128)(2,1)S(1)}, u32[]{:S(2)}, u32[]{:S(2)}) collective-permute-start(bf16[32,4096]{1,0:T(8,128)(2,1)S(1)} %get-tuple-element.21), channel_id=1, source_target_pairs={{0,256},{1,257},{8,264},{9,265},{16,272},{17,273},{24,280},{25,281... | collective-permute-start | bytes 786440 | tf_op jit(solution)/shard_map/ppermute | solution.py:223
  49.6 15.8 %collective-permute-start.2 = (bf16[32,4096]{1,0:T(8,128)(2,1)S(1)}, bf16[32,4096]{1,0:T(8,128)(2,1)S(1)}, u32[]{:S(2)}, u32[]{:S(2)}) collective-permute-start(bf16[32,4096]{1,0:T(8,128)(2,1)S(1)} %get-tuple-element.18), channel_id=1, source_target_pairs={{0,384},{1,385},{8,392},{9,393},{16,400},{17,401},{24,408},{25,409... | collective-permute-start | bytes 786440 | tf_op jit(solution)/shard_map/ppermute | solution.py:223
  81.4 7.1 %collective-permute-start.3 = (bf16[4,32,32,128]{3,2,1,0:T(8,128)(2,1)S(1)}, bf16[4,32,32,128]{3,2,1,0:T(8,128)(2,1)S(1)}, u32[]{:S(2)}, u32[]{:S(2)}) collective-permute-start(bf16[4,32,32,128]{3,2,1,0:T(8,128)(2,1)S(1)} %all_to_all.20.near_ref), channel_id=1, source_target_pairs={{0,1},{1,0},{8,9},{9,8},{16,17},{17,16},{24,25},{25,24},{32,33},{3... | collective-permute-start | bytes 3145736 | tf_op jit(solution)/shard_map/ppermute | solution.py:235
  92.6 3.5 %copy-start.7 = (s32[256,1]{0,1:T(1,128)S(1)}, s32[256,1]{0,1:T(1,128)}, u32[]{:S(2)}) copy-start(s32[256,1]{0,1:T(1,128)} %param.15) | copy-start | bytes 3076
  92.6 8.3 %all-to-all-start.3 = ((f32[4,32,256]{2,1,0:T(8,128)}), f32[4,32,256]{2,1,0:T(8,128)S(1)}, u32[]{:S(2)}, u32[]{:S(2)}) async-start(f32[4,32,256]{2,1,0:T(8,128)} %score.1), calls=%async_computation.3 | async-start | bytes 262144 | tf_op jit(solution)/shard_map/all_to_all | solution.py:238

commit v2 on v1

v2 whole, which is shorter than its diff:
```python
import functools

import jax
import jax.numpy as jnp
from jax import lax
from jax.experimental import pallas as pl
from jax.experimental.pallas import tpu as pltpu
from jax.sharding import PartitionSpec as P

LAYERS = 4
SEQ = 32
WIDTH = 64
DOMAINS = 8
AXES = ("dp", "tensor")
NX, NY, NZ, NC = 4, 8, 8, 2
STEPS = (0, 1, 3, 2)
LANES = 128
PAIRS = WIDTH * WIDTH // LANES


def flat(x, y, z, c):
    return (x * 16 + (y // 4) * 8 + z) * 8 + (y % 4) * 2 + c


def places():
    return [(x, y, z, c) for x in range(NX) for y in range(NY) for z in range(NZ) for c in range(NC)]


def partition(members):
    groups, seen = [], set()
    for place in places():
        group = [flat(*m) for m in members(*place)]
        if group[0] not in seen:
            seen.update(group)
            groups.append(group)
    return groups


def sharing_members(x, y, z, c):
    return [(i, y, z, core) for i in range(NX) for core in range(NC)]


def far_members(x, y, z, c):
    return [
        ((x & 1) | (xh << 1), (h << 2) | ((y & 3) ^ (((x >> 1) ^ xh) << 1)), (z & 1) | (zz << 1), c)
        for xh in range(2)
        for h in range(2)
        for zz in range(4)
    ]


def near_members(x, y, z, c):
    return [
        ((x & 2) | xl, y ^ ((x & 1) ^ xl), (z & 6) | zl, c)
        for xl in range(2)
        for zl in range(2)
    ]


def project_kernel(
    place_ref, in_ref, grad_ref, in_proj_ref, out_proj_ref, out_ref,
    in_buf, grad_buf, in_proj_buf, out_proj_buf, sems,
):
    x = place_ref[0]
    sources = (in_ref, grad_ref, in_proj_ref, out_proj_ref)
    buffers = (in_buf, grad_buf, in_proj_buf, out_proj_buf)
    copies = []
    for j in range(LAYERS):
        copies.append([
            pltpu.make_async_copy(source.at[x ^ j], buffer.at[j], sems.at[j, i])
            for i, (source, buffer) in enumerate(zip(sources, buffers))
        ])
        for copy in copies[j]:
            copy.start()

    def side(rows, proj):
        return lax.dot_general(
            rows.reshape(-1, rows.shape[-1]), proj, (((1,), (1,)), ((), ())), preferred_element_type=jnp.float32
        )

    for j in range(LAYERS):
        for copy in copies[j]:
            copy.wait()
        out_ref[j] = jnp.concatenate([side(in_buf[j], in_proj_buf[j]), side(grad_buf[j], out_proj_buf[j])], axis=1)


def project(place, query_inputs, query_output_grads, in_projection, out_projection):
    _, queries, seq, depth = query_inputs.shape
    hbm = pl.BlockSpec(memory_space=pltpu.HBM)
    return pl.pallas_call(
        project_kernel,
        out_shape=jax.ShapeDtypeStruct((LAYERS, queries * seq, 2 * WIDTH), jnp.float32),
        in_specs=[pl.BlockSpec(memory_space=pltpu.SMEM)] + [hbm] * 4,
        out_specs=pl.BlockSpec(memory_space=pltpu.VMEM),
        scratch_shapes=[
            pltpu.VMEM(query_inputs.shape, query_inputs.dtype),
            pltpu.VMEM(query_inputs.shape, query_inputs.dtype),
            pltpu.VMEM(in_projection.shape, in_projection.dtype),
            pltpu.VMEM(in_projection.shape, in_projection.dtype),
            pltpu.SemaphoreType.DMA((LAYERS, 4)),
        ],
        compiler_params=pltpu.CompilerParams(vmem_limit_bytes=60 * 1024 * 1024),
        name="project",
    )(place, query_inputs, query_output_grads, in_projection, out_projection)


def outer_kernel(place_ref, lengths_ref, mask_ref, parts_ref, out_ref, rows_ref):
    core = place_ref[1]
    total = parts_ref[0]
    for part in range(1, parts_ref.shape[0]):
        total = total + parts_ref[part]
    row = lax.broadcasted_iota(jnp.int32, (SEQ, SEQ), 0)
    col = lax.broadcasted_iota(jnp.int32, (SEQ, SEQ), 1)
    first = lax.broadcasted_iota(jnp.int32, (SEQ, LANES), 1) < WIDTH
    for k in range(2):
        mask = jnp.where(core == 0, mask_ref[k : k + 1, :], mask_ref[2 + k : 3 + k, :])
        kept = (row == col) & (col < lengths_ref[2 * core + k])
        weight = jnp.sum(jnp.where(kept, mask, 0).astype(jnp.float32), axis=1, keepdims=True)
        factors = total[k * SEQ : (k + 1) * SEQ]
        inner = factors[:, :WIDTH]
        inner = jnp.concatenate([inner, inner], axis=1)
        weighted = factors[:, WIDTH:] * weight
        for p in range(PAIRS):
            low = jnp.broadcast_to(weighted[:, 2 * p : 2 * p + 1], (SEQ, LANES))
            high = jnp.broadcast_to(weighted[:, 2 * p + 1 : 2 * p + 2], (SEQ, LANES))
            product = jnp.where(first, low, high) * inner
            rows_ref[2 * p + k : 2 * p + k + 1, :] = jnp.sum(product, axis=0, keepdims=True)
    block = rows_ref[...].astype(jnp.bfloat16)
    for m in range(out_ref.shape[0]):
        out_ref[m] = block


def outer(place, lengths, loss_mask, parts, copies):
    smem = pl.BlockSpec(memory_space=pltpu.SMEM)
    vmem = pl.BlockSpec(memory_space=pltpu.VMEM)
    return pl.pallas_call(
        outer_kernel,
        out_shape=jax.ShapeDtypeStruct((copies, 2 * PAIRS, LANES), jnp.bfloat16),
        in_specs=[smem, smem, vmem, vmem],
        out_specs=vmem,
        scratch_shapes=[pltpu.VMEM((2 * PAIRS, LANES), jnp.float32)],
        compiler_params=pltpu.CompilerParams(vmem_limit_bytes=16 * 1024 * 1024),
        name="outer",
    )(place, lengths, loss_mask, parts)


def finish_kernel(parts_ref, domains_ref, scores_ref, influence_ref):
    def half(core):
        total = parts_ref[core]
        for part in range(core + NC, parts_ref.shape[0], NC):
            total = total + parts_ref[part]
        return total

    total = jnp.concatenate([half(core) for core in range(NC)], axis=1)
    queries = total.shape[1]
    here = lax.broadcasted_iota(jnp.int32, (queries, queries), 0)
    there = lax.broadcasted_iota(jnp.int32, (queries, queries), 1)

    def bit(value, at, to, bits=1):
        return ((value >> at) & ((1 << bits) - 1)) << to

    target = (
        bit(here, 7, 1) + bit(here, 6, 6) + bit(here, 5, 2) + bit(here, 4, 0) + bit(here, 3, 7)
        + bit(here, 2, 5) + bit(here, 0, 3, 2)
    )
    place = (target == there).astype(jnp.float32)
    scores = jnp.dot(total, place, precision=lax.Precision.HIGHEST, preferred_element_type=jnp.float32)
    scores_ref[...] = scores
    lane = lax.broadcasted_iota(jnp.int32, (queries, DOMAINS), 1)
    onehot = (domains_ref[...] == lane).astype(jnp.float32)
    counts = jnp.sum(onehot, axis=0, keepdims=True)
    sums = jnp.dot(scores, onehot, precision=lax.Precision.HIGHEST, preferred_element_type=jnp.float32)
    influence_ref[...] = (sums / counts).T


def finish(parts, domains):
    _, rows, half = parts.shape
    queries = NC * half
    return pl.pallas_call(
        finish_kernel,
        out_shape=(
            jax.ShapeDtypeStruct((rows, queries), jnp.float32),
            jax.ShapeDtypeStruct((DOMAINS, rows), jnp.float32),
        ),
        compiler_params=pltpu.CompilerParams(vmem_limit_bytes=16 * 1024 * 1024),
        name="finish",
    )(parts, domains)


def score_kernel(place_ref, most_ref, last_ref, mate_most_ref, mate_last_ref, near_ref, out_ref, rows_buf, queries_buf):
    x, core = place_ref[0], place_ref[1]
    near, pairs, share, lanes = near_ref.shape
    for n in range(near):
        for p in range(pairs):
            queries_buf[n * share : (n + 1) * share, p * lanes : (p + 1) * lanes] = near_ref[n, p]
    at = 0
    for block_ref in (most_ref, last_ref, mate_most_ref, mate_last_ref):
        rows_buf[at : at + block_ref.shape[0], :] = block_ref[...]
        at += block_ref.shape[0]
    result = lax.dot_general(
        rows_buf[...], queries_buf[...], (((1,), (1,)), ((), ())), preferred_element_type=jnp.float32
    )
    rows = out_ref.shape[1]
    for i in range(NC):
        for n, step in enumerate(STEPS):
            at = (i * NX + n) * rows
            out_ref[pl.ds((x ^ step) * NC + (core ^ i), 1)] = result[at : at + rows][None]


def score(place, most, last, mate_most, mate_last, near):
    smem = pl.BlockSpec(memory_space=pltpu.SMEM)
    vmem = pl.BlockSpec(memory_space=pltpu.VMEM)
    rows, width = last.shape
    queries = near.shape[0] * near.shape[2]
    return pl.pallas_call(
        score_kernel,
        out_shape=jax.ShapeDtypeStruct((NX * NC, rows, queries), jnp.float32),
        in_specs=[smem] + [vmem] * 5,
        out_specs=vmem,
        scratch_shapes=[
            pltpu.VMEM((NX * NC * rows, width), jnp.bfloat16),
            pltpu.VMEM((queries, width), jnp.bfloat16),
        ],
        compiler_params=pltpu.CompilerParams(vmem_limit_bytes=24 * 1024 * 1024),
        name="score",
    )(place, most, last, mate_most, mate_last, near)


def exchange(blocks, members):
    return lax.all_to_all(blocks, AXES, 0, 0, axis_index_groups=partition(members))


def body(
    query_inputs,
    query_output_grads,
    in_projection,
    out_projection,
    train_grads,
    lengths,
    loss_mask,
    domains,
):
    dp, tensor = lax.axis_index("dp"), lax.axis_index("tensor")
    x, core, y_lo = dp >> 4, tensor & 1, tensor >> 1
    place = jnp.stack([x, core]).astype(jnp.int32)
    width = train_grads.shape[1] // LAYERS

    def columns(step):
        return lax.dynamic_slice_in_dim(train_grads, (x ^ y_lo ^ step) * width, width, axis=1)

    def from_x(step):
        return lax.ppermute(columns(step), AXES, [(flat(*p), flat(p[0] ^ step, *p[1:])) for p in places()])

    def from_mate(block):
        return lax.ppermute(block, AXES, [(flat(*p), flat(*p[:3], 1 - p[3])) for p in places()])

    parts = project(place, query_inputs, query_output_grads, in_projection, out_projection)
    parts = parts.reshape(2 * LAYERS, -1, 2 * WIDTH)
    parts = lax.all_to_all(parts, "tensor", 0, 0)
    parts, *most = lax.optimization_barrier((parts, columns(0), from_x(1), from_x(3)))
    most = jnp.concatenate(most, axis=0)

    copies = outer(place, lengths, loss_mask, parts, len(far_members(0, 0, 0, 0)))
    far = exchange(copies, far_members)
    far, last, mate_most = lax.optimization_barrier((far, from_x(2), from_mate(most)))
    far = far.transpose(1, 0, 2).reshape(PAIRS, -1, LANES)
    copies = jnp.broadcast_to(far[None], (4,) + far.shape)
    near = exchange(copies, near_members)
    mate_last = from_mate(last)

    parts = exchange(score(place, most, last, mate_most, mate_last, near), sharing_members)
    scores, influence = finish(parts, domains)
    return scores, influence.T


def solution(mesh):
    return jax.shard_map(
        body,
        mesh=mesh,
        in_specs=(
            P(None, "dp", None, "tensor"),
            P(None, "dp", None, "tensor"),
            P(None, None, "tensor"),
            P(None, None, "tensor"),
            P(("dp", "tensor"), None),
            P("dp"),
            P("dp", None),
            P(),
        ),
        out_specs=(P(("dp", "tensor"), None), P(("dp", "tensor"), None)),
        check_vma=False,
    )
```

time: 103 us -> 97.7 us (0.949)
  blocking collectives: 15.6 us -> 0 us
  starting transfers between devices: 40.5 us -> 49.3 us
  waiting for transfers between devices: 29.6 us -> 34.9 us
  local copies, waits for them, and re-layouts: 6.5 us -> 1.61 us
    all_to_all x1 -> x0, blocking collectives: 15.6 us -> none  [spread(): return lax.all_to_all(copies, AXES, 0, 0, axis_index_groups=groups)]
    all_to_all x2 -> x3, waiting for transfers between devices: 4.65 us -> 16 us  [exchange(): lax.all_to_all(blocks, AXES, 0, 0, axis_index_groups=partition(members))]
    all_to_all x2 -> x3, starting transfers between devices: 13.5 us -> 24 us  [exchange(): lax.all_to_all(blocks, AXES, 0, 0, axis_index_groups=partition(members))]
    all_to_all x1, waiting for transfers between devices: 8.72 us -> 0.01 us  [body(): parts = lax.all_to_all(parts, 'tensor', 0, 0)]
    unnamed x17 -> x13, local copies, waits for them, and re-layouts: 4.68 us -> 0.19 us
    ppermute x4 -> x5, waiting for transfers between devices: 16.2 us -> 18.9 us  [the longest x3 17.7 us: from_x(): lax.ppermute(columns(step), AXES, [(flat(*p), flat(p[0] ^ step, *p[1:]))...]
    ppermute x4 -> x5, starting transfers between devices: 16.8 us -> 15.1 us  [the longest x3 9.45 us: from_x(): lax.ppermute(columns(step), AXES, [(flat(*p), flat(p[0] ^ step, *p[1:]))...]
    pallas_call x2, Pallas kernels: 5.66 us -> 4.29 us  [the longest x1 2.31 us: outer(): pl.pallas_call(outer_kernel, out_shape=jax.ShapeDtypeStruct((copies, 2 *...]
  transfers between devices with their start and end apart: 7 -> 9, of which waited for: 5 -> 7; matrix products, arithmetic and copies ran while one was open for 0% -> 0% of each run, Pallas kernels for 0% -> 2%
where the time goes in v2:
time: 97.7 us; the launch traced here: 96.9 us
  starting transfers between devices  49.3 us (50%)
  waiting for transfers between devices  34.9 us (36%)
  Pallas kernels  9.76 us (10%)
  local copies, waits for them, and re-layouts  1.61 us (2%)
    all_to_all x3, starting transfers between devices, exchange(): lax.all_to_all(blocks, AXES, 0, 0, axis_index_groups=partition(members))  24 us
    ppermute x3, waiting for transfers between devices, from_x(): lax.ppermute(columns(step), AXES, [(flat(*p), flat(p[0] ^ step, *p[1:]))...  17.7 us
    all_to_all x3, waiting for transfers between devices, exchange(): lax.all_to_all(blocks, AXES, 0, 0, axis_index_groups=partition(members))  16 us
    all_to_all x1, starting transfers between devices, body(): parts = lax.all_to_all(parts, 'tensor', 0, 0)  10.2 us
    ppermute x3, starting transfers between devices, from_x(): lax.ppermute(columns(step), AXES, [(flat(*p), flat(p[0] ^ step, *p[1:]))...  9.45 us
    ppermute x2, starting transfers between devices, from_mate(): lax.ppermute(block, AXES, [(flat(*p), flat(*p[:3], 1 - p[3])) for p in pl...  5.67 us
    pallas_call x1, Pallas kernels, project(): pl.pallas_call(project_kernel, out_shape=jax.ShapeDtypeStruct((LAYERS, qu...  4.15 us
    pallas_call x1, Pallas kernels, outer(): pl.pallas_call(outer_kernel, out_shape=jax.ShapeDtypeStruct((copies, 2 *...  2.31 us
  transfers between devices with their start and end apart: 9, of which 7 were waited for; matrix products, arithmetic and copies ran while one was open for 0% of the time, Pallas kernels for 2%

profile of v2, /device:TPU:1, one launch (start us, length us, event | category | flops | bytes accessed | tf_op | source)
XLA Modules:
  0.0 96.9 jit_solution(2880089082012527484)
XLA Ops:
  0.6 0.6 pad_add_fusion.place_ref
  1.2 4.2 %project.1 = f32[4,128,128]{2,1,0:T(8,128)} custom-call(s32[2]{0:T(128)} %pad_add_fusion.place_ref, bf16[4,4,32,1024]{3,2,1,0:T(8,128)(2,1)} %in_ref.1, bf16[4,4,32,1024]{3,2,1,0:T(8,128)(2,1)} %grad_ref.1, bf16[4,64,1024]{2,1,0:T(8,128)(2,1)} %in_proj_ref.1, bf16[4,64,1024]{2,1,0:T(8,128)(2,1)} %out_proj_ref.1), custom_call_target="tpu_custom_call" | custom-call | tf_op jit(solution)/shard_map/project/pallas_call | solution.py:90
  5.4 10.2 %all-to-all-start = ((f32[8,64,128]{2,1,0:T(8,128)}), f32[8,64,128]{2,1,0:T(8,128)S(1)}, u32[]{:S(2)}, u32[]{:S(2)}) async-start(f32[8,64,128]{2,1,0:T(8,128)} %bitcast.6), calls=%async_computation | async-start | bytes 524288 | tf_op jit(solution)/shard_map/all_to_all | solution.py:259
  15.6 0.0 copy-done.3
  15.6 0.1 constant_dynamic-slice_fusion
  15.7 1.9 %collective-permute-start = (bf16[32,4096]{1,0:T(8,128)(2,1)S(1)}, bf16[32,4096]{1,0:T(8,128)(2,1)S(1)}, u32[]{:S(2)}, u32[]{:S(2)}) collective-permute-start(bf16[32,4096]{1,0:T(8,128)(2,1)S(1)} %get-tuple-element.21), channel_id=1, source_target_pairs={{0,128},{1,129},{8,136},{9,137},{16,144},{17,145},{24,152},{25,153... | collective-permute-start | bytes 786440 | tf_op jit(solution)/shard_map/ppermute | solution.py:252
  17.6 1.9 %collective-permute-start.1 = (bf16[32,4096]{1,0:T(8,128)(2,1)S(1)}, bf16[32,4096]{1,0:T(8,128)(2,1)S(1)}, u32[]{:S(2)}, u32[]{:S(2)}) collective-permute-start(bf16[32,4096]{1,0:T(8,128)(2,1)S(1)} %get-tuple-element.23), channel_id=1, source_target_pairs={{0,384},{1,385},{8,392},{9,393},{16,400},{17,401},{24,408},{25,409... | collective-permute-start | bytes 786440 | tf_op jit(solution)/shard_map/ppermute | solution.py:252
  19.5 5.8 %collective-permute-done = bf16[32,4096]{1,0:T(8,128)(2,1)S(1)} collective-permute-done((bf16[32,4096]{1,0:T(8,128)(2,1)S(1)}, bf16[32,4096]{1,0:T(8,128)(2,1)S(1)}, u32[]{:S(2)}, u32[]{:S(2)}) %collective-permute-start) | collective-permute-done | bytes 262176 | tf_op jit(solution)/shard_map/ppermute | solution.py:252
  25.3 3.1 %collective-permute-done.1 = bf16[32,4096]{1,0:T(8,128)(2,1)S(1)} collective-permute-done((bf16[32,4096]{1,0:T(8,128)(2,1)S(1)}, bf16[32,4096]{1,0:T(8,128)(2,1)S(1)}, u32[]{:S(2)}, u32[]{:S(2)}) %collective-permute-start.1) | collective-permute-done | bytes 262176 | tf_op jit(solution)/shard_map/ppermute | solution.py:252
  28.5 0.0 all-to-all-done.parts_ref
  28.5 0.0 copy-start
  28.5 0.0 copy-start.1
  28.5 0.0 copy-start.2
  28.6 2.9 %collective-permute-start.3 = (bf16[96,4096]{1,0:T(8,128)(2,1)S(1)}, bf16[96,4096]{1,0:T(8,128)(2,1)S(1)}, u32[]{:S(2)}, u32[]{:S(2)}) collective-permute-start(bf16[96,4096]{1,0:T(8,128)(2,1)S(1)} %constant_dynamic-update-slice_fusion.most_ref), channel_id=1, source_target_pairs={{0,1},{1,0},{8,9},{9,8},{16,17},{17,16},{24,25},{25,24},{32,33},{3... | collective-permute-start | bytes 2359304 | tf_op jit(solution)/shard_map/ppermute | solution.py:255
  31.5 2.3 %outer.1 = bf16[16,64,128]{2,1,0:T(8,128)(2,1)} custom-call(s32[2]{0:T(128)S(1)} %copy-done, s32[4]{0:T(128)S(1)} %copy-done.2, s32[4,32]{1,0:T(4,128)S(1)} %copy-done.1, f32[8,64,128]{2,1,0:T(8,128)S(1)} %all-to-all-done.parts_ref), custom_call_target="tpu_custom_call" | custom-call | tf_op jit(solution)/shard_map/outer/pallas_call | solution.py:136
  33.8 12.4 %all-to-all-start.1 = ((bf16[16,64,128]{2,1,0:T(8,128)(2,1)}), bf16[16,64,128]{2,1,0:T(8,128)(2,1)S(1)}, u32[]{:S(2)}, u32[]{:S(2)}) async-start(bf16[16,64,128]{2,1,0:T(8,128)(2,1)} %outer.1), calls=%async_computation.1 | async-start | bytes 524288 | tf_op jit(solution)/shard_map/all_to_all | solution.py:230
  46.2 5.6 %collective-permute-start.2 = (bf16[32,4096]{1,0:T(8,128)(2,1)S(1)}, bf16[32,4096]{1,0:T(8,128)(2,1)S(1)}, u32[]{:S(2)}, u32[]{:S(2)}) collective-permute-start(bf16[32,4096]{1,0:T(8,128)(2,1)S(1)} %get-tuple-element.20), channel_id=1, source_target_pairs={{0,256},{1,257},{8,264},{9,265},{16,272},{17,273},{24,280},{25,281... | collective-permute-start | bytes 786440 | tf_op jit(solution)/shard_map/ppermute | solution.py:252
  51.8 8.8 %collective-permute-done.2.last_ref = bf16[32,4096]{1,0:T(8,128)(2,1)S(1)} collective-permute-done((bf16[32,4096]{1,0:T(8,128)(2,1)S(1)}, bf16[32,4096]{1,0:T(8,128)(2,1)S(1)}, u32[]{:S(2)}, u32[]{:S(2)}) %collective-permute-start.2) | collective-permute-done | bytes 262176 | tf_op jit(solution)/shard_map/ppermute | solution.py:252
  60.6 0.2 all-to-all-done.1
  60.8 0.0 collective-permute-done.3.mate_most_ref
  60.8 0.2 copy.11
  61.0 1.1 %broadcast_in_dim.8 = bf16[4,32,32,128]{3,2,1,0:T(8,128)(2,1)} broadcast(bf16[32,32,128]{2,1,0:T(8,128)(2,1)S(1)} %bitcast.7), dimensions={1,2,3} | broadcast | bytes 1310720 | tf_op jit(solution)/shard_map/broadcast_in_dim | solution.py:267
  62.2 6.3 %all-to-all-start.2 = ((bf16[4,32,32,128]{3,2,1,0:T(8,128)(2,1)}), bf16[4,32,32,128]{3,2,1,0:T(8,128)(2,1)S(1)}, u32[]{:S(2)}, u32[]{:S(2)}) async-start(bf16[4,32,32,128]{3,2,1,0:T(8,128)(2,1)} %broadcast_in_dim.8), calls=%async_computation.2 | async-start | bytes 2097152 | tf_op jit(solution)/shard_map/all_to_all | solution.py:230
  68.5 2.8 %collective-permute-start.4 = (bf16[32,4096]{1,0:T(8,128)(2,1)S(1)}, bf16[32,4096]{1,0:T(8,128)(2,1)S(1)}, u32[]{:S(2)}, u32[]{:S(2)}) collective-permute-start(bf16[32,4096]{1,0:T(8,128)(2,1)S(1)} %collective-permute-done.2.last_ref), channel_id=1, source_target_pairs={{0,1},{1,0},{8,9},{9,8},{16,17},{17,16},{24,25},{25,24},{32,33},{3... | collective-permute-start | bytes 786440 | tf_op jit(solution)/shard_map/ppermute | solution.py:255
  71.3 1.1 %collective-permute-done.4.mate_last_ref = bf16[32,4096]{1,0:T(8,128)(2,1)S(1)} collective-permute-done((bf16[32,4096]{1,0:T(8,128)(2,1)S(1)}, bf16[32,4096]{1,0:T(8,128)(2,1)S(1)}, u32[]{:S(2)}, u32[]{:S(2)}) %collective-permute-start.4) | collective-permute-done | bytes 262176 | tf_op jit(solution)/shard_map/ppermute | solution.py:255
  72.4 10.6 %all-to-all-done.2.near_ref = bf16[4,32,32,128]{3,2,1,0:T(8,128)(2,1)S(1)} async-done(((bf16[4,32,32,128]{3,2,1,0:T(8,128)(2,1)}), bf16[4,32,32,128]{3,2,1,0:T(8,128)(2,1)S(1)}, u32[]{:S(2)}, u32[]{:S(2)}) %all-to-all-start.2) | async-done | bytes 1048608 | tf_op jit(solution)/shard_map/all_to_all | solution.py:230
  83.1 2.0 %score.1 = f32[8,32,128]{2,1,0:T(8,128)} custom-call(s32[2]{0:T(128)S(1)} %copy-done, bf16[96,4096]{1,0:T(8,128)(2,1)S(1)} %constant_dynamic-update-slice_fusion.most_ref, bf16[32,4096]{1,0:T(8,128)(2,1)S(1)} %collective-permute-done.2.last_ref, bf16[96,4096]{1,0:T(8,128)(2,1)S(1)} %collective-permute-done.3.mate_most_ref, ...), custom_call_target="tpu_custom_call" | custom-call | tf_op jit(solution)/shard_map/score/pallas_call | solution.py:215
  85.0 5.3 %all-to-all-start.3 = ((f32[8,32,128]{2,1,0:T(8,128)}), f32[8,32,128]{2,1,0:T(8,128)S(1)}, u32[]{:S(2)}, u32[]{:S(2)}) async-start(f32[8,32,128]{2,1,0:T(8,128)} %score.1), calls=%async_computation.3 | async-start | bytes 262144 | tf_op jit(solution)/shard_map/all_to_all | solution.py:230
  90.3 0.0 copy-done.4
  90.3 0.1 copy.12.domains_ref
  90.5 5.2 %all-to-all-done.3.parts_ref = f32[8,32,128]{2,1,0:T(8,128)S(1)} async-done(((f32[8,32,128]{2,1,0:T(8,128)}), f32[8,32,128]{2,1,0:T(8,128)S(1)}, u32[]{:S(2)}, u32[]{:S(2)}) %all-to-all-start.3) | async-done | bytes 131104 | tf_op jit(solution)/shard_map/all_to_all | solution.py:230
  95.6 1.3 %finish.1 = (f32[32,256]{1,0:T(8,128)}, f32[8,32]{1,0:T(8,128)}) custom-call(f32[8,32,128]{2,1,0:T(8,128)S(1)} %all-to-all-done.3.parts_ref, s32[256,1]{1,0:T(8,128)S(1)} %copy.12.domains_ref), custom_call_target="tpu_custom_call" | custom-call | tf_op jit(solution)/shard_map/finish/pallas_call | solution.py:179
  (8 shorter events, 0.1 us)
Async XLA Ops:
  1.2 14.4 %copy-start.3 = (bf16[32,16384]{1,0:T(8,128)(2,1)S(1)}, bf16[32,16384]{1,0:T(8,128)(2,1)}, u32[]{:S(2)}) copy-start(bf16[32,16384]{1,0:T(8,128)(2,1)} %param.12) | copy-start | bytes 3145732
  5.4 23.1 %all-to-all-start = ((f32[8,64,128]{2,1,0:T(8,128)}), f32[8,64,128]{2,1,0:T(8,128)S(1)}, u32[]{:S(2)}, u32[]{:S(2)}) async-start(f32[8,64,128]{2,1,0:T(8,128)} %bitcast.6), calls=%async_computation | async-start | bytes 524288 | tf_op jit(solution)/shard_map/all_to_all | solution.py:259
  15.7 9.6 %collective-permute-start = (bf16[32,4096]{1,0:T(8,128)(2,1)S(1)}, bf16[32,4096]{1,0:T(8,128)(2,1)S(1)}, u32[]{:S(2)}, u32[]{:S(2)}) collective-permute-start(bf16[32,4096]{1,0:T(8,128)(2,1)S(1)} %get-tuple-element.21), channel_id=1, source_target_pairs={{0,128},{1,129},{8,136},{9,137},{16,144},{17,145},{24,152},{25,153... | collective-permute-start | bytes 786440 | tf_op jit(solution)/shard_map/ppermute | solution.py:252
  17.6 10.9 %collective-permute-start.1 = (bf16[32,4096]{1,0:T(8,128)(2,1)S(1)}, bf16[32,4096]{1,0:T(8,128)(2,1)S(1)}, u32[]{:S(2)}, u32[]{:S(2)}) collective-permute-start(bf16[32,4096]{1,0:T(8,128)(2,1)S(1)} %get-tuple-element.23), channel_id=1, source_target_pairs={{0,384},{1,385},{8,392},{9,393},{16,400},{17,401},{24,408},{25,409... | collective-permute-start | bytes 786440 | tf_op jit(solution)/shard_map/ppermute | solution.py:252
  28.5 2.9 %copy-start = (s32[2]{0:T(128)S(1)}, s32[2]{0:T(128)}, u32[]{:S(2)}) copy-start(s32[2]{0:T(128)} %pad_add_fusion.place_ref) | copy-start | bytes 28
  28.5 2.9 %copy-start.1 = (s32[4,32]{1,0:T(4,128)S(1)}, s32[4,32]{1,0:T(4,128)}, u32[]{:S(2)}) copy-start(s32[4,32]{1,0:T(4,128)} %mask_ref.1) | copy-start | bytes 1540
  28.5 2.9 %copy-start.2 = (s32[4]{0:T(128)S(1)}, s32[4]{0:T(128)}, u32[]{:S(2)}) copy-start(s32[4]{0:T(128)} %lengths_ref.1) | copy-start | bytes 52
  28.6 32.3 %collective-permute-start.3 = (bf16[96,4096]{1,0:T(8,128)(2,1)S(1)}, bf16[96,4096]{1,0:T(8,128)(2,1)S(1)}, u32[]{:S(2)}, u32[]{:S(2)}) collective-permute-start(bf16[96,4096]{1,0:T(8,128)(2,1)S(1)} %constant_dynamic-update-slice_fusion.most_ref), channel_id=1, source_target_pairs={{0,1},{1,0},{8,9},{9,8},{16,17},{17,16},{24,25},{25,24},{32,33},{3... | collective-permute-start | bytes 2359304 | tf_op jit(solution)/shard_map/ppermute | solution.py:255
  33.8 27.0 %all-to-all-start.1 = ((bf16[16,64,128]{2,1,0:T(8,128)(2,1)}), bf16[16,64,128]{2,1,0:T(8,128)(2,1)S(1)}, u32[]{:S(2)}, u32[]{:S(2)}) async-start(bf16[16,64,128]{2,1,0:T(8,128)(2,1)} %outer.1), calls=%async_computation.1 | async-start | bytes 524288 | tf_op jit(solution)/shard_map/all_to_all | solution.py:230
  46.2 14.4 %collective-permute-start.2 = (bf16[32,4096]{1,0:T(8,128)(2,1)S(1)}, bf16[32,4096]{1,0:T(8,128)(2,1)S(1)}, u32[]{:S(2)}, u32[]{:S(2)}) collective-permute-start(bf16[32,4096]{1,0:T(8,128)(2,1)S(1)} %get-tuple-element.20), channel_id=1, source_target_pairs={{0,256},{1,257},{8,264},{9,265},{16,272},{17,273},{24,280},{25,281... | collective-permute-start | bytes 786440 | tf_op jit(solution)/shard_map/ppermute | solution.py:252
  62.2 20.9 %all-to-all-start.2 = ((bf16[4,32,32,128]{3,2,1,0:T(8,128)(2,1)}), bf16[4,32,32,128]{3,2,1,0:T(8,128)(2,1)S(1)}, u32[]{:S(2)}, u32[]{:S(2)}) async-start(bf16[4,32,32,128]{3,2,1,0:T(8,128)(2,1)} %broadcast_in_dim.8), calls=%async_computation.2 | async-start | bytes 2097152 | tf_op jit(solution)/shard_map/all_to_all | solution.py:230
  68.5 3.9 %collective-permute-start.4 = (bf16[32,4096]{1,0:T(8,128)(2,1)S(1)}, bf16[32,4096]{1,0:T(8,128)(2,1)S(1)}, u32[]{:S(2)}, u32[]{:S(2)}) collective-permute-start(bf16[32,4096]{1,0:T(8,128)(2,1)S(1)} %collective-permute-done.2.last_ref), channel_id=1, source_target_pairs={{0,1},{1,0},{8,9},{9,8},{16,17},{17,16},{24,25},{25,24},{32,33},{3... | collective-permute-start | bytes 786440 | tf_op jit(solution)/shard_map/ppermute | solution.py:255
  85.0 5.3 %copy-start.4 = (s32[256,1]{0,1:T(1,128)S(1)}, s32[256,1]{0,1:T(1,128)}, u32[]{:S(2)}) copy-start(s32[256,1]{0,1:T(1,128)} %param.15) | copy-start | bytes 3076
  85.0 10.6 %all-to-all-start.3 = ((f32[8,32,128]{2,1,0:T(8,128)}), f32[8,32,128]{2,1,0:T(8,128)S(1)}, u32[]{:S(2)}, u32[]{:S(2)}) async-start(f32[8,32,128]{2,1,0:T(8,128)} %score.1), calls=%async_computation.3 | async-start | bytes 262144 | tf_op jit(solution)/shard_map/all_to_all | solution.py:230

commit v3 on v2

--- a/solution.py
+++ b/solution.py
@@ -13,7 +13,7 @@
 DOMAINS = 8
 AXES = ("dp", "tensor")
 NX, NY, NZ, NC = 4, 8, 8, 2
-STEPS = (0, 1, 3, 2)
+STEPS = (0, 2, 1, 3)
 LANES = 128
 PAIRS = WIDTH * WIDTH // LANES
 
@@ -37,24 +37,29 @@
 
 
 def sharing_members(x, y, z, c):
-    return [(i, y, z, core) for i in range(NX) for core in range(NC)]
-
-
-def far_members(x, y, z, c):
+    return [(i, y, (z & 6) | zl, core) for i in range(NX) for zl in range(2) for core in range(NC)]
+
+
+def class_members(x, y, z, c):
     return [
-        ((x & 1) | (xh << 1), (h << 2) | ((y & 3) ^ (((x >> 1) ^ xh) << 1)), (z & 1) | (zz << 1), c)
-        for xh in range(2)
-        for h in range(2)
-        for zz in range(4)
+        (i, (h << 2) | ((y & 3) ^ x ^ i), k, c) for i in range(NX) for h in range(2) for k in range(NZ)
     ]
 
 
-def near_members(x, y, z, c):
-    return [
-        ((x & 2) | xl, y ^ ((x & 1) ^ xl), (z & 6) | zl, c)
-        for xl in range(2)
-        for zl in range(2)
-    ]
+def swapped(block, change):
+    return lax.ppermute(block, AXES, [(flat(*change(*p)), flat(*p)) for p in places()])
+
+
+def swap_x(block, step):
+    return swapped(block, lambda x, y, z, c: (x ^ step, y, z, c))
+
+
+def swap_z(block):
+    return swapped(block, lambda x, y, z, c: (x, y, z ^ 1, c))
+
+
+def swap_core(block):
+    return swapped(block, lambda x, y, z, c: (x, y, z, c ^ 1))
 
 
 def project_kernel(
@@ -126,20 +131,22 @@
             product = jnp.where(first, low, high) * inner
             rows_ref[2 * p + k : 2 * p + k + 1, :] = jnp.sum(product, axis=0, keepdims=True)
     block = rows_ref[...].astype(jnp.bfloat16)
+    half = out_ref.shape[1]
     for m in range(out_ref.shape[0]):
-        out_ref[m] = block
-
-
-def outer(place, lengths, loss_mask, parts, copies):
+        out_ref[m] = block[(m & 1) * half : (m & 1) * half + half]
+
+
+def outer(place, lengths, loss_mask, parts, members):
     smem = pl.BlockSpec(memory_space=pltpu.SMEM)
     vmem = pl.BlockSpec(memory_space=pltpu.VMEM)
     return pl.pallas_call(
         outer_kernel,
-        out_shape=jax.ShapeDtypeStruct((copies, 2 * PAIRS, LANES), jnp.bfloat16),
+        out_shape=jax.ShapeDtypeStruct((members, PAIRS, LANES), jnp.bfloat16),
         in_specs=[smem, smem, vmem, vmem],
         out_specs=vmem,
         scratch_shapes=[pltpu.VMEM((2 * PAIRS, LANES), jnp.float32)],
         compiler_params=pltpu.CompilerParams(vmem_limit_bytes=16 * 1024 * 1024),
+        cost_estimate=pl.CostEstimate(flops=0, bytes_accessed=60 * 1024 * 1024, transcendentals=0),
         name="outer",
     )(place, lengths, loss_mask, parts)
 
@@ -155,14 +162,7 @@
     queries = total.shape[1]
     here = lax.broadcasted_iota(jnp.int32, (queries, queries), 0)
     there = lax.broadcasted_iota(jnp.int32, (queries, queries), 1)
-
-    def bit(value, at, to, bits=1):
-        return ((value >> at) & ((1 << bits) - 1)) << to
-
-    target = (
-        bit(here, 7, 1) + bit(here, 6, 6) + bit(here, 5, 2) + bit(here, 4, 0) + bit(here, 3, 7)
-        + bit(here, 2, 5) + bit(here, 0, 3, 2)
-    )
+    target = ((here & 63) << 2) + ((here >> 7) << 1) + ((here >> 6) & 1)
     place = (target == there).astype(jnp.float32)
     scores = jnp.dot(total, place, precision=lax.Precision.HIGHEST, preferred_element_type=jnp.float32)
     scores_ref[...] = scores
@@ -187,43 +187,53 @@
     )(parts, domains)
 
 
-def score_kernel(place_ref, most_ref, last_ref, mate_most_ref, mate_last_ref, near_ref, out_ref, rows_buf, queries_buf):
-    x, core = place_ref[0], place_ref[1]
-    near, pairs, share, lanes = near_ref.shape
-    for n in range(near):
-        for p in range(pairs):
-            queries_buf[n * share : (n + 1) * share, p * lanes : (p + 1) * lanes] = near_ref[n, p]
+def score_kernel(place_ref, *refs):
+    *rows_refs, blocks_ref, out_ref, rows_buf, queries_buf = refs
+    x, core, z_low = place_ref[0], place_ref[1], place_ref[2]
+    lines, sources, lanes = blocks_ref.shape
+    for line in range(lines):
+        pair, query = line // 2, line % 2
+        queries_buf[query * sources : (query + 1) * sources, pair * lanes : (pair + 1) * lanes] = blocks_ref[line]
     at = 0
-    for block_ref in (most_ref, last_ref, mate_most_ref, mate_last_ref):
-        rows_buf[at : at + block_ref.shape[0], :] = block_ref[...]
-        at += block_ref.shape[0]
+    for ref in rows_refs:
+        rows_buf[at : at + ref.shape[0], :] = ref[...]
+        at += ref.shape[0]
     result = lax.dot_general(
         rows_buf[...], queries_buf[...], (((1,), (1,)), ((), ())), preferred_element_type=jnp.float32
     )
     rows = out_ref.shape[1]
-    for i in range(NC):
-        for n, step in enumerate(STEPS):
-            at = (i * NX + n) * rows
-            out_ref[pl.ds((x ^ step) * NC + (core ^ i), 1)] = result[at : at + rows][None]
-
-
-def score(place, most, last, mate_most, mate_last, near):
+    at = 0
+    for other_core in range(NC):
+        for step in STEPS:
+            for other_z in range(2):
+                member = ((x ^ step) * 2 + (z_low ^ other_z)) * NC + (core ^ other_core)
+                out_ref[pl.ds(member, 1)] = result[at : at + rows][None]
+                at += rows
+
+
+def score(place, rows, blocks):
     smem = pl.BlockSpec(memory_space=pltpu.SMEM)
     vmem = pl.BlockSpec(memory_space=pltpu.VMEM)
-    rows, width = last.shape
-    queries = near.shape[0] * near.shape[2]
+    count = sum(block.shape[0] for block in rows)
+    width = rows[0].shape[1]
+    members = 2 * NX * NC
+    queries = 2 * blocks.shape[1]
     return pl.pallas_call(
         score_kernel,
-        out_shape=jax.ShapeDtypeStruct((NX * NC, rows, queries), jnp.float32),
-        in_specs=[smem] + [vmem] * 5,
+        out_shape=jax.ShapeDtypeStruct((members, count // members, queries), jnp.float32),
+        in_specs=[smem] + [vmem] * (len(rows) + 1),
         out_specs=vmem,
         scratch_shapes=[
-            pltpu.VMEM((NX * NC * rows, width), jnp.bfloat16),
+            pltpu.VMEM((count, width), jnp.bfloat16),
             pltpu.VMEM((queries, width), jnp.bfloat16),
         ],
         compiler_params=pltpu.CompilerParams(vmem_limit_bytes=24 * 1024 * 1024),
         name="score",
-    )(place, most, last, mate_most, mate_last, near)
+    )(place, *rows, blocks)
+
+
+def after(block, *others):
+    return lax.optimization_barrier((block,) + others)[0]
 
 
 def exchange(blocks, members):
@@ -241,34 +251,47 @@
     domains,
 ):
     dp, tensor = lax.axis_index("dp"), lax.axis_index("tensor")
-    x, core, y_lo = dp >> 4, tensor & 1, tensor >> 1
-    place = jnp.stack([x, core]).astype(jnp.int32)
-    width = train_grads.shape[1] // LAYERS
+    x, z_low, core, y_lo = dp >> 4, dp & 1, tensor & 1, tensor >> 1
+    place = jnp.stack([x, core, z_low]).astype(jnp.int32)
+    count, ktot = train_grads.shape
+    width = ktot // LAYERS // 2
+
+    def half(which):
+        return jnp.concatenate(
+            [lax.dynamic_slice_in_dim(train_grads, (2 * i + which) * width, width, axis=1) for i in range(LAYERS)], axis=1
+        )
+
+    kept, other = half(z_low), swap_z(half(1 - z_low))
 
     def columns(step):
-        return lax.dynamic_slice_in_dim(train_grads, (x ^ y_lo ^ step) * width, width, axis=1)
-
-    def from_x(step):
-        return lax.ppermute(columns(step), AXES, [(flat(*p), flat(p[0] ^ step, *p[1:])) for p in places()])
-
-    def from_mate(block):
-        return lax.ppermute(block, AXES, [(flat(*p), flat(*p[:3], 1 - p[3])) for p in places()])
-
+        at = (x ^ y_lo ^ step) * width
+        return jnp.concatenate(
+            [lax.dynamic_slice_in_dim(block, at, width, axis=1) for block in (kept, other)], axis=0
+        )
+
+    layer = lax.dynamic_slice_in_dim(train_grads, (x ^ y_lo ^ 2) * 2 * width, 2 * width, axis=1)
+    layer = after(swap_x(layer, 2), other)
     parts = project(place, query_inputs, query_output_grads, in_projection, out_projection)
     parts = parts.reshape(2 * LAYERS, -1, 2 * WIDTH)
+
     parts = lax.all_to_all(parts, "tensor", 0, 0)
-    parts, *most = lax.optimization_barrier((parts, columns(0), from_x(1), from_x(3)))
-    most = jnp.concatenate(most, axis=0)
-
-    copies = outer(place, lengths, loss_mask, parts, len(far_members(0, 0, 0, 0)))
-    far = exchange(copies, far_members)
-    far, last, mate_most = lax.optimization_barrier((far, from_x(2), from_mate(most)))
-    far = far.transpose(1, 0, 2).reshape(PAIRS, -1, LANES)
-    copies = jnp.broadcast_to(far[None], (4,) + far.shape)
-    near = exchange(copies, near_members)
-    mate_last = from_mate(last)
-
-    parts = exchange(score(place, most, last, mate_most, mate_last, near), sharing_members)
+
+    across = [
+        lax.dynamic_slice_in_dim(layer, z_low * width, width, axis=1),
+        swap_z(lax.dynamic_slice_in_dim(layer, (1 - z_low) * width, width, axis=1)),
+    ]
+
+    rows = [
+        jnp.concatenate([columns(0)] + across, axis=0),
+        jnp.concatenate([swap_x(columns(step), step) for step in STEPS[2:]], axis=0),
+    ]
+    blocks = outer(place, lengths, loss_mask, parts, len(class_members(0, 0, 0, 0)))
+
+    blocks = exchange(blocks, class_members)
+    blocks = blocks.transpose(1, 0, 2)
+    rows += [swap_core(block) for block in rows]
+
+    parts = exchange(score(place, rows, blocks), sharing_members)
     scores, influence = finish(parts, domains)
     return scores, influence.T
 

time: 97.7 us -> 79.6 us (0.81)
  waiting for transfers between devices: 34.9 us -> 14.8 us
  starting transfers between devices: 49.3 us -> 52.1 us
  local copies, waits for them, and re-layouts: 1.61 us -> 0.61 us
    ppermute x5 -> x7, waiting for transfers between devices: 18.9 us -> 3.94 us  [swapped(): lax.ppermute(block, AXES, [(flat(*change(*p)), flat(*p)) for p in places()])]
    ppermute x5 -> x7, starting transfers between devices: 15.1 us -> 25.8 us  [swapped(): lax.ppermute(block, AXES, [(flat(*change(*p)), flat(*p)) for p in places()])]
    all_to_all x3 -> x2, waiting for transfers between devices: 16 us -> 7.03 us  [exchange(): lax.all_to_all(blocks, AXES, 0, 0, axis_index_groups=partition(members))]
    all_to_all x3 -> x2, starting transfers between devices: 24 us -> 16.1 us  [exchange(): lax.all_to_all(blocks, AXES, 0, 0, axis_index_groups=partition(members))]
    all_to_all x1, waiting for transfers between devices: 0.01 us -> 3.84 us  [body(): parts = lax.all_to_all(parts, 'tensor', 0, 0)]
    broadcast_in_dim x1 -> x0, local copies, waits for them, and re-layouts: 1.14 us -> none  [body(): copies = jnp.broadcast_to(far[None], (4,) + far.shape)]
  transfers between devices with their start and end apart: 9 -> 10, of which waited for: 7 -> 4; matrix products, arithmetic and copies ran while one was open for 0% -> 1% of each run, Pallas kernels for 2% -> 3%
where the time goes in v3:
time: 79.6 us; the launch traced here: 79 us
  starting transfers between devices  52.1 us (65%)
  waiting for transfers between devices  14.8 us (19%)
  Pallas kernels  9.84 us (12%)
  between operations  0.92 us (1%)
    ppermute x7, starting transfers between devices, swapped(): lax.ppermute(block, AXES, [(flat(*change(*p)), flat(*p)) for p in places()])  25.8 us
    all_to_all x2, starting transfers between devices, exchange(): lax.all_to_all(blocks, AXES, 0, 0, axis_index_groups=partition(members))  16.1 us
    all_to_all x1, starting transfers between devices, body(): parts = lax.all_to_all(parts, 'tensor', 0, 0)  10.2 us
    all_to_all x2, waiting for transfers between devices, exchange(): lax.all_to_all(blocks, AXES, 0, 0, axis_index_groups=partition(members))  7.03 us
    pallas_call x1, Pallas kernels, project(): pl.pallas_call(project_kernel, out_shape=jax.ShapeDtypeStruct((LAYERS, qu...  4.16 us
    ppermute x7, waiting for transfers between devices, swapped(): lax.ppermute(block, AXES, [(flat(*change(*p)), flat(*p)) for p in places()])  3.94 us
    all_to_all x1, waiting for transfers between devices, body(): parts = lax.all_to_all(parts, 'tensor', 0, 0)  3.84 us
    pallas_call x1, Pallas kernels, outer(): pl.pallas_call(outer_kernel, out_shape=jax.ShapeDtypeStruct((members, PAI...  2.45 us
  transfers between devices with their start and end apart: 10, of which 4 were waited for; matrix products, arithmetic and copies ran while one was open for 1% of the time, Pallas kernels for 3%

profile of v3, /device:TPU:1, one launch (start us, length us, event | category | flops | bytes accessed | tf_op | source)
XLA Modules:
  0.0 79.0 jit_solution(5258318565496902085)
XLA Ops:
  0.6 0.6 pad_add_fusion.place_ref
  1.2 4.2 %project.1 = f32[4,128,128]{2,1,0:T(8,128)} custom-call(s32[3]{0:T(128)} %pad_add_fusion.place_ref, bf16[4,4,32,1024]{3,2,1,0:T(8,128)(2,1)} %in_ref.1, bf16[4,4,32,1024]{3,2,1,0:T(8,128)(2,1)} %grad_ref.1, bf16[4,64,1024]{2,1,0:T(8,128)(2,1)} %in_proj_ref.1, bf16[4,64,1024]{2,1,0:T(8,128)(2,1)} %out_proj_ref.1), custom_call_target="tpu_custom_call" | custom-call | tf_op jit(solution)/shard_map/project/pallas_call | solution.py:95
  5.4 10.2 %all-to-all-start = ((f32[8,64,128]{2,1,0:T(8,128)}), f32[8,64,128]{2,1,0:T(8,128)S(1)}, u32[]{:S(2)}, u32[]{:S(2)}) async-start(f32[8,64,128]{2,1,0:T(8,128)} %bitcast.9), calls=%async_computation | async-start | bytes 524288 | tf_op jit(solution)/shard_map/all_to_all | solution.py:277
  15.6 0.0 copy-done.3
  15.6 1.9 %collective-permute-start.1 = (bf16[32,4096]{1,0:T(8,128)(2,1)S(1)}, bf16[32,4096]{1,0:T(8,128)(2,1)S(1)}, u32[]{:S(2)}, u32[]{:S(2)}) collective-permute-start(bf16[32,4096]{1,0:T(8,128)(2,1)S(1)} %constant_dynamic-slice_fusion.6), channel_id=1, source_target_pairs={{256,0},{257,1},{264,8},{265,9},{272,16},{273,17},{280,24},{281,25... | collective-permute-start | bytes 786440 | tf_op jit(solution)/shard_map/ppermute | solution.py:50
  17.6 0.1 constant_dynamic-slice_fusion.16
  17.7 2.9 %collective-permute-start = (bf16[32,8192]{1,0:T(8,128)(2,1)S(1)}, bf16[32,8192]{1,0:T(8,128)(2,1)S(1)}, u32[]{:S(2)}, u32[]{:S(2)}) collective-permute-start(bf16[32,8192]{1,0:T(8,128)(2,1)S(1)} %pad_maximum_fusion.1), channel_id=1, source_target_pairs={{8,0},{9,1},{0,8},{1,9},{24,16},{25,17},{16,24},{17,25},{40,32},{4... | collective-permute-start | bytes 1572872 | tf_op jit(solution)/shard_map/ppermute | solution.py:50
  20.7 0.0 copy-start.1
  20.7 0.0 copy-start.2
  20.8 3.8 %all-to-all-done.parts_ref = f32[8,64,128]{2,1,0:T(8,128)S(1)} async-done(((f32[8,64,128]{2,1,0:T(8,128)}), f32[8,64,128]{2,1,0:T(8,128)S(1)}, u32[]{:S(2)}, u32[]{:S(2)}) %all-to-all-start) | async-done | bytes 262176 | tf_op jit(solution)/shard_map/all_to_all | solution.py:277
  24.6 0.0 copy-done.1
  24.6 2.4 %outer.1 = bf16[64,32,128]{2,1,0:T(8,128)(2,1)} custom-call(s32[3]{0:T(128)S(1)} %copy-done, s32[4]{0:T(128)S(1)} %copy-done.2, s32[4,32]{1,0:T(4,128)S(1)} %copy-done.1, f32[8,64,128]{2,1,0:T(8,128)S(1)} %all-to-all-done.parts_ref), custom_call_target="tpu_custom_call" | custom-call | bytes 62914560 | tf_op jit(solution)/shard_map/outer/pallas_call | solution.py:142
  27.1 11.4 %all-to-all-start.1 = ((bf16[64,32,128]{2,1,0:T(8,128)(2,1)}), bf16[64,32,128]{2,1,0:T(8,128)(2,1)S(1)}, u32[]{:S(2)}, u32[]{:S(2)}) async-start(bf16[64,32,128]{2,1,0:T(8,128)(2,1)} %outer.1), calls=%async_computation.1 | async-start | bytes 1048576 | tf_op jit(solution)/shard_map/all_to_all | solution.py:240
  38.5 0.0 collective-permute-done.1
  38.5 0.0 collective-permute-done
  38.5 2.9 %collective-permute-start.2 = (bf16[32,2048]{1,0:T(8,128)(2,1)S(1)}, bf16[32,2048]{1,0:T(8,128)(2,1)S(1)}, u32[]{:S(2)}, u32[]{:S(2)}) collective-permute-start(bf16[32,2048]{1,0:T(8,128)(2,1)S(1)} %get-tuple-element.23), channel_id=1, source_target_pairs={{8,0},{9,1},{0,8},{1,9},{24,16},{25,17},{16,24},{17,25},{40,32},{4... | collective-permute-start | bytes 393224 | tf_op jit(solution)/shard_map/ppermute | solution.py:50
  41.5 4.3 %collective-permute-start.3 = (bf16[64,2048]{1,0:T(8,128)(2,1)S(1)}, bf16[64,2048]{1,0:T(8,128)(2,1)S(1)}, u32[]{:S(2)}, u32[]{:S(2)}) collective-permute-start(bf16[64,2048]{1,0:T(8,128)(2,1)S(1)} %pad_maximum_fusion.3), channel_id=1, source_target_pairs={{128,0},{129,1},{136,8},{137,9},{144,16},{145,17},{152,24},{153,25... | collective-permute-start | bytes 786440 | tf_op jit(solution)/shard_map/ppermute | solution.py:50
  45.8 4.6 %collective-permute-start.4 = (bf16[64,2048]{1,0:T(8,128)(2,1)S(1)}, bf16[64,2048]{1,0:T(8,128)(2,1)S(1)}, u32[]{:S(2)}, u32[]{:S(2)}) collective-permute-start(bf16[64,2048]{1,0:T(8,128)(2,1)S(1)} %pad_maximum_fusion.4), channel_id=1, source_target_pairs={{384,0},{385,1},{392,8},{393,9},{400,16},{401,17},{408,24},{409,25... | collective-permute-start | bytes 786440 | tf_op jit(solution)/shard_map/ppermute | solution.py:50
  50.5 0.0 collective-permute-done.2
  50.5 5.5 %collective-permute-start.5 = (bf16[128,2048]{1,0:T(8,128)(2,1)S(1)}, bf16[128,2048]{1,0:T(8,128)(2,1)S(1)}, u32[]{:S(2)}, u32[]{:S(2)}) collective-permute-start(bf16[128,2048]{1,0:T(8,128)(2,1)S(1)} %pad_maximum_fusion.2.refs_0_), channel_id=1, source_target_pairs={{1,0},{0,1},{9,8},{8,9},{17,16},{16,17},{25,24},{24,25},{33,32},{3... | collective-permute-start | bytes 1572872 | tf_op jit(solution)/shard_map/ppermute | solution.py:50
  56.1 0.0 collective-permute-done.3
  56.1 2.6 %collective-permute-done.4 = bf16[64,2048]{1,0:T(8,128)(2,1)S(1)} collective-permute-done((bf16[64,2048]{1,0:T(8,128)(2,1)S(1)}, bf16[64,2048]{1,0:T(8,128)(2,1)S(1)}, u32[]{:S(2)}, u32[]{:S(2)}) %collective-permute-start.4) | collective-permute-done | bytes 262176 | tf_op jit(solution)/shard_map/ppermute | solution.py:50
  58.8 3.6 %collective-permute-start.6 = (bf16[128,2048]{1,0:T(8,128)(2,1)S(1)}, bf16[128,2048]{1,0:T(8,128)(2,1)S(1)}, u32[]{:S(2)}, u32[]{:S(2)}) collective-permute-start(bf16[128,2048]{1,0:T(8,128)(2,1)S(1)} %constant_dynamic-update-slice_fusion.refs_1_), channel_id=1, source_target_pairs={{1,0},{0,1},{9,8},{8,9},{17,16},{16,17},{25,24},{24,25},{33,32},{3... | collective-permute-start | bytes 1572872 | tf_op jit(solution)/shard_map/ppermute | solution.py:50
  62.4 0.0 all-to-all-done.1
  62.4 0.2 copy.15
  62.6 0.0 collective-permute-done.5.refs_2_
  62.6 1.3 %collective-permute-done.6.refs_3_ = bf16[128,2048]{1,0:T(8,128)(2,1)S(1)} collective-permute-done((bf16[128,2048]{1,0:T(8,128)(2,1)S(1)}, bf16[128,2048]{1,0:T(8,128)(2,1)S(1)}, u32[]{:S(2)}, u32[]{:S(2)}) %collective-permute-start.6) | collective-permute-done | bytes 524320 | tf_op jit(solution)/shard_map/ppermute | solution.py:50
  63.9 2.0 %score.1 = f32[16,32,128]{2,1,0:T(8,128)} custom-call(s32[3]{0:T(128)S(1)} %copy-done, bf16[128,2048]{1,0:T(8,128)(2,1)S(1)} %pad_maximum_fusion.2.refs_0_, bf16[128,2048]{1,0:T(8,128)(2,1)S(1)} %constant_dynamic-update-slice_fusion.refs_1_, bf16[128,2048]{1,0:T(8,128)(2,1)S(1)} %collective-permute-done.5.refs_2_, ...), custom_call_target="tpu_custom_call" | custom-call | tf_op jit(solution)/shard_map/score/pallas_call | solution.py:221
  65.9 4.7 %all-to-all-start.2 = ((f32[16,32,128]{2,1,0:T(8,128)}), f32[16,32,128]{2,1,0:T(8,128)S(1)}, u32[]{:S(2)}, u32[]{:S(2)}) async-start(f32[16,32,128]{2,1,0:T(8,128)} %score.1), calls=%async_computation.2 | async-start | bytes 524288 | tf_op jit(solution)/shard_map/all_to_all | solution.py:240
  70.6 0.1 copy.13.domains_ref
  70.7 7.0 %all-to-all-done.2.parts_ref = f32[16,32,128]{2,1,0:T(8,128)S(1)} async-done(((f32[16,32,128]{2,1,0:T(8,128)}), f32[16,32,128]{2,1,0:T(8,128)S(1)}, u32[]{:S(2)}, u32[]{:S(2)}) %all-to-all-start.2) | async-done | bytes 262176 | tf_op jit(solution)/shard_map/all_to_all | solution.py:240
  77.8 1.2 %finish.1 = (f32[32,256]{1,0:T(8,128)}, f32[8,32]{1,0:T(8,128)}) custom-call(f32[16,32,128]{2,1,0:T(8,128)S(1)} %all-to-all-done.2.parts_ref, s32[256,1]{1,0:T(8,128)S(1)} %copy.13.domains_ref), custom_call_target="tpu_custom_call" | custom-call | tf_op jit(solution)/shard_map/finish/pallas_call | solution.py:179
  (17 shorter events, 0.3 us)
Async XLA Ops:
  1.2 14.4 %copy-start.3 = (bf16[32,16384]{1,0:T(8,128)(2,1)S(1)}, bf16[32,16384]{1,0:T(8,128)(2,1)}, u32[]{:S(2)}) copy-start(bf16[32,16384]{1,0:T(8,128)(2,1)} %param.12) | copy-start | bytes 3145732
  5.4 19.2 %all-to-all-start = ((f32[8,64,128]{2,1,0:T(8,128)}), f32[8,64,128]{2,1,0:T(8,128)S(1)}, u32[]{:S(2)}, u32[]{:S(2)}) async-start(f32[8,64,128]{2,1,0:T(8,128)} %bitcast.9), calls=%async_computation | async-start | bytes 524288 | tf_op jit(solution)/shard_map/all_to_all | solution.py:277
  15.6 22.9 %collective-permute-start.1 = (bf16[32,4096]{1,0:T(8,128)(2,1)S(1)}, bf16[32,4096]{1,0:T(8,128)(2,1)S(1)}, u32[]{:S(2)}, u32[]{:S(2)}) collective-permute-start(bf16[32,4096]{1,0:T(8,128)(2,1)S(1)} %constant_dynamic-slice_fusion.6), channel_id=1, source_target_pairs={{256,0},{257,1},{264,8},{265,9},{272,16},{273,17},{280,24},{281,25... | collective-permute-start | bytes 786440 | tf_op jit(solution)/shard_map/ppermute | solution.py:50
  17.7 20.8 %collective-permute-start = (bf16[32,8192]{1,0:T(8,128)(2,1)S(1)}, bf16[32,8192]{1,0:T(8,128)(2,1)S(1)}, u32[]{:S(2)}, u32[]{:S(2)}) collective-permute-start(bf16[32,8192]{1,0:T(8,128)(2,1)S(1)} %pad_maximum_fusion.1), channel_id=1, source_target_pairs={{8,0},{9,1},{0,8},{1,9},{24,16},{25,17},{16,24},{17,25},{40,32},{4... | collective-permute-start | bytes 1572872 | tf_op jit(solution)/shard_map/ppermute | solution.py:50
  20.7 3.9 %copy-start = (s32[3]{0:T(128)S(1)}, s32[3]{0:T(128)}, u32[]{:S(2)}) copy-start(s32[3]{0:T(128)} %pad_add_fusion.place_ref) | copy-start | bytes 40
  20.7 3.9 %copy-start.1 = (s32[4,32]{1,0:T(4,128)S(1)}, s32[4,32]{1,0:T(4,128)}, u32[]{:S(2)}) copy-start(s32[4,32]{1,0:T(4,128)} %mask_ref.1) | copy-start | bytes 1540
  20.7 3.9 %copy-start.2 = (s32[4]{0:T(128)S(1)}, s32[4]{0:T(128)}, u32[]{:S(2)}) copy-start(s32[4]{0:T(128)} %lengths_ref.1) | copy-start | bytes 52
  27.1 35.3 %all-to-all-start.1 = ((bf16[64,32,128]{2,1,0:T(8,128)(2,1)}), bf16[64,32,128]{2,1,0:T(8,128)(2,1)S(1)}, u32[]{:S(2)}, u32[]{:S(2)}) async-start(bf16[64,32,128]{2,1,0:T(8,128)(2,1)} %outer.1), calls=%async_computation.1 | async-start | bytes 1048576 | tf_op jit(solution)/shard_map/all_to_all | solution.py:240
  38.5 11.9 %collective-permute-start.2 = (bf16[32,2048]{1,0:T(8,128)(2,1)S(1)}, bf16[32,2048]{1,0:T(8,128)(2,1)S(1)}, u32[]{:S(2)}, u32[]{:S(2)}) collective-permute-start(bf16[32,2048]{1,0:T(8,128)(2,1)S(1)} %get-tuple-element.23), channel_id=1, source_target_pairs={{8,0},{9,1},{0,8},{1,9},{24,16},{25,17},{16,24},{17,25},{40,32},{4... | collective-permute-start | bytes 393224 | tf_op jit(solution)/shard_map/ppermute | solution.py:50
  41.5 14.5 %collective-permute-start.3 = (bf16[64,2048]{1,0:T(8,128)(2,1)S(1)}, bf16[64,2048]{1,0:T(8,128)(2,1)S(1)}, u32[]{:S(2)}, u32[]{:S(2)}) collective-permute-start(bf16[64,2048]{1,0:T(8,128)(2,1)S(1)} %pad_maximum_fusion.3), channel_id=1, source_target_pairs={{128,0},{129,1},{136,8},{137,9},{144,16},{145,17},{152,24},{153,25... | collective-permute-start | bytes 786440 | tf_op jit(solution)/shard_map/ppermute | solution.py:50
  45.8 12.9 %collective-permute-start.4 = (bf16[64,2048]{1,0:T(8,128)(2,1)S(1)}, bf16[64,2048]{1,0:T(8,128)(2,1)S(1)}, u32[]{:S(2)}, u32[]{:S(2)}) collective-permute-start(bf16[64,2048]{1,0:T(8,128)(2,1)S(1)} %pad_maximum_fusion.4), channel_id=1, source_target_pairs={{384,0},{385,1},{392,8},{393,9},{400,16},{401,17},{408,24},{409,25... | collective-permute-start | bytes 786440 | tf_op jit(solution)/shard_map/ppermute | solution.py:50
  50.5 12.1 %collective-permute-start.5 = (bf16[128,2048]{1,0:T(8,128)(2,1)S(1)}, bf16[128,2048]{1,0:T(8,128)(2,1)S(1)}, u32[]{:S(2)}, u32[]{:S(2)}) collective-permute-start(bf16[128,2048]{1,0:T(8,128)(2,1)S(1)} %pad_maximum_fusion.2.refs_0_), channel_id=1, source_target_pairs={{1,0},{0,1},{9,8},{8,9},{17,16},{16,17},{25,24},{24,25},{33,32},{3... | collective-permute-start | bytes 1572872 | tf_op jit(solution)/shard_map/ppermute | solution.py:50
  58.8 5.1 %collective-permute-start.6 = (bf16[128,2048]{1,0:T(8,128)(2,1)S(1)}, bf16[128,2048]{1,0:T(8,128)(2,1)S(1)}, u32[]{:S(2)}, u32[]{:S(2)}) collective-permute-start(bf16[128,2048]{1,0:T(8,128)(2,1)S(1)} %constant_dynamic-update-slice_fusion.refs_1_), channel_id=1, source_target_pairs={{1,0},{0,1},{9,8},{8,9},{17,16},{16,17},{25,24},{24,25},{33,32},{3... | collective-permute-start | bytes 1572872 | tf_op jit(solution)/shard_map/ppermute | solution.py:50
  65.9 4.7 %copy-start.4 = (s32[256,1]{0,1:T(1,128)S(1)}, s32[256,1]{0,1:T(1,128)}, u32[]{:S(2)}) copy-start(s32[256,1]{0,1:T(1,128)} %param.15) | copy-start | bytes 3076
  65.9 11.9 %all-to-all-start.2 = ((f32[16,32,128]{2,1,0:T(8,128)}), f32[16,32,128]{2,1,0:T(8,128)S(1)}, u32[]{:S(2)}, u32[]{:S(2)}) async-start(f32[16,32,128]{2,1,0:T(8,128)} %score.1), calls=%async_computation.2 | async-start | bytes 524288 | tf_op jit(solution)/shard_map/all_to_all | solution.py:240

commit v4 on v3

--- a/solution.py
+++ b/solution.py
@@ -62,20 +62,24 @@
     return swapped(block, lambda x, y, z, c: (x, y, z, c ^ 1))
 
 
+def here():
+    dp, tensor = lax.axis_index("dp"), lax.axis_index("tensor")
+    return dp >> 4, tensor >> 1, dp & 1, tensor & 1
+
+
 def project_kernel(
-    place_ref, in_ref, grad_ref, in_proj_ref, out_proj_ref, out_ref,
-    in_buf, grad_buf, in_proj_buf, out_proj_buf, sems,
+    in_ref, grad_ref, in_proj_ref, out_proj_ref, out_ref, in_buf, grad_buf, in_proj_buf, out_proj_buf, sems
 ):
-    x = place_ref[0]
+    x, _, _, _ = here()
     sources = (in_ref, grad_ref, in_proj_ref, out_proj_ref)
     buffers = (in_buf, grad_buf, in_proj_buf, out_proj_buf)
     copies = []
-    for j in range(LAYERS):
+    for layer in range(LAYERS):
         copies.append([
-            pltpu.make_async_copy(source.at[x ^ j], buffer.at[j], sems.at[j, i])
+            pltpu.make_async_copy(source.at[layer], buffer.at[layer], sems.at[layer, i])
             for i, (source, buffer) in enumerate(zip(sources, buffers))
         ])
-        for copy in copies[j]:
+        for copy in copies[layer]:
             copy.start()
 
     def side(rows, proj):
@@ -83,19 +87,20 @@
             rows.reshape(-1, rows.shape[-1]), proj, (((1,), (1,)), ((), ())), preferred_element_type=jnp.float32
         )
 
-    for j in range(LAYERS):
-        for copy in copies[j]:
+    for layer in range(LAYERS):
+        for copy in copies[layer]:
             copy.wait()
-        out_ref[j] = jnp.concatenate([side(in_buf[j], in_proj_buf[j]), side(grad_buf[j], out_proj_buf[j])], axis=1)
-
-
-def project(place, query_inputs, query_output_grads, in_projection, out_projection):
+        both = [side(in_buf[layer], in_proj_buf[layer]), side(grad_buf[layer], out_proj_buf[layer])]
+        out_ref[pl.ds(x ^ layer, 1)] = jnp.concatenate(both, axis=1)[None]
+
+
+def project(query_inputs, query_output_grads, in_projection, out_projection):
     _, queries, seq, depth = query_inputs.shape
     hbm = pl.BlockSpec(memory_space=pltpu.HBM)
     return pl.pallas_call(
         project_kernel,
         out_shape=jax.ShapeDtypeStruct((LAYERS, queries * seq, 2 * WIDTH), jnp.float32),
-        in_specs=[pl.BlockSpec(memory_space=pltpu.SMEM)] + [hbm] * 4,
+        in_specs=[hbm] * 4,
         out_specs=pl.BlockSpec(memory_space=pltpu.VMEM),
         scratch_shapes=[
             pltpu.VMEM(query_inputs.shape, query_inputs.dtype),
@@ -106,11 +111,11 @@
         ],
         compiler_params=pltpu.CompilerParams(vmem_limit_bytes=60 * 1024 * 1024),
         name="project",
-    )(place, query_inputs, query_output_grads, in_projection, out_projection)
-
-
-def outer_kernel(place_ref, lengths_ref, mask_ref, parts_ref, out_ref, rows_ref):
-    core = place_ref[1]
+    )(query_inputs, query_output_grads, in_projection, out_projection)
+
+
+def outer_kernel(lengths_ref, mask_ref, parts_ref, out_ref, rows_ref):
+    _, _, _, core = here()
     total = parts_ref[0]
     for part in range(1, parts_ref.shape[0]):
         total = total + parts_ref[part]
@@ -136,19 +141,19 @@
         out_ref[m] = block[(m & 1) * half : (m & 1) * half + half]
 
 
-def outer(place, lengths, loss_mask, parts, members):
+def outer(lengths, loss_mask, parts, members):
     smem = pl.BlockSpec(memory_space=pltpu.SMEM)
     vmem = pl.BlockSpec(memory_space=pltpu.VMEM)
     return pl.pallas_call(
         outer_kernel,
         out_shape=jax.ShapeDtypeStruct((members, PAIRS, LANES), jnp.bfloat16),
-        in_specs=[smem, smem, vmem, vmem],
+        in_specs=[smem, vmem, vmem],
         out_specs=vmem,
         scratch_shapes=[pltpu.VMEM((2 * PAIRS, LANES), jnp.float32)],
         compiler_params=pltpu.CompilerParams(vmem_limit_bytes=16 * 1024 * 1024),
         cost_estimate=pl.CostEstimate(flops=0, bytes_accessed=60 * 1024 * 1024, transcendentals=0),
         name="outer",
-    )(place, lengths, loss_mask, parts)
+    )(lengths, loss_mask, parts)
 
 
 def finish_kernel(parts_ref, domains_ref, scores_ref, influence_ref):
@@ -160,9 +165,9 @@
 
     total = jnp.concatenate([half(core) for core in range(NC)], axis=1)
     queries = total.shape[1]
-    here = lax.broadcasted_iota(jnp.int32, (queries, queries), 0)
+    column = lax.broadcasted_iota(jnp.int32, (queries, queries), 0)
     there = lax.broadcasted_iota(jnp.int32, (queries, queries), 1)
-    target = ((here & 63) << 2) + ((here >> 7) << 1) + ((here >> 6) & 1)
+    target = ((column & 63) << 2) + ((column >> 7) << 1) + ((column >> 6) & 1)
     place = (target == there).astype(jnp.float32)
     scores = jnp.dot(total, place, precision=lax.Precision.HIGHEST, preferred_element_type=jnp.float32)
     scores_ref[...] = scores
@@ -187,9 +192,9 @@
     )(parts, domains)
 
 
-def score_kernel(place_ref, *refs):
+def score_kernel(*refs):
     *rows_refs, blocks_ref, out_ref, rows_buf, queries_buf = refs
-    x, core, z_low = place_ref[0], place_ref[1], place_ref[2]
+    x, _, z_low, core = here()
     lines, sources, lanes = blocks_ref.shape
     for line in range(lines):
         pair, query = line // 2, line % 2
@@ -211,8 +216,7 @@
                 at += rows
 
 
-def score(place, rows, blocks):
-    smem = pl.BlockSpec(memory_space=pltpu.SMEM)
+def score(rows, blocks):
     vmem = pl.BlockSpec(memory_space=pltpu.VMEM)
     count = sum(block.shape[0] for block in rows)
     width = rows[0].shape[1]
@@ -221,7 +225,7 @@
     return pl.pallas_call(
         score_kernel,
         out_shape=jax.ShapeDtypeStruct((members, count // members, queries), jnp.float32),
-        in_specs=[smem] + [vmem] * (len(rows) + 1),
+        in_specs=[vmem] * (len(rows) + 1),
         out_specs=vmem,
         scratch_shapes=[
             pltpu.VMEM((count, width), jnp.bfloat16),
@@ -229,7 +233,7 @@
         ],
         compiler_params=pltpu.CompilerParams(vmem_limit_bytes=24 * 1024 * 1024),
         name="score",
-    )(place, *rows, blocks)
+    )(*rows, blocks)
 
 
 def after(block, *others):
@@ -250,9 +254,7 @@
     loss_mask,
     domains,
 ):
-    dp, tensor = lax.axis_index("dp"), lax.axis_index("tensor")
-    x, z_low, core, y_lo = dp >> 4, dp & 1, tensor & 1, tensor >> 1
-    place = jnp.stack([x, core, z_low]).astype(jnp.int32)
+    x, y_lo, z_low, _ = here()
     count, ktot = train_grads.shape
     width = ktot // LAYERS // 2
 
@@ -271,9 +273,8 @@
 
     layer = lax.dynamic_slice_in_dim(train_grads, (x ^ y_lo ^ 2) * 2 * width, 2 * width, axis=1)
     layer = after(swap_x(layer, 2), other)
-    parts = project(place, query_inputs, query_output_grads, in_projection, out_projection)
+    parts = project(query_inputs, query_output_grads, in_projection, out_projection)
     parts = parts.reshape(2 * LAYERS, -1, 2 * WIDTH)
-
     parts = lax.all_to_all(parts, "tensor", 0, 0)
 
     across = [
@@ -285,13 +286,12 @@
         jnp.concatenate([columns(0)] + across, axis=0),
         jnp.concatenate([swap_x(columns(step), step) for step in STEPS[2:]], axis=0),
     ]
-    blocks = outer(place, lengths, loss_mask, parts, len(class_members(0, 0, 0, 0)))
-
+    blocks = outer(lengths, loss_mask, parts, len(class_members(0, 0, 0, 0)))
     blocks = exchange(blocks, class_members)
     blocks = blocks.transpose(1, 0, 2)
     rows += [swap_core(block) for block in rows]
 
-    parts = exchange(score(place, rows, blocks), sharing_members)
+    parts = exchange(score(rows, blocks), sharing_members)
     scores, influence = finish(parts, domains)
     return scores, influence.T
 

time: 79.6 us -> 77.7 us (0.976)
  Pallas kernels: 9.84 us -> 8.57 us
where the time goes in v4:
time: 77.7 us; the launch traced here: 77.2 us
  starting transfers between devices  52.1 us (67%)
  waiting for transfers between devices  14.8 us (19%)
  Pallas kernels  8.57 us (11%)
  between operations  0.92 us (1%)
    ppermute x7, starting transfers between devices, swapped(): lax.ppermute(block, AXES, [(flat(*change(*p)), flat(*p)) for p in places()])  25.7 us
    all_to_all x2, starting transfers between devices, exchange(): lax.all_to_all(blocks, AXES, 0, 0, axis_index_groups=partition(members))  16.1 us
    all_to_all x1, starting transfers between devices, body(): parts = lax.all_to_all(parts, 'tensor', 0, 0)  10.2 us
    all_to_all x2, waiting for transfers between devices, exchange(): lax.all_to_all(blocks, AXES, 0, 0, axis_index_groups=partition(members))  7.03 us
    ppermute x7, waiting for transfers between devices, swapped(): lax.ppermute(block, AXES, [(flat(*change(*p)), flat(*p)) for p in places()])  3.94 us
    all_to_all x1, waiting for transfers between devices, body(): parts = lax.all_to_all(parts, 'tensor', 0, 0)  3.87 us
    pallas_call x1, Pallas kernels, project(): pl.pallas_call(project_kernel, out_shape=jax.ShapeDtypeStruct((LAYERS, qu...  3.45 us
    pallas_call x1, Pallas kernels, outer(): pl.pallas_call(outer_kernel, out_shape=jax.ShapeDtypeStruct((members, PAI...  2.45 us
  transfers between devices with their start and end apart: 10, of which 4 were waited for; matrix products, arithmetic and copies ran while one was open for 1% of the time, Pallas kernels for 3%

profile of v4, /device:TPU:1, one launch (start us, length us, event | category | flops | bytes accessed | tf_op | source)
XLA Modules:
  0.0 77.2 jit_solution(10720920180236471061)
XLA Ops:
  0.6 0.0 copy-start.2
  0.6 3.5 %project.1 = f32[4,128,128]{2,1,0:T(8,128)} custom-call(bf16[4,4,32,1024]{3,2,1,0:T(8,128)(2,1)} %in_ref.1, bf16[4,4,32,1024]{3,2,1,0:T(8,128)(2,1)} %grad_ref.1, bf16[4,64,1024]{2,1,0:T(8,128)(2,1)} %in_proj_ref.1, bf16[4,64,1024]{2,1,0:T(8,128)(2,1)} %out_proj_ref.1), custom_call_target="tpu_custom_call" | custom-call | tf_op jit(solution)/shard_map/project/pallas_call | solution.py:100
  4.1 10.2 %all-to-all-start = ((f32[8,64,128]{2,1,0:T(8,128)}), f32[8,64,128]{2,1,0:T(8,128)S(1)}, u32[]{:S(2)}, u32[]{:S(2)}) async-start(f32[8,64,128]{2,1,0:T(8,128)} %bitcast.6), calls=%async_computation | async-start | bytes 524288 | tf_op jit(solution)/shard_map/all_to_all | solution.py:278
  14.3 0.0 copy-done.2
  14.3 1.9 %collective-permute-start.1 = (bf16[32,4096]{1,0:T(8,128)(2,1)S(1)}, bf16[32,4096]{1,0:T(8,128)(2,1)S(1)}, u32[]{:S(2)}, u32[]{:S(2)}) collective-permute-start(bf16[32,4096]{1,0:T(8,128)(2,1)S(1)} %constant_dynamic-slice_fusion.6), channel_id=1, source_target_pairs={{256,0},{257,1},{264,8},{265,9},{272,16},{273,17},{280,24},{281,25... | collective-permute-start | bytes 786440 | tf_op jit(solution)/shard_map/ppermute | solution.py:50
  16.3 0.1 constant_dynamic-slice_fusion.16
  16.4 2.9 %collective-permute-start = (bf16[32,8192]{1,0:T(8,128)(2,1)S(1)}, bf16[32,8192]{1,0:T(8,128)(2,1)S(1)}, u32[]{:S(2)}, u32[]{:S(2)}) collective-permute-start(bf16[32,8192]{1,0:T(8,128)(2,1)S(1)} %pad_maximum_fusion.1), channel_id=1, source_target_pairs={{8,0},{9,1},{0,8},{1,9},{24,16},{25,17},{16,24},{17,25},{40,32},{4... | collective-permute-start | bytes 1572872 | tf_op jit(solution)/shard_map/ppermute | solution.py:50
  19.4 0.0 copy-start
  19.4 0.0 copy-start.1
  19.5 3.9 %all-to-all-done.parts_ref = f32[8,64,128]{2,1,0:T(8,128)S(1)} async-done(((f32[8,64,128]{2,1,0:T(8,128)}), f32[8,64,128]{2,1,0:T(8,128)S(1)}, u32[]{:S(2)}, u32[]{:S(2)}) %all-to-all-start) | async-done | bytes 262176 | tf_op jit(solution)/shard_map/all_to_all | solution.py:278
  23.3 0.0 copy-done
  23.3 2.4 %outer.1 = bf16[64,32,128]{2,1,0:T(8,128)(2,1)} custom-call(s32[4]{0:T(128)S(1)} %copy-done.1, s32[4,32]{1,0:T(4,128)S(1)} %copy-done, f32[8,64,128]{2,1,0:T(8,128)S(1)} %all-to-all-done.parts_ref), custom_call_target="tpu_custom_call" | custom-call | bytes 62914560 | tf_op jit(solution)/shard_map/outer/pallas_call | solution.py:147
  25.8 11.4 %all-to-all-start.1 = ((bf16[64,32,128]{2,1,0:T(8,128)(2,1)}), bf16[64,32,128]{2,1,0:T(8,128)(2,1)S(1)}, u32[]{:S(2)}, u32[]{:S(2)}) async-start(bf16[64,32,128]{2,1,0:T(8,128)(2,1)} %outer.1), calls=%async_computation.1 | async-start | bytes 1048576 | tf_op jit(solution)/shard_map/all_to_all | solution.py:244
  37.2 0.0 collective-permute-done.1
  37.2 0.0 collective-permute-done
  37.2 2.9 %collective-permute-start.2 = (bf16[32,2048]{1,0:T(8,128)(2,1)S(1)}, bf16[32,2048]{1,0:T(8,128)(2,1)S(1)}, u32[]{:S(2)}, u32[]{:S(2)}) collective-permute-start(bf16[32,2048]{1,0:T(8,128)(2,1)S(1)} %get-tuple-element.23), channel_id=1, source_target_pairs={{8,0},{9,1},{0,8},{1,9},{24,16},{25,17},{16,24},{17,25},{40,32},{4... | collective-permute-start | bytes 393224 | tf_op jit(solution)/shard_map/ppermute | solution.py:50
  40.2 4.3 %collective-permute-start.3 = (bf16[64,2048]{1,0:T(8,128)(2,1)S(1)}, bf16[64,2048]{1,0:T(8,128)(2,1)S(1)}, u32[]{:S(2)}, u32[]{:S(2)}) collective-permute-start(bf16[64,2048]{1,0:T(8,128)(2,1)S(1)} %pad_maximum_fusion.3), channel_id=1, source_target_pairs={{128,0},{129,1},{136,8},{137,9},{144,16},{145,17},{152,24},{153,25... | collective-permute-start | bytes 786440 | tf_op jit(solution)/shard_map/ppermute | solution.py:50
  44.6 4.6 %collective-permute-start.4 = (bf16[64,2048]{1,0:T(8,128)(2,1)S(1)}, bf16[64,2048]{1,0:T(8,128)(2,1)S(1)}, u32[]{:S(2)}, u32[]{:S(2)}) collective-permute-start(bf16[64,2048]{1,0:T(8,128)(2,1)S(1)} %pad_maximum_fusion.4), channel_id=1, source_target_pairs={{384,0},{385,1},{392,8},{393,9},{400,16},{401,17},{408,24},{409,25... | collective-permute-start | bytes 786440 | tf_op jit(solution)/shard_map/ppermute | solution.py:50
  49.2 0.0 collective-permute-done.2
  49.2 5.5 %collective-permute-start.5 = (bf16[128,2048]{1,0:T(8,128)(2,1)S(1)}, bf16[128,2048]{1,0:T(8,128)(2,1)S(1)}, u32[]{:S(2)}, u32[]{:S(2)}) collective-permute-start(bf16[128,2048]{1,0:T(8,128)(2,1)S(1)} %pad_maximum_fusion.2.refs_0_), channel_id=1, source_target_pairs={{1,0},{0,1},{9,8},{8,9},{17,16},{16,17},{25,24},{24,25},{33,32},{3... | collective-permute-start | bytes 1572872 | tf_op jit(solution)/shard_map/ppermute | solution.py:50
  54.8 0.0 collective-permute-done.3
  54.8 2.6 %collective-permute-done.4 = bf16[64,2048]{1,0:T(8,128)(2,1)S(1)} collective-permute-done((bf16[64,2048]{1,0:T(8,128)(2,1)S(1)}, bf16[64,2048]{1,0:T(8,128)(2,1)S(1)}, u32[]{:S(2)}, u32[]{:S(2)}) %collective-permute-start.4) | collective-permute-done | bytes 262176 | tf_op jit(solution)/shard_map/ppermute | solution.py:50
  57.5 3.6 %collective-permute-start.6 = (bf16[128,2048]{1,0:T(8,128)(2,1)S(1)}, bf16[128,2048]{1,0:T(8,128)(2,1)S(1)}, u32[]{:S(2)}, u32[]{:S(2)}) collective-permute-start(bf16[128,2048]{1,0:T(8,128)(2,1)S(1)} %constant_dynamic-update-slice_fusion.refs_1_), channel_id=1, source_target_pairs={{1,0},{0,1},{9,8},{8,9},{17,16},{16,17},{25,24},{24,25},{33,32},{3... | collective-permute-start | bytes 1572872 | tf_op jit(solution)/shard_map/ppermute | solution.py:50
  61.1 0.0 all-to-all-done.1
  61.1 0.2 copy.15
  61.3 0.0 collective-permute-done.5.refs_2_
  61.3 1.3 %collective-permute-done.6.refs_3_ = bf16[128,2048]{1,0:T(8,128)(2,1)S(1)} collective-permute-done((bf16[128,2048]{1,0:T(8,128)(2,1)S(1)}, bf16[128,2048]{1,0:T(8,128)(2,1)S(1)}, u32[]{:S(2)}, u32[]{:S(2)}) %collective-permute-start.6) | collective-permute-done | bytes 524320 | tf_op jit(solution)/shard_map/ppermute | solution.py:50
  62.6 1.4 %score.1 = f32[16,32,128]{2,1,0:T(8,128)} custom-call(bf16[128,2048]{1,0:T(8,128)(2,1)S(1)} %pad_maximum_fusion.2.refs_0_, bf16[128,2048]{1,0:T(8,128)(2,1)S(1)} %constant_dynamic-update-slice_fusion.refs_1_, bf16[128,2048]{1,0:T(8,128)(2,1)S(1)} %collective-permute-done.5.refs_2_, bf16[128,2048]{1,0:T(8,128)(2,1)S(1)} %collective-permute-done.6.refs_3_, ...), custom_call_target="tpu_custom_call" | custom-call | tf_op jit(solution)/shard_map/score/pallas_call | solution.py:225
  64.0 4.7 %all-to-all-start.2 = ((f32[16,32,128]{2,1,0:T(8,128)}), f32[16,32,128]{2,1,0:T(8,128)S(1)}, u32[]{:S(2)}, u32[]{:S(2)}) async-start(f32[16,32,128]{2,1,0:T(8,128)} %score.1), calls=%async_computation.2 | async-start | bytes 524288 | tf_op jit(solution)/shard_map/all_to_all | solution.py:244
  68.7 0.1 copy.13.domains_ref
  68.9 7.0 %all-to-all-done.2.parts_ref = f32[16,32,128]{2,1,0:T(8,128)S(1)} async-done(((f32[16,32,128]{2,1,0:T(8,128)}), f32[16,32,128]{2,1,0:T(8,128)S(1)}, u32[]{:S(2)}, u32[]{:S(2)}) %all-to-all-start.2) | async-done | bytes 262176 | tf_op jit(solution)/shard_map/all_to_all | solution.py:244
  75.9 1.2 %finish.1 = (f32[32,256]{1,0:T(8,128)}, f32[8,32]{1,0:T(8,128)}) custom-call(f32[16,32,128]{2,1,0:T(8,128)S(1)} %all-to-all-done.2.parts_ref, s32[256,1]{1,0:T(8,128)S(1)} %copy.13.domains_ref), custom_call_target="tpu_custom_call" | custom-call | tf_op jit(solution)/shard_map/finish/pallas_call | solution.py:184
  (14 shorter events, 0.3 us)
Async XLA Ops:
  0.6 13.7 %copy-start.2 = (bf16[32,16384]{1,0:T(8,128)(2,1)S(1)}, bf16[32,16384]{1,0:T(8,128)(2,1)}, u32[]{:S(2)}) copy-start(bf16[32,16384]{1,0:T(8,128)(2,1)} %param.12) | copy-start | bytes 3145732
  4.1 19.2 %all-to-all-start = ((f32[8,64,128]{2,1,0:T(8,128)}), f32[8,64,128]{2,1,0:T(8,128)S(1)}, u32[]{:S(2)}, u32[]{:S(2)}) async-start(f32[8,64,128]{2,1,0:T(8,128)} %bitcast.6), calls=%async_computation | async-start | bytes 524288 | tf_op jit(solution)/shard_map/all_to_all | solution.py:278
  14.3 22.9 %collective-permute-start.1 = (bf16[32,4096]{1,0:T(8,128)(2,1)S(1)}, bf16[32,4096]{1,0:T(8,128)(2,1)S(1)}, u32[]{:S(2)}, u32[]{:S(2)}) collective-permute-start(bf16[32,4096]{1,0:T(8,128)(2,1)S(1)} %constant_dynamic-slice_fusion.6), channel_id=1, source_target_pairs={{256,0},{257,1},{264,8},{265,9},{272,16},{273,17},{280,24},{281,25... | collective-permute-start | bytes 786440 | tf_op jit(solution)/shard_map/ppermute | solution.py:50
  16.4 20.8 %collective-permute-start = (bf16[32,8192]{1,0:T(8,128)(2,1)S(1)}, bf16[32,8192]{1,0:T(8,128)(2,1)S(1)}, u32[]{:S(2)}, u32[]{:S(2)}) collective-permute-start(bf16[32,8192]{1,0:T(8,128)(2,1)S(1)} %pad_maximum_fusion.1), channel_id=1, source_target_pairs={{8,0},{9,1},{0,8},{1,9},{24,16},{25,17},{16,24},{17,25},{40,32},{4... | collective-permute-start | bytes 1572872 | tf_op jit(solution)/shard_map/ppermute | solution.py:50
  19.4 3.9 %copy-start = (s32[4,32]{1,0:T(4,128)S(1)}, s32[4,32]{1,0:T(4,128)}, u32[]{:S(2)}) copy-start(s32[4,32]{1,0:T(4,128)} %mask_ref.1) | copy-start | bytes 1540
  19.4 3.9 %copy-start.1 = (s32[4]{0:T(128)S(1)}, s32[4]{0:T(128)}, u32[]{:S(2)}) copy-start(s32[4]{0:T(128)} %lengths_ref.1) | copy-start | bytes 52
  25.8 35.3 %all-to-all-start.1 = ((bf16[64,32,128]{2,1,0:T(8,128)(2,1)}), bf16[64,32,128]{2,1,0:T(8,128)(2,1)S(1)}, u32[]{:S(2)}, u32[]{:S(2)}) async-start(bf16[64,32,128]{2,1,0:T(8,128)(2,1)} %outer.1), calls=%async_computation.1 | async-start | bytes 1048576 | tf_op jit(solution)/shard_map/all_to_all | solution.py:244
  37.2 11.9 %collective-permute-start.2 = (bf16[32,2048]{1,0:T(8,128)(2,1)S(1)}, bf16[32,2048]{1,0:T(8,128)(2,1)S(1)}, u32[]{:S(2)}, u32[]{:S(2)}) collective-permute-start(bf16[32,2048]{1,0:T(8,128)(2,1)S(1)} %get-tuple-element.23), channel_id=1, source_target_pairs={{8,0},{9,1},{0,8},{1,9},{24,16},{25,17},{16,24},{17,25},{40,32},{4... | collective-permute-start | bytes 393224 | tf_op jit(solution)/shard_map/ppermute | solution.py:50
  40.2 14.5 %collective-permute-start.3 = (bf16[64,2048]{1,0:T(8,128)(2,1)S(1)}, bf16[64,2048]{1,0:T(8,128)(2,1)S(1)}, u32[]{:S(2)}, u32[]{:S(2)}) collective-permute-start(bf16[64,2048]{1,0:T(8,128)(2,1)S(1)} %pad_maximum_fusion.3), channel_id=1, source_target_pairs={{128,0},{129,1},{136,8},{137,9},{144,16},{145,17},{152,24},{153,25... | collective-permute-start | bytes 786440 | tf_op jit(solution)/shard_map/ppermute | solution.py:50
  44.6 12.9 %collective-permute-start.4 = (bf16[64,2048]{1,0:T(8,128)(2,1)S(1)}, bf16[64,2048]{1,0:T(8,128)(2,1)S(1)}, u32[]{:S(2)}, u32[]{:S(2)}) collective-permute-start(bf16[64,2048]{1,0:T(8,128)(2,1)S(1)} %pad_maximum_fusion.4), channel_id=1, source_target_pairs={{384,0},{385,1},{392,8},{393,9},{400,16},{401,17},{408,24},{409,25... | collective-permute-start | bytes 786440 | tf_op jit(solution)/shard_map/ppermute | solution.py:50
  49.2 12.1 %collective-permute-start.5 = (bf16[128,2048]{1,0:T(8,128)(2,1)S(1)}, bf16[128,2048]{1,0:T(8,128)(2,1)S(1)}, u32[]{:S(2)}, u32[]{:S(2)}) collective-permute-start(bf16[128,2048]{1,0:T(8,128)(2,1)S(1)} %pad_maximum_fusion.2.refs_0_), channel_id=1, source_target_pairs={{1,0},{0,1},{9,8},{8,9},{17,16},{16,17},{25,24},{24,25},{33,32},{3... | collective-permute-start | bytes 1572872 | tf_op jit(solution)/shard_map/ppermute | solution.py:50
  57.5 5.1 %collective-permute-start.6 = (bf16[128,2048]{1,0:T(8,128)(2,1)S(1)}, bf16[128,2048]{1,0:T(8,128)(2,1)S(1)}, u32[]{:S(2)}, u32[]{:S(2)}) collective-permute-start(bf16[128,2048]{1,0:T(8,128)(2,1)S(1)} %constant_dynamic-update-slice_fusion.refs_1_), channel_id=1, source_target_pairs={{1,0},{0,1},{9,8},{8,9},{17,16},{16,17},{25,24},{24,25},{33,32},{3... | collective-permute-start | bytes 1572872 | tf_op jit(solution)/shard_map/ppermute | solution.py:50
  64.0 4.7 %copy-start.3 = (s32[256,1]{0,1:T(1,128)S(1)}, s32[256,1]{0,1:T(1,128)}, u32[]{:S(2)}) copy-start(s32[256,1]{0,1:T(1,128)} %param.15) | copy-start | bytes 3076
  64.0 11.9 %all-to-all-start.2 = ((f32[16,32,128]{2,1,0:T(8,128)}), f32[16,32,128]{2,1,0:T(8,128)S(1)}, u32[]{:S(2)}, u32[]{:S(2)}) async-start(f32[16,32,128]{2,1,0:T(8,128)} %score.1), calls=%async_computation.2 | async-start | bytes 524288 | tf_op jit(solution)/shard_map/all_to_all | solution.py:244

commit v5 on v4

--- a/solution.py
+++ b/solution.py
@@ -13,7 +13,7 @@
 DOMAINS = 8
 AXES = ("dp", "tensor")
 NX, NY, NZ, NC = 4, 8, 8, 2
-STEPS = (0, 2, 1, 3)
+ORDER = ((0, 0), (0, 1), (2, 0), (1, 0), (1, 1), (3, 0), (3, 1), (2, 1))
 LANES = 128
 PAIRS = WIDTH * WIDTH // LANES
 
@@ -114,7 +114,7 @@
     )(query_inputs, query_output_grads, in_projection, out_projection)
 
 
-def outer_kernel(lengths_ref, mask_ref, parts_ref, out_ref, rows_ref):
+def outer_kernel(lengths_ref, mask_ref, parts_ref, out_ref, rows_ref, blocks_buf, sems):
     _, _, _, core = here()
     total = parts_ref[0]
     for part in range(1, parts_ref.shape[0]):
@@ -122,38 +122,49 @@
     row = lax.broadcasted_iota(jnp.int32, (SEQ, SEQ), 0)
     col = lax.broadcasted_iota(jnp.int32, (SEQ, SEQ), 1)
     first = lax.broadcasted_iota(jnp.int32, (SEQ, LANES), 1) < WIDTH
+    inner, weighted = [], []
     for k in range(2):
         mask = jnp.where(core == 0, mask_ref[k : k + 1, :], mask_ref[2 + k : 3 + k, :])
         kept = (row == col) & (col < lengths_ref[2 * core + k])
         weight = jnp.sum(jnp.where(kept, mask, 0).astype(jnp.float32), axis=1, keepdims=True)
         factors = total[k * SEQ : (k + 1) * SEQ]
-        inner = factors[:, :WIDTH]
-        inner = jnp.concatenate([inner, inner], axis=1)
-        weighted = factors[:, WIDTH:] * weight
-        for p in range(PAIRS):
-            low = jnp.broadcast_to(weighted[:, 2 * p : 2 * p + 1], (SEQ, LANES))
-            high = jnp.broadcast_to(weighted[:, 2 * p + 1 : 2 * p + 2], (SEQ, LANES))
-            product = jnp.where(first, low, high) * inner
-            rows_ref[2 * p + k : 2 * p + k + 1, :] = jnp.sum(product, axis=0, keepdims=True)
-    block = rows_ref[...].astype(jnp.bfloat16)
-    half = out_ref.shape[1]
-    for m in range(out_ref.shape[0]):
-        out_ref[m] = block[(m & 1) * half : (m & 1) * half + half]
+        inner.append(jnp.concatenate([factors[:, :WIDTH]] * 2, axis=1))
+        weighted.append(factors[:, WIDTH:] * weight)
+    members, half, _ = blocks_buf.shape[1:]
+    copies = []
+    for part in range(2):
+        for p in range(part * half // 2, (part + 1) * half // 2):
+            for k in range(2):
+                low = jnp.broadcast_to(weighted[k][:, 2 * p : 2 * p + 1], (SEQ, LANES))
+                high = jnp.broadcast_to(weighted[k][:, 2 * p + 1 : 2 * p + 2], (SEQ, LANES))
+                product = jnp.where(first, low, high) * inner[k]
+                rows_ref[2 * p + k : 2 * p + k + 1, :] = jnp.sum(product, axis=0, keepdims=True)
+        block = rows_ref[part * half : (part + 1) * half, :].astype(jnp.bfloat16)
+        for m in range(members):
+            blocks_buf[part, m] = block
+        copies.append(pltpu.make_async_copy(blocks_buf.at[part], out_ref.at[:, part], sems.at[part]))
+        copies[part].start()
+    for copy in copies:
+        copy.wait()
 
 
 def outer(lengths, loss_mask, parts, members):
-    smem = pl.BlockSpec(memory_space=pltpu.SMEM)
     vmem = pl.BlockSpec(memory_space=pltpu.VMEM)
-    return pl.pallas_call(
+    blocks = pl.pallas_call(
         outer_kernel,
-        out_shape=jax.ShapeDtypeStruct((members, PAIRS, LANES), jnp.bfloat16),
-        in_specs=[smem, vmem, vmem],
-        out_specs=vmem,
-        scratch_shapes=[pltpu.VMEM((2 * PAIRS, LANES), jnp.float32)],
+        out_shape=jax.ShapeDtypeStruct((members // 2, 2, PAIRS, LANES), jnp.bfloat16),
+        in_specs=[pl.BlockSpec(memory_space=pltpu.SMEM), vmem, vmem],
+        out_specs=pl.BlockSpec(memory_space=pltpu.HBM),
+        scratch_shapes=[
+            pltpu.VMEM((2 * PAIRS, LANES), jnp.float32),
+            pltpu.VMEM((2, members // 2, PAIRS, LANES), jnp.bfloat16),
+            pltpu.SemaphoreType.DMA((2,)),
+        ],
         compiler_params=pltpu.CompilerParams(vmem_limit_bytes=16 * 1024 * 1024),
         cost_estimate=pl.CostEstimate(flops=0, bytes_accessed=60 * 1024 * 1024, transcendentals=0),
         name="outer",
     )(lengths, loss_mask, parts)
+    return blocks.reshape(members, PAIRS, LANES)
 
 
 def finish_kernel(parts_ref, domains_ref, scores_ref, influence_ref):
@@ -209,11 +220,10 @@
     rows = out_ref.shape[1]
     at = 0
     for other_core in range(NC):
-        for step in STEPS:
-            for other_z in range(2):
-                member = ((x ^ step) * 2 + (z_low ^ other_z)) * NC + (core ^ other_core)
-                out_ref[pl.ds(member, 1)] = result[at : at + rows][None]
-                at += rows
+        for step, other_z in ORDER:
+            member = ((x ^ step) * 2 + (z_low ^ other_z)) * NC + (core ^ other_core)
+            out_ref[pl.ds(member, 1)] = result[at : at + rows][None]
+            at += rows
 
 
 def score(rows, blocks):
@@ -282,9 +292,10 @@
         swap_z(lax.dynamic_slice_in_dim(layer, (1 - z_low) * width, width, axis=1)),
     ]
 
+    ring = [swap_x(columns(step), step) for step in (1, 3)]
     rows = [
-        jnp.concatenate([columns(0)] + across, axis=0),
-        jnp.concatenate([swap_x(columns(step), step) for step in STEPS[2:]], axis=0),
+        jnp.concatenate([columns(0), across[0], ring[0]], axis=0),
+        jnp.concatenate([ring[1], across[1]], axis=0),
     ]
     blocks = outer(lengths, loss_mask, parts, len(class_members(0, 0, 0, 0)))
     blocks = exchange(blocks, class_members)

time: 77.7 us -> 75.7 us (0.974)
  starting transfers between devices: 52.1 us -> 49.7 us
    ppermute x7, starting transfers between devices: 25.7 us -> 23.6 us  [swapped(): lax.ppermute(block, AXES, [(flat(*change(*p)), flat(*p)) for p in places()])]
  transfers between devices with their start and end apart: 10 -> 10, of which waited for: 4 -> 6; matrix products, arithmetic and copies ran while one was open for 1% -> 1% of each run, Pallas kernels for 3% -> 3%
where the time goes in v5:
time: 75.7 us; the launch traced here: 75.1 us
  starting transfers between devices  49.7 us (66%)
  waiting for transfers between devices  15.4 us (20%)
  Pallas kernels  8.37 us (11%)
  between operations  0.9 us (1%)
    ppermute x7, starting transfers between devices, swapped(): lax.ppermute(block, AXES, [(flat(*change(*p)), flat(*p)) for p in places()])  23.6 us
    all_to_all x2, starting transfers between devices, exchange(): lax.all_to_all(blocks, AXES, 0, 0, axis_index_groups=partition(members))  15.9 us
    all_to_all x1, starting transfers between devices, body(): parts = lax.all_to_all(parts, 'tensor', 0, 0)  10.2 us
    all_to_all x2, waiting for transfers between devices, exchange(): lax.all_to_all(blocks, AXES, 0, 0, axis_index_groups=partition(members))  7.03 us
    ppermute x7, waiting for transfers between devices, swapped(): lax.ppermute(block, AXES, [(flat(*change(*p)), flat(*p)) for p in places()])  4.49 us
    all_to_all x1, waiting for transfers between devices, body(): parts = lax.all_to_all(parts, 'tensor', 0, 0)  3.87 us
    pallas_call x1, Pallas kernels, project(): pl.pallas_call(project_kernel, out_shape=jax.ShapeDtypeStruct((LAYERS, qu...  3.45 us
    pallas_call x1, Pallas kernels, outer(): pl.pallas_call(outer_kernel, out_shape=jax.ShapeDtypeStruct((members // 2...  2.24 us
  transfers between devices with their start and end apart: 10, of which 6 were waited for; matrix products, arithmetic and copies ran while one was open for 1% of the time, Pallas kernels for 3%

profile of v5, /device:TPU:1, one launch (start us, length us, event | category | flops | bytes accessed | tf_op | source)
XLA Modules:
  0.0 75.1 jit_solution(2610119417983599865)
XLA Ops:
  0.6 0.0 copy-start.2
  0.6 3.5 %project.1 = f32[4,128,128]{2,1,0:T(8,128)} custom-call(bf16[4,4,32,1024]{3,2,1,0:T(8,128)(2,1)} %in_ref.1, bf16[4,4,32,1024]{3,2,1,0:T(8,128)(2,1)} %grad_ref.1, bf16[4,64,1024]{2,1,0:T(8,128)(2,1)} %in_proj_ref.1, bf16[4,64,1024]{2,1,0:T(8,128)(2,1)} %out_proj_ref.1), custom_call_target="tpu_custom_call" | custom-call | tf_op jit(solution)/shard_map/project/pallas_call | solution.py:100
  4.1 10.2 %all-to-all-start = ((f32[8,64,128]{2,1,0:T(8,128)}), f32[8,64,128]{2,1,0:T(8,128)S(1)}, u32[]{:S(2)}, u32[]{:S(2)}) async-start(f32[8,64,128]{2,1,0:T(8,128)} %bitcast.7), calls=%async_computation | async-start | bytes 524288 | tf_op jit(solution)/shard_map/all_to_all | solution.py:288
  14.3 0.0 copy-done.2
  14.3 1.9 %collective-permute-start.1 = (bf16[32,4096]{1,0:T(8,128)(2,1)S(1)}, bf16[32,4096]{1,0:T(8,128)(2,1)S(1)}, u32[]{:S(2)}, u32[]{:S(2)}) collective-permute-start(bf16[32,4096]{1,0:T(8,128)(2,1)S(1)} %constant_dynamic-slice_fusion.6), channel_id=1, source_target_pairs={{256,0},{257,1},{264,8},{265,9},{272,16},{273,17},{280,24},{281,25... | collective-permute-start | bytes 786440 | tf_op jit(solution)/shard_map/ppermute | solution.py:50
  16.3 0.1 constant_dynamic-slice_fusion.16
  16.4 0.0 copy-start
  16.4 0.0 copy-start.1
  16.4 2.9 %collective-permute-start = (bf16[32,8192]{1,0:T(8,128)(2,1)S(1)}, bf16[32,8192]{1,0:T(8,128)(2,1)S(1)}, u32[]{:S(2)}, u32[]{:S(2)}) collective-permute-start(bf16[32,8192]{1,0:T(8,128)(2,1)S(1)} %pad_maximum_fusion.2), channel_id=1, source_target_pairs={{8,0},{9,1},{0,8},{1,9},{24,16},{25,17},{16,24},{17,25},{40,32},{4... | collective-permute-start | bytes 1572872 | tf_op jit(solution)/shard_map/ppermute | solution.py:50
  19.5 3.9 %all-to-all-done.parts_ref = f32[8,64,128]{2,1,0:T(8,128)S(1)} async-done(((f32[8,64,128]{2,1,0:T(8,128)}), f32[8,64,128]{2,1,0:T(8,128)S(1)}, u32[]{:S(2)}, u32[]{:S(2)}) %all-to-all-start) | async-done | bytes 262176 | tf_op jit(solution)/shard_map/all_to_all | solution.py:288
  23.3 2.2 %outer.1 = bf16[32,2,32,128]{3,2,1,0:T(8,128)(2,1)} custom-call(s32[4]{0:T(128)S(1)} %copy-done.1, s32[4,32]{1,0:T(4,128)S(1)} %copy-done, f32[8,64,128]{2,1,0:T(8,128)S(1)} %all-to-all-done.parts_ref), custom_call_target="tpu_custom_call" | custom-call | bytes 62914560 | tf_op jit(solution)/shard_map/outer/pallas_call | solution.py:153
  25.6 11.4 %all-to-all-start.1 = ((bf16[64,32,128]{2,1,0:T(8,128)(2,1)}), bf16[64,32,128]{2,1,0:T(8,128)(2,1)S(1)}, u32[]{:S(2)}, u32[]{:S(2)}) async-start(bf16[64,32,128]{2,1,0:T(8,128)(2,1)} %bitcast.1), calls=%async_computation.1 | async-start | bytes 1048576 | tf_op jit(solution)/shard_map/all_to_all | solution.py:254
  37.0 0.0 collective-permute-done
  37.1 4.1 %collective-permute-start.2 = (bf16[64,2048]{1,0:T(8,128)(2,1)S(1)}, bf16[64,2048]{1,0:T(8,128)(2,1)S(1)}, u32[]{:S(2)}, u32[]{:S(2)}) collective-permute-start(bf16[64,2048]{1,0:T(8,128)(2,1)S(1)} %pad_maximum_fusion.3), channel_id=1, source_target_pairs={{128,0},{129,1},{136,8},{137,9},{144,16},{145,17},{152,24},{153,25... | collective-permute-start | bytes 786440 | tf_op jit(solution)/shard_map/ppermute | solution.py:50
  41.2 0.0 collective-permute-done.1
  41.2 4.6 %collective-permute-start.3 = (bf16[64,2048]{1,0:T(8,128)(2,1)S(1)}, bf16[64,2048]{1,0:T(8,128)(2,1)S(1)}, u32[]{:S(2)}, u32[]{:S(2)}) collective-permute-start(bf16[64,2048]{1,0:T(8,128)(2,1)S(1)} %pad_maximum_fusion.4), channel_id=1, source_target_pairs={{384,0},{385,1},{392,8},{393,9},{400,16},{401,17},{408,24},{409,25... | collective-permute-start | bytes 786440 | tf_op jit(solution)/shard_map/ppermute | solution.py:50
  45.9 3.1 %collective-permute-start.4 = (bf16[32,2048]{1,0:T(8,128)(2,1)S(1)}, bf16[32,2048]{1,0:T(8,128)(2,1)S(1)}, u32[]{:S(2)}, u32[]{:S(2)}) collective-permute-start(bf16[32,2048]{1,0:T(8,128)(2,1)S(1)} %get-tuple-element.22), channel_id=1, source_target_pairs={{8,0},{9,1},{0,8},{1,9},{24,16},{25,17},{16,24},{17,25},{40,32},{4... | collective-permute-start | bytes 393224 | tf_op jit(solution)/shard_map/ppermute | solution.py:50
  49.0 1.8 %collective-permute-done.2 = bf16[64,2048]{1,0:T(8,128)(2,1)S(1)} collective-permute-done((bf16[64,2048]{1,0:T(8,128)(2,1)S(1)}, bf16[64,2048]{1,0:T(8,128)(2,1)S(1)}, u32[]{:S(2)}, u32[]{:S(2)}) %collective-permute-start.2) | collective-permute-done | bytes 262176 | tf_op jit(solution)/shard_map/ppermute | solution.py:50
  50.9 3.9 %collective-permute-start.5 = (bf16[160,2048]{1,0:T(8,128)(2,1)S(1)}, bf16[160,2048]{1,0:T(8,128)(2,1)S(1)}, u32[]{:S(2)}, u32[]{:S(2)}) collective-permute-start(bf16[160,2048]{1,0:T(8,128)(2,1)S(1)} %pad_maximum_fusion.refs_0_), channel_id=1, source_target_pairs={{1,0},{0,1},{9,8},{8,9},{17,16},{16,17},{25,24},{24,25},{33,32},{3... | collective-permute-start | bytes 1966088 | tf_op jit(solution)/shard_map/ppermute | solution.py:50
  54.8 0.6 collective-permute-done.3
  55.4 1.0 %collective-permute-done.4 = bf16[32,2048]{1,0:T(8,128)(2,1)S(1)} collective-permute-done((bf16[32,2048]{1,0:T(8,128)(2,1)S(1)}, bf16[32,2048]{1,0:T(8,128)(2,1)S(1)}, u32[]{:S(2)}, u32[]{:S(2)}) %collective-permute-start.4) | collective-permute-done | bytes 131104 | tf_op jit(solution)/shard_map/ppermute | solution.py:50
  56.4 3.1 %collective-permute-start.6 = (bf16[96,2048]{1,0:T(8,128)(2,1)S(1)}, bf16[96,2048]{1,0:T(8,128)(2,1)S(1)}, u32[]{:S(2)}, u32[]{:S(2)}) collective-permute-start(bf16[96,2048]{1,0:T(8,128)(2,1)S(1)} %constant_dynamic-update-slice_fusion.refs_1_), channel_id=1, source_target_pairs={{1,0},{0,1},{9,8},{8,9},{17,16},{16,17},{25,24},{24,25},{33,32},{3... | collective-permute-start | bytes 1179656 | tf_op jit(solution)/shard_map/ppermute | solution.py:50
  59.5 0.0 all-to-all-done.1
  59.5 0.2 copy.15
  59.7 1.1 %collective-permute-done.6.refs_3_ = bf16[96,2048]{1,0:T(8,128)(2,1)S(1)} collective-permute-done((bf16[96,2048]{1,0:T(8,128)(2,1)S(1)}, bf16[96,2048]{1,0:T(8,128)(2,1)S(1)}, u32[]{:S(2)}, u32[]{:S(2)}) %collective-permute-start.6) | collective-permute-done | bytes 393248 | tf_op jit(solution)/shard_map/ppermute | solution.py:50
  60.8 0.0 collective-permute-done.5.refs_2_
  60.8 1.4 %score.1 = f32[16,32,128]{2,1,0:T(8,128)} custom-call(bf16[160,2048]{1,0:T(8,128)(2,1)S(1)} %pad_maximum_fusion.refs_0_, bf16[96,2048]{1,0:T(8,128)(2,1)S(1)} %constant_dynamic-update-slice_fusion.refs_1_, bf16[160,2048]{1,0:T(8,128)(2,1)S(1)} %collective-permute-done.5.refs_2_, bf16[96,2048]{1,0:T(8,128)(2,1)S(1)} %collective-permute-done.6.refs_3_, ...), custom_call_target="tpu_custom_call" | custom-call | tf_op jit(solution)/shard_map/score/pallas_call | solution.py:235
  62.2 4.5 %all-to-all-start.2 = ((f32[16,32,128]{2,1,0:T(8,128)}), f32[16,32,128]{2,1,0:T(8,128)S(1)}, u32[]{:S(2)}, u32[]{:S(2)}) async-start(f32[16,32,128]{2,1,0:T(8,128)} %score.1), calls=%async_computation.2 | async-start | bytes 524288 | tf_op jit(solution)/shard_map/all_to_all | solution.py:254
  66.7 0.0 copy-done.3
  66.7 0.1 copy.13.domains_ref
  66.8 7.0 %all-to-all-done.2.parts_ref = f32[16,32,128]{2,1,0:T(8,128)S(1)} async-done(((f32[16,32,128]{2,1,0:T(8,128)}), f32[16,32,128]{2,1,0:T(8,128)S(1)}, u32[]{:S(2)}, u32[]{:S(2)}) %all-to-all-start.2) | async-done | bytes 262176 | tf_op jit(solution)/shard_map/all_to_all | solution.py:254
  73.9 1.2 %finish.1 = (f32[32,256]{1,0:T(8,128)}, f32[8,32]{1,0:T(8,128)}) custom-call(f32[16,32,128]{2,1,0:T(8,128)S(1)} %all-to-all-done.2.parts_ref, s32[256,1]{1,0:T(8,128)S(1)} %copy.13.domains_ref), custom_call_target="tpu_custom_call" | custom-call | tf_op jit(solution)/shard_map/finish/pallas_call | solution.py:195
  (14 shorter events, 0.3 us)
Async XLA Ops:
  0.6 13.7 %copy-start.2 = (bf16[32,16384]{1,0:T(8,128)(2,1)S(1)}, bf16[32,16384]{1,0:T(8,128)(2,1)}, u32[]{:S(2)}) copy-start(bf16[32,16384]{1,0:T(8,128)(2,1)} %param.12) | copy-start | bytes 3145732
  4.1 19.2 %all-to-all-start = ((f32[8,64,128]{2,1,0:T(8,128)}), f32[8,64,128]{2,1,0:T(8,128)S(1)}, u32[]{:S(2)}, u32[]{:S(2)}) async-start(f32[8,64,128]{2,1,0:T(8,128)} %bitcast.7), calls=%async_computation | async-start | bytes 524288 | tf_op jit(solution)/shard_map/all_to_all | solution.py:288
  14.3 26.9 %collective-permute-start.1 = (bf16[32,4096]{1,0:T(8,128)(2,1)S(1)}, bf16[32,4096]{1,0:T(8,128)(2,1)S(1)}, u32[]{:S(2)}, u32[]{:S(2)}) collective-permute-start(bf16[32,4096]{1,0:T(8,128)(2,1)S(1)} %constant_dynamic-slice_fusion.6), channel_id=1, source_target_pairs={{256,0},{257,1},{264,8},{265,9},{272,16},{273,17},{280,24},{281,25... | collective-permute-start | bytes 786440 | tf_op jit(solution)/shard_map/ppermute | solution.py:50
  16.4 6.9 %copy-start = (s32[4,32]{1,0:T(4,128)S(1)}, s32[4,32]{1,0:T(4,128)}, u32[]{:S(2)}) copy-start(s32[4,32]{1,0:T(4,128)} %mask_ref.1) | copy-start | bytes 1540
  16.4 6.9 %copy-start.1 = (s32[4]{0:T(128)S(1)}, s32[4]{0:T(128)}, u32[]{:S(2)}) copy-start(s32[4]{0:T(128)} %lengths_ref.1) | copy-start | bytes 52
  16.4 20.6 %collective-permute-start = (bf16[32,8192]{1,0:T(8,128)(2,1)S(1)}, bf16[32,8192]{1,0:T(8,128)(2,1)S(1)}, u32[]{:S(2)}, u32[]{:S(2)}) collective-permute-start(bf16[32,8192]{1,0:T(8,128)(2,1)S(1)} %pad_maximum_fusion.2), channel_id=1, source_target_pairs={{8,0},{9,1},{0,8},{1,9},{24,16},{25,17},{16,24},{17,25},{40,32},{4... | collective-permute-start | bytes 1572872 | tf_op jit(solution)/shard_map/ppermute | solution.py:50
  25.6 33.9 %all-to-all-start.1 = ((bf16[64,32,128]{2,1,0:T(8,128)(2,1)}), bf16[64,32,128]{2,1,0:T(8,128)(2,1)S(1)}, u32[]{:S(2)}, u32[]{:S(2)}) async-start(bf16[64,32,128]{2,1,0:T(8,128)(2,1)} %bitcast.1), calls=%async_computation.1 | async-start | bytes 1048576 | tf_op jit(solution)/shard_map/all_to_all | solution.py:254
  37.1 13.7 %collective-permute-start.2 = (bf16[64,2048]{1,0:T(8,128)(2,1)S(1)}, bf16[64,2048]{1,0:T(8,128)(2,1)S(1)}, u32[]{:S(2)}, u32[]{:S(2)}) collective-permute-start(bf16[64,2048]{1,0:T(8,128)(2,1)S(1)} %pad_maximum_fusion.3), channel_id=1, source_target_pairs={{128,0},{129,1},{136,8},{137,9},{144,16},{145,17},{152,24},{153,25... | collective-permute-start | bytes 786440 | tf_op jit(solution)/shard_map/ppermute | solution.py:50
  41.2 14.1 %collective-permute-start.3 = (bf16[64,2048]{1,0:T(8,128)(2,1)S(1)}, bf16[64,2048]{1,0:T(8,128)(2,1)S(1)}, u32[]{:S(2)}, u32[]{:S(2)}) collective-permute-start(bf16[64,2048]{1,0:T(8,128)(2,1)S(1)} %pad_maximum_fusion.4), channel_id=1, source_target_pairs={{384,0},{385,1},{392,8},{393,9},{400,16},{401,17},{408,24},{409,25... | collective-permute-start | bytes 786440 | tf_op jit(solution)/shard_map/ppermute | solution.py:50
  45.9 10.5 %collective-permute-start.4 = (bf16[32,2048]{1,0:T(8,128)(2,1)S(1)}, bf16[32,2048]{1,0:T(8,128)(2,1)S(1)}, u32[]{:S(2)}, u32[]{:S(2)}) collective-permute-start(bf16[32,2048]{1,0:T(8,128)(2,1)S(1)} %get-tuple-element.22), channel_id=1, source_target_pairs={{8,0},{9,1},{0,8},{1,9},{24,16},{25,17},{16,24},{17,25},{40,32},{4... | collective-permute-start | bytes 393224 | tf_op jit(solution)/shard_map/ppermute | solution.py:50
  50.9 9.9 %collective-permute-start.5 = (bf16[160,2048]{1,0:T(8,128)(2,1)S(1)}, bf16[160,2048]{1,0:T(8,128)(2,1)S(1)}, u32[]{:S(2)}, u32[]{:S(2)}) collective-permute-start(bf16[160,2048]{1,0:T(8,128)(2,1)S(1)} %pad_maximum_fusion.refs_0_), channel_id=1, source_target_pairs={{1,0},{0,1},{9,8},{8,9},{17,16},{16,17},{25,24},{24,25},{33,32},{3... | collective-permute-start | bytes 1966088 | tf_op jit(solution)/shard_map/ppermute | solution.py:50
  56.4 4.4 %collective-permute-start.6 = (bf16[96,2048]{1,0:T(8,128)(2,1)S(1)}, bf16[96,2048]{1,0:T(8,128)(2,1)S(1)}, u32[]{:S(2)}, u32[]{:S(2)}) collective-permute-start(bf16[96,2048]{1,0:T(8,128)(2,1)S(1)} %constant_dynamic-update-slice_fusion.refs_1_), channel_id=1, source_target_pairs={{1,0},{0,1},{9,8},{8,9},{17,16},{16,17},{25,24},{24,25},{33,32},{3... | collective-permute-start | bytes 1179656 | tf_op jit(solution)/shard_map/ppermute | solution.py:50
  60.8 5.9 %copy-start.3 = (s32[256,1]{0,1:T(1,128)S(1)}, s32[256,1]{0,1:T(1,128)}, u32[]{:S(2)}) copy-start(s32[256,1]{0,1:T(1,128)} %param.15) | copy-start | bytes 3076
  62.2 11.6 %all-to-all-start.2 = ((f32[16,32,128]{2,1,0:T(8,128)}), f32[16,32,128]{2,1,0:T(8,128)S(1)}, u32[]{:S(2)}, u32[]{:S(2)}) async-start(f32[16,32,128]{2,1,0:T(8,128)} %score.1), calls=%async_computation.2 | async-start | bytes 524288 | tf_op jit(solution)/shard_map/all_to_all | solution.py:254

commit v6 on v5

--- a/solution.py
+++ b/solution.py
@@ -169,9 +169,9 @@
 
 def finish_kernel(parts_ref, domains_ref, scores_ref, influence_ref):
     def half(core):
-        total = parts_ref[core]
+        total = parts_ref[core].astype(jnp.float32)
         for part in range(core + NC, parts_ref.shape[0], NC):
-            total = total + parts_ref[part]
+            total = total + parts_ref[part].astype(jnp.float32)
         return total
 
     total = jnp.concatenate([half(core) for core in range(NC)], axis=1)
@@ -222,7 +222,7 @@
     for other_core in range(NC):
         for step, other_z in ORDER:
             member = ((x ^ step) * 2 + (z_low ^ other_z)) * NC + (core ^ other_core)
-            out_ref[pl.ds(member, 1)] = result[at : at + rows][None]
+            out_ref[pl.ds(member, 1)] = result[at : at + rows].astype(out_ref.dtype)[None]
             at += rows
 
 
@@ -234,7 +234,7 @@
     queries = 2 * blocks.shape[1]
     return pl.pallas_call(
         score_kernel,
-        out_shape=jax.ShapeDtypeStruct((members, count // members, queries), jnp.float32),
+        out_shape=jax.ShapeDtypeStruct((members, count // members, queries), jnp.bfloat16),
         in_specs=[vmem] * (len(rows) + 1),
         out_specs=vmem,
         scratch_shapes=[

time: 75.7 us -> 74.6 us (0.985)
  waiting for transfers between devices: 15.4 us -> 14.4 us
    all_to_all x2, waiting for transfers between devices: 7.03 us -> 6 us  [exchange(): lax.all_to_all(blocks, AXES, 0, 0, axis_index_groups=partition(members))]
where the time goes in v6:
time: 74.6 us; the launch traced here: 74 us
  starting transfers between devices  49.7 us (67%)
  waiting for transfers between devices  14.4 us (19%)
  Pallas kernels  8.31 us (11%)
  between operations  0.9 us (1%)
    ppermute x7, starting transfers between devices, swapped(): lax.ppermute(block, AXES, [(flat(*change(*p)), flat(*p)) for p in places()])  23.6 us
    all_to_all x2, starting transfers between devices, exchange(): lax.all_to_all(blocks, AXES, 0, 0, axis_index_groups=partition(members))  15.9 us
    all_to_all x1, starting transfers between devices, body(): parts = lax.all_to_all(parts, 'tensor', 0, 0)  10.2 us
    all_to_all x2, waiting for transfers between devices, exchange(): lax.all_to_all(blocks, AXES, 0, 0, axis_index_groups=partition(members))  6 us
    ppermute x7, waiting for transfers between devices, swapped(): lax.ppermute(block, AXES, [(flat(*change(*p)), flat(*p)) for p in places()])  4.49 us
    all_to_all x1, waiting for transfers between devices, body(): parts = lax.all_to_all(parts, 'tensor', 0, 0)  3.87 us
    pallas_call x1, Pallas kernels, project(): pl.pallas_call(project_kernel, out_shape=jax.ShapeDtypeStruct((LAYERS, qu...  3.45 us
    pallas_call x1, Pallas kernels, outer(): pl.pallas_call(outer_kernel, out_shape=jax.ShapeDtypeStruct((members // 2...  2.24 us
  transfers between devices with their start and end apart: 10, of which 6 were waited for; matrix products, arithmetic and copies ran while one was open for 1% of the time, Pallas kernels for 3%

profile of v6, /device:TPU:1, one launch (start us, length us, event | category | flops | bytes accessed | tf_op | source)
XLA Modules:
  0.0 74.0 jit_solution(13399961640553436291)
XLA Ops:
  0.6 0.0 copy-start.2
  0.6 3.5 %project.1 = f32[4,128,128]{2,1,0:T(8,128)} custom-call(bf16[4,4,32,1024]{3,2,1,0:T(8,128)(2,1)} %in_ref.1, bf16[4,4,32,1024]{3,2,1,0:T(8,128)(2,1)} %grad_ref.1, bf16[4,64,1024]{2,1,0:T(8,128)(2,1)} %in_proj_ref.1, bf16[4,64,1024]{2,1,0:T(8,128)(2,1)} %out_proj_ref.1), custom_call_target="tpu_custom_call" | custom-call | tf_op jit(solution)/shard_map/project/pallas_call | solution.py:100
  4.1 10.2 %all-to-all-start = ((f32[8,64,128]{2,1,0:T(8,128)}), f32[8,64,128]{2,1,0:T(8,128)S(1)}, u32[]{:S(2)}, u32[]{:S(2)}) async-start(f32[8,64,128]{2,1,0:T(8,128)} %bitcast.7), calls=%async_computation | async-start | bytes 524288 | tf_op jit(solution)/shard_map/all_to_all | solution.py:288
  14.3 0.0 copy-done.2
  14.3 1.9 %collective-permute-start.1 = (bf16[32,4096]{1,0:T(8,128)(2,1)S(1)}, bf16[32,4096]{1,0:T(8,128)(2,1)S(1)}, u32[]{:S(2)}, u32[]{:S(2)}) collective-permute-start(bf16[32,4096]{1,0:T(8,128)(2,1)S(1)} %constant_dynamic-slice_fusion.6), channel_id=1, source_target_pairs={{256,0},{257,1},{264,8},{265,9},{272,16},{273,17},{280,24},{281,25... | collective-permute-start | bytes 786440 | tf_op jit(solution)/shard_map/ppermute | solution.py:50
  16.3 0.1 constant_dynamic-slice_fusion.16
  16.4 0.0 copy-start
  16.4 0.0 copy-start.1
  16.4 2.9 %collective-permute-start = (bf16[32,8192]{1,0:T(8,128)(2,1)S(1)}, bf16[32,8192]{1,0:T(8,128)(2,1)S(1)}, u32[]{:S(2)}, u32[]{:S(2)}) collective-permute-start(bf16[32,8192]{1,0:T(8,128)(2,1)S(1)} %pad_maximum_fusion.2), channel_id=1, source_target_pairs={{8,0},{9,1},{0,8},{1,9},{24,16},{25,17},{16,24},{17,25},{40,32},{4... | collective-permute-start | bytes 1572872 | tf_op jit(solution)/shard_map/ppermute | solution.py:50
  19.5 3.9 %all-to-all-done.parts_ref = f32[8,64,128]{2,1,0:T(8,128)S(1)} async-done(((f32[8,64,128]{2,1,0:T(8,128)}), f32[8,64,128]{2,1,0:T(8,128)S(1)}, u32[]{:S(2)}, u32[]{:S(2)}) %all-to-all-start) | async-done | bytes 262176 | tf_op jit(solution)/shard_map/all_to_all | solution.py:288
  23.3 0.0 copy-done
  23.3 2.2 %outer.1 = bf16[32,2,32,128]{3,2,1,0:T(8,128)(2,1)} custom-call(s32[4]{0:T(128)S(1)} %copy-done.1, s32[4,32]{1,0:T(4,128)S(1)} %copy-done, f32[8,64,128]{2,1,0:T(8,128)S(1)} %all-to-all-done.parts_ref), custom_call_target="tpu_custom_call" | custom-call | bytes 62914560 | tf_op jit(solution)/shard_map/outer/pallas_call | solution.py:153
  25.6 11.4 %all-to-all-start.1 = ((bf16[64,32,128]{2,1,0:T(8,128)(2,1)}), bf16[64,32,128]{2,1,0:T(8,128)(2,1)S(1)}, u32[]{:S(2)}, u32[]{:S(2)}) async-start(bf16[64,32,128]{2,1,0:T(8,128)(2,1)} %bitcast.1), calls=%async_computation.1 | async-start | bytes 1048576 | tf_op jit(solution)/shard_map/all_to_all | solution.py:254
  37.0 0.0 collective-permute-done
  37.1 4.1 %collective-permute-start.2 = (bf16[64,2048]{1,0:T(8,128)(2,1)S(1)}, bf16[64,2048]{1,0:T(8,128)(2,1)S(1)}, u32[]{:S(2)}, u32[]{:S(2)}) collective-permute-start(bf16[64,2048]{1,0:T(8,128)(2,1)S(1)} %pad_maximum_fusion.3), channel_id=1, source_target_pairs={{128,0},{129,1},{136,8},{137,9},{144,16},{145,17},{152,24},{153,25... | collective-permute-start | bytes 786440 | tf_op jit(solution)/shard_map/ppermute | solution.py:50
  41.2 0.0 collective-permute-done.1
  41.2 4.6 %collective-permute-start.3 = (bf16[64,2048]{1,0:T(8,128)(2,1)S(1)}, bf16[64,2048]{1,0:T(8,128)(2,1)S(1)}, u32[]{:S(2)}, u32[]{:S(2)}) collective-permute-start(bf16[64,2048]{1,0:T(8,128)(2,1)S(1)} %pad_maximum_fusion.4), channel_id=1, source_target_pairs={{384,0},{385,1},{392,8},{393,9},{400,16},{401,17},{408,24},{409,25... | collective-permute-start | bytes 786440 | tf_op jit(solution)/shard_map/ppermute | solution.py:50
  45.9 3.1 %collective-permute-start.4 = (bf16[32,2048]{1,0:T(8,128)(2,1)S(1)}, bf16[32,2048]{1,0:T(8,128)(2,1)S(1)}, u32[]{:S(2)}, u32[]{:S(2)}) collective-permute-start(bf16[32,2048]{1,0:T(8,128)(2,1)S(1)} %get-tuple-element.22), channel_id=1, source_target_pairs={{8,0},{9,1},{0,8},{1,9},{24,16},{25,17},{16,24},{17,25},{40,32},{4... | collective-permute-start | bytes 393224 | tf_op jit(solution)/shard_map/ppermute | solution.py:50
  49.0 1.8 %collective-permute-done.2 = bf16[64,2048]{1,0:T(8,128)(2,1)S(1)} collective-permute-done((bf16[64,2048]{1,0:T(8,128)(2,1)S(1)}, bf16[64,2048]{1,0:T(8,128)(2,1)S(1)}, u32[]{:S(2)}, u32[]{:S(2)}) %collective-permute-start.2) | collective-permute-done | bytes 262176 | tf_op jit(solution)/shard_map/ppermute | solution.py:50
  50.9 3.9 %collective-permute-start.5 = (bf16[160,2048]{1,0:T(8,128)(2,1)S(1)}, bf16[160,2048]{1,0:T(8,128)(2,1)S(1)}, u32[]{:S(2)}, u32[]{:S(2)}) collective-permute-start(bf16[160,2048]{1,0:T(8,128)(2,1)S(1)} %pad_maximum_fusion.refs_0_), channel_id=1, source_target_pairs={{1,0},{0,1},{9,8},{8,9},{17,16},{16,17},{25,24},{24,25},{33,32},{3... | collective-permute-start | bytes 1966088 | tf_op jit(solution)/shard_map/ppermute | solution.py:50
  54.8 0.6 collective-permute-done.3
  55.4 1.0 %collective-permute-done.4 = bf16[32,2048]{1,0:T(8,128)(2,1)S(1)} collective-permute-done((bf16[32,2048]{1,0:T(8,128)(2,1)S(1)}, bf16[32,2048]{1,0:T(8,128)(2,1)S(1)}, u32[]{:S(2)}, u32[]{:S(2)}) %collective-permute-start.4) | collective-permute-done | bytes 131104 | tf_op jit(solution)/shard_map/ppermute | solution.py:50
  56.4 3.1 %collective-permute-start.6 = (bf16[96,2048]{1,0:T(8,128)(2,1)S(1)}, bf16[96,2048]{1,0:T(8,128)(2,1)S(1)}, u32[]{:S(2)}, u32[]{:S(2)}) collective-permute-start(bf16[96,2048]{1,0:T(8,128)(2,1)S(1)} %constant_dynamic-update-slice_fusion.refs_1_), channel_id=1, source_target_pairs={{1,0},{0,1},{9,8},{8,9},{17,16},{16,17},{25,24},{24,25},{33,32},{3... | collective-permute-start | bytes 1179656 | tf_op jit(solution)/shard_map/ppermute | solution.py:50
  59.5 0.0 all-to-all-done.1
  59.5 0.2 copy.15
  59.7 1.1 %collective-permute-done.6.refs_3_ = bf16[96,2048]{1,0:T(8,128)(2,1)S(1)} collective-permute-done((bf16[96,2048]{1,0:T(8,128)(2,1)S(1)}, bf16[96,2048]{1,0:T(8,128)(2,1)S(1)}, u32[]{:S(2)}, u32[]{:S(2)}) %collective-permute-start.6) | collective-permute-done | bytes 393248 | tf_op jit(solution)/shard_map/ppermute | solution.py:50
  60.8 0.0 collective-permute-done.5.refs_2_
  60.8 1.4 %score.1 = bf16[16,32,128]{2,1,0:T(8,128)(2,1)} custom-call(bf16[160,2048]{1,0:T(8,128)(2,1)S(1)} %pad_maximum_fusion.refs_0_, bf16[96,2048]{1,0:T(8,128)(2,1)S(1)} %constant_dynamic-update-slice_fusion.refs_1_, bf16[160,2048]{1,0:T(8,128)(2,1)S(1)} %collective-permute-done.5.refs_2_, bf16[96,2048]{1,0:T(8,128)(2,1)S(1)} %collective-permute-done.6.refs_3_, ...), custom_call_target="tpu_custom_call" | custom-call | tf_op jit(solution)/shard_map/score/pallas_call | solution.py:235
  62.2 4.5 %all-to-all-start.2 = ((bf16[16,32,128]{2,1,0:T(8,128)(2,1)}), bf16[16,32,128]{2,1,0:T(8,128)(2,1)S(1)}, u32[]{:S(2)}, u32[]{:S(2)}) async-start(bf16[16,32,128]{2,1,0:T(8,128)(2,1)} %score.1), calls=%async_computation.2 | async-start | bytes 262144 | tf_op jit(solution)/shard_map/all_to_all | solution.py:254
  66.6 0.1 copy.13.domains_ref
  66.8 6.0 %all-to-all-done.2.parts_ref = bf16[16,32,128]{2,1,0:T(8,128)(2,1)S(1)} async-done(((bf16[16,32,128]{2,1,0:T(8,128)(2,1)}), bf16[16,32,128]{2,1,0:T(8,128)(2,1)S(1)}, u32[]{:S(2)}, u32[]{:S(2)}) %all-to-all-start.2) | async-done | bytes 131104 | tf_op jit(solution)/shard_map/all_to_all | solution.py:254
  72.8 1.2 %finish.1 = (f32[32,256]{1,0:T(8,128)}, f32[8,32]{1,0:T(8,128)}) custom-call(bf16[16,32,128]{2,1,0:T(8,128)(2,1)S(1)} %all-to-all-done.2.parts_ref, s32[256,1]{1,0:T(8,128)S(1)} %copy.13.domains_ref), custom_call_target="tpu_custom_call" | custom-call | tf_op jit(solution)/shard_map/finish/pallas_call | solution.py:195
  (14 shorter events, 0.3 us)
Async XLA Ops:
  0.6 13.7 %copy-start.2 = (bf16[32,16384]{1,0:T(8,128)(2,1)S(1)}, bf16[32,16384]{1,0:T(8,128)(2,1)}, u32[]{:S(2)}) copy-start(bf16[32,16384]{1,0:T(8,128)(2,1)} %param.12) | copy-start | bytes 3145732
  4.1 19.2 %all-to-all-start = ((f32[8,64,128]{2,1,0:T(8,128)}), f32[8,64,128]{2,1,0:T(8,128)S(1)}, u32[]{:S(2)}, u32[]{:S(2)}) async-start(f32[8,64,128]{2,1,0:T(8,128)} %bitcast.7), calls=%async_computation | async-start | bytes 524288 | tf_op jit(solution)/shard_map/all_to_all | solution.py:288
  14.3 26.9 %collective-permute-start.1 = (bf16[32,4096]{1,0:T(8,128)(2,1)S(1)}, bf16[32,4096]{1,0:T(8,128)(2,1)S(1)}, u32[]{:S(2)}, u32[]{:S(2)}) collective-permute-start(bf16[32,4096]{1,0:T(8,128)(2,1)S(1)} %constant_dynamic-slice_fusion.6), channel_id=1, source_target_pairs={{256,0},{257,1},{264,8},{265,9},{272,16},{273,17},{280,24},{281,25... | collective-permute-start | bytes 786440 | tf_op jit(solution)/shard_map/ppermute | solution.py:50
  16.4 6.9 %copy-start = (s32[4,32]{1,0:T(4,128)S(1)}, s32[4,32]{1,0:T(4,128)}, u32[]{:S(2)}) copy-start(s32[4,32]{1,0:T(4,128)} %mask_ref.1) | copy-start | bytes 1540
  16.4 6.9 %copy-start.1 = (s32[4]{0:T(128)S(1)}, s32[4]{0:T(128)}, u32[]{:S(2)}) copy-start(s32[4]{0:T(128)} %lengths_ref.1) | copy-start | bytes 52
  16.4 20.6 %collective-permute-start = (bf16[32,8192]{1,0:T(8,128)(2,1)S(1)}, bf16[32,8192]{1,0:T(8,128)(2,1)S(1)}, u32[]{:S(2)}, u32[]{:S(2)}) collective-permute-start(bf16[32,8192]{1,0:T(8,128)(2,1)S(1)} %pad_maximum_fusion.2), channel_id=1, source_target_pairs={{8,0},{9,1},{0,8},{1,9},{24,16},{25,17},{16,24},{17,25},{40,32},{4... | collective-permute-start | bytes 1572872 | tf_op jit(solution)/shard_map/ppermute | solution.py:50
  25.6 33.9 %all-to-all-start.1 = ((bf16[64,32,128]{2,1,0:T(8,128)(2,1)}), bf16[64,32,128]{2,1,0:T(8,128)(2,1)S(1)}, u32[]{:S(2)}, u32[]{:S(2)}) async-start(bf16[64,32,128]{2,1,0:T(8,128)(2,1)} %bitcast.1), calls=%async_computation.1 | async-start | bytes 1048576 | tf_op jit(solution)/shard_map/all_to_all | solution.py:254
  37.1 13.7 %collective-permute-start.2 = (bf16[64,2048]{1,0:T(8,128)(2,1)S(1)}, bf16[64,2048]{1,0:T(8,128)(2,1)S(1)}, u32[]{:S(2)}, u32[]{:S(2)}) collective-permute-start(bf16[64,2048]{1,0:T(8,128)(2,1)S(1)} %pad_maximum_fusion.3), channel_id=1, source_target_pairs={{128,0},{129,1},{136,8},{137,9},{144,16},{145,17},{152,24},{153,25... | collective-permute-start | bytes 786440 | tf_op jit(solution)/shard_map/ppermute | solution.py:50
  41.2 14.1 %collective-permute-start.3 = (bf16[64,2048]{1,0:T(8,128)(2,1)S(1)}, bf16[64,2048]{1,0:T(8,128)(2,1)S(1)}, u32[]{:S(2)}, u32[]{:S(2)}) collective-permute-start(bf16[64,2048]{1,0:T(8,128)(2,1)S(1)} %pad_maximum_fusion.4), channel_id=1, source_target_pairs={{384,0},{385,1},{392,8},{393,9},{400,16},{401,17},{408,24},{409,25... | collective-permute-start | bytes 786440 | tf_op jit(solution)/shard_map/ppermute | solution.py:50
  45.9 10.5 %collective-permute-start.4 = (bf16[32,2048]{1,0:T(8,128)(2,1)S(1)}, bf16[32,2048]{1,0:T(8,128)(2,1)S(1)}, u32[]{:S(2)}, u32[]{:S(2)}) collective-permute-start(bf16[32,2048]{1,0:T(8,128)(2,1)S(1)} %get-tuple-element.22), channel_id=1, source_target_pairs={{8,0},{9,1},{0,8},{1,9},{24,16},{25,17},{16,24},{17,25},{40,32},{4... | collective-permute-start | bytes 393224 | tf_op jit(solution)/shard_map/ppermute | solution.py:50
  50.9 9.9 %collective-permute-start.5 = (bf16[160,2048]{1,0:T(8,128)(2,1)S(1)}, bf16[160,2048]{1,0:T(8,128)(2,1)S(1)}, u32[]{:S(2)}, u32[]{:S(2)}) collective-permute-start(bf16[160,2048]{1,0:T(8,128)(2,1)S(1)} %pad_maximum_fusion.refs_0_), channel_id=1, source_target_pairs={{1,0},{0,1},{9,8},{8,9},{17,16},{16,17},{25,24},{24,25},{33,32},{3... | collective-permute-start | bytes 1966088 | tf_op jit(solution)/shard_map/ppermute | solution.py:50
  56.4 4.4 %collective-permute-start.6 = (bf16[96,2048]{1,0:T(8,128)(2,1)S(1)}, bf16[96,2048]{1,0:T(8,128)(2,1)S(1)}, u32[]{:S(2)}, u32[]{:S(2)}) collective-permute-start(bf16[96,2048]{1,0:T(8,128)(2,1)S(1)} %constant_dynamic-update-slice_fusion.refs_1_), channel_id=1, source_target_pairs={{1,0},{0,1},{9,8},{8,9},{17,16},{16,17},{25,24},{24,25},{33,32},{3... | collective-permute-start | bytes 1179656 | tf_op jit(solution)/shard_map/ppermute | solution.py:50
  60.8 5.9 %copy-start.3 = (s32[256,1]{0,1:T(1,128)S(1)}, s32[256,1]{0,1:T(1,128)}, u32[]{:S(2)}) copy-start(s32[256,1]{0,1:T(1,128)} %param.15) | copy-start | bytes 3076
  62.2 10.6 %all-to-all-start.2 = ((bf16[16,32,128]{2,1,0:T(8,128)(2,1)}), bf16[16,32,128]{2,1,0:T(8,128)(2,1)S(1)}, u32[]{:S(2)}, u32[]{:S(2)}) async-start(bf16[16,32,128]{2,1,0:T(8,128)(2,1)} %score.1), calls=%async_computation.2 | async-start | bytes 262144 | tf_op jit(solution)/shard_map/all_to_all | solution.py:254

commit v7 on v6

--- a/solution.py
+++ b/solution.py
@@ -182,11 +182,16 @@
     place = (target == there).astype(jnp.float32)
     scores = jnp.dot(total, place, precision=lax.Precision.HIGHEST, preferred_element_type=jnp.float32)
     scores_ref[...] = scores
-    lane = lax.broadcasted_iota(jnp.int32, (queries, DOMAINS), 1)
-    onehot = (domains_ref[...] == lane).astype(jnp.float32)
-    counts = jnp.sum(onehot, axis=0, keepdims=True)
-    sums = jnp.dot(scores, onehot, precision=lax.Precision.HIGHEST, preferred_element_type=jnp.float32)
-    influence_ref[...] = (sums / counts).T
+    onehot = (domains_ref[...] == lax.broadcasted_iota(jnp.int32, (DOMAINS, queries), 0)).astype(jnp.float32)
+    counts = jnp.sum(onehot, axis=1, keepdims=True)
+    sums = lax.dot_general(
+        onehot,
+        scores,
+        (((1,), (1,)), ((), ())),
+        precision=lax.Precision.HIGHEST,
+        preferred_element_type=jnp.float32,
+    )
+    influence_ref[...] = sums / counts
 
 
 def finish(parts, domains):
@@ -200,7 +205,7 @@
         ),
         compiler_params=pltpu.CompilerParams(vmem_limit_bytes=16 * 1024 * 1024),
         name="finish",
-    )(parts, domains)
+    )(parts, domains.reshape(1, queries))
 
 
 def score_kernel(*refs):

time: 74.6 us -> 73.5 us (0.985)
  blocking collectives: 0 us -> 10.4 us
  waiting for transfers between devices: 14.4 us -> 8.35 us
  starting transfers between devices: 49.7 us -> 45.2 us
  Pallas kernels: 8.31 us -> 7.51 us
    all_to_all x0 -> x1, blocking collectives: none -> 10.4 us  [exchange(): lax.all_to_all(blocks, AXES, 0, 0, axis_index_groups=partition(members))]
    all_to_all x2 -> x1, waiting for transfers between devices: 6 us -> 0.01 us  [exchange(): lax.all_to_all(blocks, AXES, 0, 0, axis_index_groups=partition(members))]
    all_to_all x2 -> x1, starting transfers between devices: 15.9 us -> 11.4 us  [exchange(): lax.all_to_all(blocks, AXES, 0, 0, axis_index_groups=partition(members))]
  transfers between devices with their start and end apart: 10 -> 9, of which waited for: 6 -> 5; matrix products, arithmetic and copies ran while one was open for 1% -> 1% of each run, Pallas kernels for 3% -> 3%
where the time goes in v7:
time: 73.5 us; the launch traced here: 73 us
  starting transfers between devices  45.2 us (61%)
  blocking collectives  10.4 us (14%)
  waiting for transfers between devices  8.35 us (11%)
  Pallas kernels  7.51 us (10%)
  between operations  0.89 us (1%)
    ppermute x7, starting transfers between devices, swapped(): lax.ppermute(block, AXES, [(flat(*change(*p)), flat(*p)) for p in places()])  23.6 us
    all_to_all x1, starting transfers between devices, exchange(): lax.all_to_all(blocks, AXES, 0, 0, axis_index_groups=partition(members))  11.4 us
    all_to_all x1, blocking collectives, exchange(): lax.all_to_all(blocks, AXES, 0, 0, axis_index_groups=partition(members))  10.4 us
    all_to_all x1, starting transfers between devices, body(): parts = lax.all_to_all(parts, 'tensor', 0, 0)  10.2 us
    ppermute x7, waiting for transfers between devices, swapped(): lax.ppermute(block, AXES, [(flat(*change(*p)), flat(*p)) for p in places()])  4.49 us
    all_to_all x1, waiting for transfers between devices, body(): parts = lax.all_to_all(parts, 'tensor', 0, 0)  3.87 us
    pallas_call x1, Pallas kernels, project(): pl.pallas_call(project_kernel, out_shape=jax.ShapeDtypeStruct((LAYERS, qu...  3.44 us
    pallas_call x1, Pallas kernels, outer(): pl.pallas_call(outer_kernel, out_shape=jax.ShapeDtypeStruct((members // 2...  2.24 us
  transfers between devices with their start and end apart: 9, of which 5 were waited for; matrix products, arithmetic and copies ran while one was open for 1% of the time, Pallas kernels for 3%

profile of v7, /device:TPU:1, one launch (start us, length us, event | category | flops | bytes accessed | tf_op | source)
XLA Modules:
  0.0 73.0 jit_solution(5494212736301948428)
XLA Ops:
  0.6 0.0 copy-start.3
  0.6 3.4 %project.1 = f32[4,128,128]{2,1,0:T(8,128)} custom-call(bf16[4,4,32,1024]{3,2,1,0:T(8,128)(2,1)} %in_ref.1, bf16[4,4,32,1024]{3,2,1,0:T(8,128)(2,1)} %grad_ref.1, bf16[4,64,1024]{2,1,0:T(8,128)(2,1)} %in_proj_ref.1, bf16[4,64,1024]{2,1,0:T(8,128)(2,1)} %out_proj_ref.1), custom_call_target="tpu_custom_call" | custom-call | tf_op jit(solution)/shard_map/project/pallas_call | solution.py:100
  4.1 10.2 %all-to-all-start = ((f32[8,64,128]{2,1,0:T(8,128)}), f32[8,64,128]{2,1,0:T(8,128)S(1)}, u32[]{:S(2)}, u32[]{:S(2)}) async-start(f32[8,64,128]{2,1,0:T(8,128)} %bitcast.9), calls=%async_computation | async-start | bytes 524288 | tf_op jit(solution)/shard_map/all_to_all | solution.py:293
  14.3 0.0 copy-done.3
  14.3 1.9 %collective-permute-start.1 = (bf16[32,4096]{1,0:T(8,128)(2,1)S(1)}, bf16[32,4096]{1,0:T(8,128)(2,1)S(1)}, u32[]{:S(2)}, u32[]{:S(2)}) collective-permute-start(bf16[32,4096]{1,0:T(8,128)(2,1)S(1)} %constant_dynamic-slice_fusion.6), channel_id=1, source_target_pairs={{256,0},{257,1},{264,8},{265,9},{272,16},{273,17},{280,24},{281,25... | collective-permute-start | bytes 786440 | tf_op jit(solution)/shard_map/ppermute | solution.py:50
  16.3 0.1 constant_dynamic-slice_fusion.16
  16.4 0.0 copy-start
  16.4 0.0 copy-start.2
  16.4 2.9 %collective-permute-start = (bf16[32,8192]{1,0:T(8,128)(2,1)S(1)}, bf16[32,8192]{1,0:T(8,128)(2,1)S(1)}, u32[]{:S(2)}, u32[]{:S(2)}) collective-permute-start(bf16[32,8192]{1,0:T(8,128)(2,1)S(1)} %pad_maximum_fusion.2), channel_id=1, source_target_pairs={{8,0},{9,1},{0,8},{1,9},{24,16},{25,17},{16,24},{17,25},{40,32},{4... | collective-permute-start | bytes 1572872 | tf_op jit(solution)/shard_map/ppermute | solution.py:50
  19.5 3.9 %all-to-all-done.parts_ref = f32[8,64,128]{2,1,0:T(8,128)S(1)} async-done(((f32[8,64,128]{2,1,0:T(8,128)}), f32[8,64,128]{2,1,0:T(8,128)S(1)}, u32[]{:S(2)}, u32[]{:S(2)}) %all-to-all-start) | async-done | bytes 262176 | tf_op jit(solution)/shard_map/all_to_all | solution.py:293
  23.3 0.0 copy-done
  23.3 0.0 copy-done.2
  23.3 2.2 %outer.1 = bf16[32,2,32,128]{3,2,1,0:T(8,128)(2,1)} custom-call(s32[4]{0:T(128)S(1)} %copy-done.2, s32[4,32]{1,0:T(4,128)S(1)} %copy-done, f32[8,64,128]{2,1,0:T(8,128)S(1)} %all-to-all-done.parts_ref), custom_call_target="tpu_custom_call" | custom-call | bytes 62914560 | tf_op jit(solution)/shard_map/outer/pallas_call | solution.py:153
  25.6 11.4 %all-to-all-start.1 = ((bf16[64,32,128]{2,1,0:T(8,128)(2,1)}), bf16[64,32,128]{2,1,0:T(8,128)(2,1)S(1)}, u32[]{:S(2)}, u32[]{:S(2)}) async-start(bf16[64,32,128]{2,1,0:T(8,128)(2,1)} %bitcast.1), calls=%async_computation.1 | async-start | bytes 1048576 | tf_op jit(solution)/shard_map/all_to_all | solution.py:259
  37.0 0.0 collective-permute-done
  37.1 4.1 %collective-permute-start.2 = (bf16[64,2048]{1,0:T(8,128)(2,1)S(1)}, bf16[64,2048]{1,0:T(8,128)(2,1)S(1)}, u32[]{:S(2)}, u32[]{:S(2)}) collective-permute-start(bf16[64,2048]{1,0:T(8,128)(2,1)S(1)} %pad_maximum_fusion.3), channel_id=1, source_target_pairs={{128,0},{129,1},{136,8},{137,9},{144,16},{145,17},{152,24},{153,25... | collective-permute-start | bytes 786440 | tf_op jit(solution)/shard_map/ppermute | solution.py:50
  41.2 0.0 collective-permute-done.1
  41.2 4.6 %collective-permute-start.3 = (bf16[64,2048]{1,0:T(8,128)(2,1)S(1)}, bf16[64,2048]{1,0:T(8,128)(2,1)S(1)}, u32[]{:S(2)}, u32[]{:S(2)}) collective-permute-start(bf16[64,2048]{1,0:T(8,128)(2,1)S(1)} %pad_maximum_fusion.4), channel_id=1, source_target_pairs={{384,0},{385,1},{392,8},{393,9},{400,16},{401,17},{408,24},{409,25... | collective-permute-start | bytes 786440 | tf_op jit(solution)/shard_map/ppermute | solution.py:50
  45.9 3.1 %collective-permute-start.4 = (bf16[32,2048]{1,0:T(8,128)(2,1)S(1)}, bf16[32,2048]{1,0:T(8,128)(2,1)S(1)}, u32[]{:S(2)}, u32[]{:S(2)}) collective-permute-start(bf16[32,2048]{1,0:T(8,128)(2,1)S(1)} %get-tuple-element.22), channel_id=1, source_target_pairs={{8,0},{9,1},{0,8},{1,9},{24,16},{25,17},{16,24},{17,25},{40,32},{4... | collective-permute-start | bytes 393224 | tf_op jit(solution)/shard_map/ppermute | solution.py:50
  49.0 1.8 %collective-permute-done.2 = bf16[64,2048]{1,0:T(8,128)(2,1)S(1)} collective-permute-done((bf16[64,2048]{1,0:T(8,128)(2,1)S(1)}, bf16[64,2048]{1,0:T(8,128)(2,1)S(1)}, u32[]{:S(2)}, u32[]{:S(2)}) %collective-permute-start.2) | collective-permute-done | bytes 262176 | tf_op jit(solution)/shard_map/ppermute | solution.py:50
  50.9 3.9 %collective-permute-start.5 = (bf16[160,2048]{1,0:T(8,128)(2,1)S(1)}, bf16[160,2048]{1,0:T(8,128)(2,1)S(1)}, u32[]{:S(2)}, u32[]{:S(2)}) collective-permute-start(bf16[160,2048]{1,0:T(8,128)(2,1)S(1)} %pad_maximum_fusion.refs_0_), channel_id=1, source_target_pairs={{1,0},{0,1},{9,8},{8,9},{17,16},{16,17},{25,24},{24,25},{33,32},{3... | collective-permute-start | bytes 1966088 | tf_op jit(solution)/shard_map/ppermute | solution.py:50
  54.8 0.6 collective-permute-done.3
  55.4 1.0 %collective-permute-done.4 = bf16[32,2048]{1,0:T(8,128)(2,1)S(1)} collective-permute-done((bf16[32,2048]{1,0:T(8,128)(2,1)S(1)}, bf16[32,2048]{1,0:T(8,128)(2,1)S(1)}, u32[]{:S(2)}, u32[]{:S(2)}) %collective-permute-start.4) | collective-permute-done | bytes 131104 | tf_op jit(solution)/shard_map/ppermute | solution.py:50
  56.4 3.1 %collective-permute-start.6 = (bf16[96,2048]{1,0:T(8,128)(2,1)S(1)}, bf16[96,2048]{1,0:T(8,128)(2,1)S(1)}, u32[]{:S(2)}, u32[]{:S(2)}) collective-permute-start(bf16[96,2048]{1,0:T(8,128)(2,1)S(1)} %constant_dynamic-update-slice_fusion.refs_1_), channel_id=1, source_target_pairs={{1,0},{0,1},{9,8},{8,9},{17,16},{16,17},{25,24},{24,25},{33,32},{3... | collective-permute-start | bytes 1179656 | tf_op jit(solution)/shard_map/ppermute | solution.py:50
  59.5 0.0 all-to-all-done.1
  59.5 0.2 copy.13
  59.7 1.1 %collective-permute-done.6.refs_3_ = bf16[96,2048]{1,0:T(8,128)(2,1)S(1)} collective-permute-done((bf16[96,2048]{1,0:T(8,128)(2,1)S(1)}, bf16[96,2048]{1,0:T(8,128)(2,1)S(1)}, u32[]{:S(2)}, u32[]{:S(2)}) %collective-permute-start.6) | collective-permute-done | bytes 393248 | tf_op jit(solution)/shard_map/ppermute | solution.py:50
  60.8 0.0 collective-permute-done.5.refs_2_
  60.8 0.7 %score.1 = bf16[16,32,128]{2,1,0:T(8,128)(2,1)S(1)} custom-call(bf16[160,2048]{1,0:T(8,128)(2,1)S(1)} %pad_maximum_fusion.refs_0_, bf16[96,2048]{1,0:T(8,128)(2,1)S(1)} %constant_dynamic-update-slice_fusion.refs_1_, bf16[160,2048]{1,0:T(8,128)(2,1)S(1)} %collective-permute-done.5.refs_2_, bf16[96,2048]{1,0:T(8,128)(2,1)S(1)} %collective-permute-done.6.refs_3_, ...), custom_call_target="tpu_custom_call" | custom-call | tf_op jit(solution)/shard_map/score/pallas_call | solution.py:240
  61.5 10.4 %all_to_all.15.parts_ref = bf16[16,32,128]{2,1,0:T(8,128)(2,1)S(1)} all-to-all(bf16[16,32,128]{2,1,0:T(8,128)(2,1)S(1)} %score.1), channel_id=1, replica_groups={{0,1,8,9,128,129,136,137,256,257,264,265,384,385,392,393},{16,17,24,25,..., dimensions={0} | all-to-all | bytes 262144 | tf_op jit(solution)/shard_map/all_to_all | solution.py:259
  71.9 0.0 copy-done.1
  71.9 1.1 %finish.1 = (f32[32,256]{1,0:T(8,128)}, f32[8,32]{1,0:T(8,128)}) custom-call(bf16[16,32,128]{2,1,0:T(8,128)(2,1)S(1)} %all_to_all.15.parts_ref, s32[1,256]{1,0:T(1,128)S(1)} %bitcast.8), custom_call_target="tpu_custom_call" | custom-call | tf_op jit(solution)/shard_map/finish/pallas_call | solution.py:200
  (12 shorter events, 0.3 us)
Async XLA Ops:
  0.6 13.7 %copy-start.3 = (bf16[32,16384]{1,0:T(8,128)(2,1)S(1)}, bf16[32,16384]{1,0:T(8,128)(2,1)}, u32[]{:S(2)}) copy-start(bf16[32,16384]{1,0:T(8,128)(2,1)} %param.12) | copy-start | bytes 3145732
  4.1 19.2 %all-to-all-start = ((f32[8,64,128]{2,1,0:T(8,128)}), f32[8,64,128]{2,1,0:T(8,128)S(1)}, u32[]{:S(2)}, u32[]{:S(2)}) async-start(f32[8,64,128]{2,1,0:T(8,128)} %bitcast.9), calls=%async_computation | async-start | bytes 524288 | tf_op jit(solution)/shard_map/all_to_all | solution.py:293
  14.3 26.9 %collective-permute-start.1 = (bf16[32,4096]{1,0:T(8,128)(2,1)S(1)}, bf16[32,4096]{1,0:T(8,128)(2,1)S(1)}, u32[]{:S(2)}, u32[]{:S(2)}) collective-permute-start(bf16[32,4096]{1,0:T(8,128)(2,1)S(1)} %constant_dynamic-slice_fusion.6), channel_id=1, source_target_pairs={{256,0},{257,1},{264,8},{265,9},{272,16},{273,17},{280,24},{281,25... | collective-permute-start | bytes 786440 | tf_op jit(solution)/shard_map/ppermute | solution.py:50
  16.4 6.9 %copy-start = (s32[4,32]{1,0:T(4,128)S(1)}, s32[4,32]{1,0:T(4,128)}, u32[]{:S(2)}) copy-start(s32[4,32]{1,0:T(4,128)} %mask_ref.1) | copy-start | bytes 1540
  16.4 6.9 %copy-start.2 = (s32[4]{0:T(128)S(1)}, s32[4]{0:T(128)}, u32[]{:S(2)}) copy-start(s32[4]{0:T(128)} %lengths_ref.1) | copy-start | bytes 52
  16.4 20.6 %collective-permute-start = (bf16[32,8192]{1,0:T(8,128)(2,1)S(1)}, bf16[32,8192]{1,0:T(8,128)(2,1)S(1)}, u32[]{:S(2)}, u32[]{:S(2)}) collective-permute-start(bf16[32,8192]{1,0:T(8,128)(2,1)S(1)} %pad_maximum_fusion.2), channel_id=1, source_target_pairs={{8,0},{9,1},{0,8},{1,9},{24,16},{25,17},{16,24},{17,25},{40,32},{4... | collective-permute-start | bytes 1572872 | tf_op jit(solution)/shard_map/ppermute | solution.py:50
  25.6 33.9 %all-to-all-start.1 = ((bf16[64,32,128]{2,1,0:T(8,128)(2,1)}), bf16[64,32,128]{2,1,0:T(8,128)(2,1)S(1)}, u32[]{:S(2)}, u32[]{:S(2)}) async-start(bf16[64,32,128]{2,1,0:T(8,128)(2,1)} %bitcast.1), calls=%async_computation.1 | async-start | bytes 1048576 | tf_op jit(solution)/shard_map/all_to_all | solution.py:259
  37.1 13.7 %collective-permute-start.2 = (bf16[64,2048]{1,0:T(8,128)(2,1)S(1)}, bf16[64,2048]{1,0:T(8,128)(2,1)S(1)}, u32[]{:S(2)}, u32[]{:S(2)}) collective-permute-start(bf16[64,2048]{1,0:T(8,128)(2,1)S(1)} %pad_maximum_fusion.3), channel_id=1, source_target_pairs={{128,0},{129,1},{136,8},{137,9},{144,16},{145,17},{152,24},{153,25... | collective-permute-start | bytes 786440 | tf_op jit(solution)/shard_map/ppermute | solution.py:50
  41.2 14.1 %collective-permute-start.3 = (bf16[64,2048]{1,0:T(8,128)(2,1)S(1)}, bf16[64,2048]{1,0:T(8,128)(2,1)S(1)}, u32[]{:S(2)}, u32[]{:S(2)}) collective-permute-start(bf16[64,2048]{1,0:T(8,128)(2,1)S(1)} %pad_maximum_fusion.4), channel_id=1, source_target_pairs={{384,0},{385,1},{392,8},{393,9},{400,16},{401,17},{408,24},{409,25... | collective-permute-start | bytes 786440 | tf_op jit(solution)/shard_map/ppermute | solution.py:50
  45.9 10.5 %collective-permute-start.4 = (bf16[32,2048]{1,0:T(8,128)(2,1)S(1)}, bf16[32,2048]{1,0:T(8,128)(2,1)S(1)}, u32[]{:S(2)}, u32[]{:S(2)}) collective-permute-start(bf16[32,2048]{1,0:T(8,128)(2,1)S(1)} %get-tuple-element.22), channel_id=1, source_target_pairs={{8,0},{9,1},{0,8},{1,9},{24,16},{25,17},{16,24},{17,25},{40,32},{4... | collective-permute-start | bytes 393224 | tf_op jit(solution)/shard_map/ppermute | solution.py:50
  50.9 9.9 %collective-permute-start.5 = (bf16[160,2048]{1,0:T(8,128)(2,1)S(1)}, bf16[160,2048]{1,0:T(8,128)(2,1)S(1)}, u32[]{:S(2)}, u32[]{:S(2)}) collective-permute-start(bf16[160,2048]{1,0:T(8,128)(2,1)S(1)} %pad_maximum_fusion.refs_0_), channel_id=1, source_target_pairs={{1,0},{0,1},{9,8},{8,9},{17,16},{16,17},{25,24},{24,25},{33,32},{3... | collective-permute-start | bytes 1966088 | tf_op jit(solution)/shard_map/ppermute | solution.py:50
  56.4 4.4 %collective-permute-start.6 = (bf16[96,2048]{1,0:T(8,128)(2,1)S(1)}, bf16[96,2048]{1,0:T(8,128)(2,1)S(1)}, u32[]{:S(2)}, u32[]{:S(2)}) collective-permute-start(bf16[96,2048]{1,0:T(8,128)(2,1)S(1)} %constant_dynamic-update-slice_fusion.refs_1_), channel_id=1, source_target_pairs={{1,0},{0,1},{9,8},{8,9},{17,16},{16,17},{25,24},{24,25},{33,32},{3... | collective-permute-start | bytes 1179656 | tf_op jit(solution)/shard_map/ppermute | solution.py:50
  60.8 11.2 %copy-start.1 = (s32[256,1]{0,1:T(1,128)S(1)}, s32[256,1]{0,1:T(1,128)}, u32[]{:S(2)}) copy-start(s32[256,1]{0,1:T(1,128)} %param.15) | copy-start | bytes 3076

commit v8 on v7

--- a/solution.py
+++ b/solution.py
@@ -68,7 +68,7 @@
 
 
 def project_kernel(
-    in_ref, grad_ref, in_proj_ref, out_proj_ref, out_ref, in_buf, grad_buf, in_proj_buf, out_proj_buf, sems
+    in_ref, grad_ref, in_proj_ref, out_proj_ref, out_ref, in_buf, grad_buf, in_proj_buf, out_proj_buf, out_buf, sems, out_sems
 ):
     x, _, _, _ = here()
     sources = (in_ref, grad_ref, in_proj_ref, out_proj_ref)
@@ -87,11 +87,16 @@
             rows.reshape(-1, rows.shape[-1]), proj, (((1,), (1,)), ((), ())), preferred_element_type=jnp.float32
         )
 
+    stores = []
     for layer in range(LAYERS):
         for copy in copies[layer]:
             copy.wait()
         both = [side(in_buf[layer], in_proj_buf[layer]), side(grad_buf[layer], out_proj_buf[layer])]
-        out_ref[pl.ds(x ^ layer, 1)] = jnp.concatenate(both, axis=1)[None]
+        out_buf[layer] = jnp.concatenate(both, axis=1)
+        stores.append(pltpu.make_async_copy(out_buf.at[layer], out_ref.at[x ^ layer], out_sems.at[layer]))
+        stores[layer].start()
+    for store in stores:
+        store.wait()
 
 
 def project(query_inputs, query_output_grads, in_projection, out_projection):
@@ -101,13 +106,15 @@
         project_kernel,
         out_shape=jax.ShapeDtypeStruct((LAYERS, queries * seq, 2 * WIDTH), jnp.float32),
         in_specs=[hbm] * 4,
-        out_specs=pl.BlockSpec(memory_space=pltpu.VMEM),
+        out_specs=hbm,
         scratch_shapes=[
             pltpu.VMEM(query_inputs.shape, query_inputs.dtype),
             pltpu.VMEM(query_inputs.shape, query_inputs.dtype),
             pltpu.VMEM(in_projection.shape, in_projection.dtype),
             pltpu.VMEM(in_projection.shape, in_projection.dtype),
+            pltpu.VMEM((LAYERS, queries * seq, 2 * WIDTH), jnp.float32),
             pltpu.SemaphoreType.DMA((LAYERS, 4)),
+            pltpu.SemaphoreType.DMA((LAYERS,)),
         ],
         compiler_params=pltpu.CompilerParams(vmem_limit_bytes=60 * 1024 * 1024),
         name="project",

time: 73.5 us -> 73.5 us (level)
  no operation moved by 1% of the time
where the time goes in v8:
time: 73.5 us; the launch traced here: 73 us
  starting transfers between devices  45.4 us (62%)
  blocking collectives  10.5 us (14%)
  waiting for transfers between devices  8.12 us (11%)
  Pallas kernels  7.48 us (10%)
  between operations  0.89 us (1%)
    ppermute x7, starting transfers between devices, swapped(): lax.ppermute(block, AXES, [(flat(*change(*p)), flat(*p)) for p in places()])  23.8 us
    all_to_all x1, starting transfers between devices, exchange(): lax.all_to_all(blocks, AXES, 0, 0, axis_index_groups=partition(members))  11.4 us
    all_to_all x1, blocking collectives, exchange(): lax.all_to_all(blocks, AXES, 0, 0, axis_index_groups=partition(members))  10.5 us
    all_to_all x1, starting transfers between devices, body(): parts = lax.all_to_all(parts, 'tensor', 0, 0)  10.2 us
    ppermute x7, waiting for transfers between devices, swapped(): lax.ppermute(block, AXES, [(flat(*change(*p)), flat(*p)) for p in places()])  4.25 us
    all_to_all x1, waiting for transfers between devices, body(): parts = lax.all_to_all(parts, 'tensor', 0, 0)  3.86 us
    pallas_call x1, Pallas kernels, project(): pl.pallas_call(project_kernel, out_shape=jax.ShapeDtypeStruct((LAYERS, qu...  3.42 us
    pallas_call x1, Pallas kernels, outer(): pl.pallas_call(outer_kernel, out_shape=jax.ShapeDtypeStruct((members // 2...  2.24 us
  transfers between devices with their start and end apart: 9, of which 5 were waited for; matrix products, arithmetic and copies ran while one was open for 1% of the time, Pallas kernels for 3%

profile of v8, /device:TPU:1, one launch (start us, length us, event | category | flops | bytes accessed | tf_op | source)
XLA Modules:
  0.0 73.0 jit_solution(2721015125038846759)
XLA Ops:
  0.6 0.0 copy-start.3
  0.6 3.4 %project.1 = f32[4,128,128]{2,1,0:T(8,128)} custom-call(bf16[4,4,32,1024]{3,2,1,0:T(8,128)(2,1)} %in_ref.1, bf16[4,4,32,1024]{3,2,1,0:T(8,128)(2,1)} %grad_ref.1, bf16[4,64,1024]{2,1,0:T(8,128)(2,1)} %in_proj_ref.1, bf16[4,64,1024]{2,1,0:T(8,128)(2,1)} %out_proj_ref.1), custom_call_target="tpu_custom_call" | custom-call | tf_op jit(solution)/shard_map/project/pallas_call | solution.py:105
  4.1 10.2 %all-to-all-start = ((f32[8,64,128]{2,1,0:T(8,128)}), f32[8,64,128]{2,1,0:T(8,128)S(1)}, u32[]{:S(2)}, u32[]{:S(2)}) async-start(f32[8,64,128]{2,1,0:T(8,128)} %bitcast.9), calls=%async_computation | async-start | bytes 524288 | tf_op jit(solution)/shard_map/all_to_all | solution.py:300
  14.3 0.0 copy-done.3
  14.3 1.9 %collective-permute-start.1 = (bf16[32,4096]{1,0:T(8,128)(2,1)S(1)}, bf16[32,4096]{1,0:T(8,128)(2,1)S(1)}, u32[]{:S(2)}, u32[]{:S(2)}) collective-permute-start(bf16[32,4096]{1,0:T(8,128)(2,1)S(1)} %constant_dynamic-slice_fusion.6), channel_id=1, source_target_pairs={{256,0},{257,1},{264,8},{265,9},{272,16},{273,17},{280,24},{281,25... | collective-permute-start | bytes 786440 | tf_op jit(solution)/shard_map/ppermute | solution.py:50
  16.2 0.1 constant_dynamic-slice_fusion.16
  16.4 0.0 copy-start
  16.4 0.0 copy-start.2
  16.4 2.9 %collective-permute-start = (bf16[32,8192]{1,0:T(8,128)(2,1)S(1)}, bf16[32,8192]{1,0:T(8,128)(2,1)S(1)}, u32[]{:S(2)}, u32[]{:S(2)}) collective-permute-start(bf16[32,8192]{1,0:T(8,128)(2,1)S(1)} %pad_maximum_fusion.2), channel_id=1, source_target_pairs={{8,0},{9,1},{0,8},{1,9},{24,16},{25,17},{16,24},{17,25},{40,32},{4... | collective-permute-start | bytes 1572872 | tf_op jit(solution)/shard_map/ppermute | solution.py:50
  19.4 3.9 %all-to-all-done.parts_ref = f32[8,64,128]{2,1,0:T(8,128)S(1)} async-done(((f32[8,64,128]{2,1,0:T(8,128)}), f32[8,64,128]{2,1,0:T(8,128)S(1)}, u32[]{:S(2)}, u32[]{:S(2)}) %all-to-all-start) | async-done | bytes 262176 | tf_op jit(solution)/shard_map/all_to_all | solution.py:300
  23.3 0.0 copy-done
  23.3 0.0 copy-done.2
  23.3 2.2 %outer.1 = bf16[32,2,32,128]{3,2,1,0:T(8,128)(2,1)} custom-call(s32[4]{0:T(128)S(1)} %copy-done.2, s32[4,32]{1,0:T(4,128)S(1)} %copy-done, f32[8,64,128]{2,1,0:T(8,128)S(1)} %all-to-all-done.parts_ref), custom_call_target="tpu_custom_call" | custom-call | bytes 62914560 | tf_op jit(solution)/shard_map/outer/pallas_call | solution.py:160
  25.5 11.4 %all-to-all-start.1 = ((bf16[64,32,128]{2,1,0:T(8,128)(2,1)}), bf16[64,32,128]{2,1,0:T(8,128)(2,1)S(1)}, u32[]{:S(2)}, u32[]{:S(2)}) async-start(bf16[64,32,128]{2,1,0:T(8,128)(2,1)} %bitcast.1), calls=%async_computation.1 | async-start | bytes 1048576 | tf_op jit(solution)/shard_map/all_to_all | solution.py:266
  37.0 0.0 collective-permute-done
  37.1 4.1 %collective-permute-start.2 = (bf16[64,2048]{1,0:T(8,128)(2,1)S(1)}, bf16[64,2048]{1,0:T(8,128)(2,1)S(1)}, u32[]{:S(2)}, u32[]{:S(2)}) collective-permute-start(bf16[64,2048]{1,0:T(8,128)(2,1)S(1)} %pad_maximum_fusion.3), channel_id=1, source_target_pairs={{128,0},{129,1},{136,8},{137,9},{144,16},{145,17},{152,24},{153,25... | collective-permute-start | bytes 786440 | tf_op jit(solution)/shard_map/ppermute | solution.py:50
  41.2 0.0 collective-permute-done.1
  41.2 4.6 %collective-permute-start.3 = (bf16[64,2048]{1,0:T(8,128)(2,1)S(1)}, bf16[64,2048]{1,0:T(8,128)(2,1)S(1)}, u32[]{:S(2)}, u32[]{:S(2)}) collective-permute-start(bf16[64,2048]{1,0:T(8,128)(2,1)S(1)} %pad_maximum_fusion.4), channel_id=1, source_target_pairs={{384,0},{385,1},{392,8},{393,9},{400,16},{401,17},{408,24},{409,25... | collective-permute-start | bytes 786440 | tf_op jit(solution)/shard_map/ppermute | solution.py:50
  45.8 3.1 %collective-permute-start.4 = (bf16[32,2048]{1,0:T(8,128)(2,1)S(1)}, bf16[32,2048]{1,0:T(8,128)(2,1)S(1)}, u32[]{:S(2)}, u32[]{:S(2)}) collective-permute-start(bf16[32,2048]{1,0:T(8,128)(2,1)S(1)} %get-tuple-element.22), channel_id=1, source_target_pairs={{8,0},{9,1},{0,8},{1,9},{24,16},{25,17},{16,24},{17,25},{40,32},{4... | collective-permute-start | bytes 393224 | tf_op jit(solution)/shard_map/ppermute | solution.py:50
  48.9 1.6 %collective-permute-done.2 = bf16[64,2048]{1,0:T(8,128)(2,1)S(1)} collective-permute-done((bf16[64,2048]{1,0:T(8,128)(2,1)S(1)}, bf16[64,2048]{1,0:T(8,128)(2,1)S(1)}, u32[]{:S(2)}, u32[]{:S(2)}) %collective-permute-start.2) | collective-permute-done | bytes 262176 | tf_op jit(solution)/shard_map/ppermute | solution.py:50
  50.6 4.2 %collective-permute-start.5 = (bf16[160,2048]{1,0:T(8,128)(2,1)S(1)}, bf16[160,2048]{1,0:T(8,128)(2,1)S(1)}, u32[]{:S(2)}, u32[]{:S(2)}) collective-permute-start(bf16[160,2048]{1,0:T(8,128)(2,1)S(1)} %pad_maximum_fusion.refs_0_), channel_id=1, source_target_pairs={{1,0},{0,1},{9,8},{8,9},{17,16},{16,17},{25,24},{24,25},{33,32},{3... | collective-permute-start | bytes 1966088 | tf_op jit(solution)/shard_map/ppermute | solution.py:50
  54.7 0.5 collective-permute-done.3
  55.3 1.1 %collective-permute-done.4 = bf16[32,2048]{1,0:T(8,128)(2,1)S(1)} collective-permute-done((bf16[32,2048]{1,0:T(8,128)(2,1)S(1)}, bf16[32,2048]{1,0:T(8,128)(2,1)S(1)}, u32[]{:S(2)}, u32[]{:S(2)}) %collective-permute-start.4) | collective-permute-done | bytes 131104 | tf_op jit(solution)/shard_map/ppermute | solution.py:50
  56.3 3.0 %collective-permute-start.6 = (bf16[96,2048]{1,0:T(8,128)(2,1)S(1)}, bf16[96,2048]{1,0:T(8,128)(2,1)S(1)}, u32[]{:S(2)}, u32[]{:S(2)}) collective-permute-start(bf16[96,2048]{1,0:T(8,128)(2,1)S(1)} %constant_dynamic-update-slice_fusion.refs_1_), channel_id=1, source_target_pairs={{1,0},{0,1},{9,8},{8,9},{17,16},{16,17},{25,24},{24,25},{33,32},{3... | collective-permute-start | bytes 1179656 | tf_op jit(solution)/shard_map/ppermute | solution.py:50
  59.3 0.0 all-to-all-done.1
  59.4 0.2 copy.13
  59.6 1.1 %collective-permute-done.6.refs_3_ = bf16[96,2048]{1,0:T(8,128)(2,1)S(1)} collective-permute-done((bf16[96,2048]{1,0:T(8,128)(2,1)S(1)}, bf16[96,2048]{1,0:T(8,128)(2,1)S(1)}, u32[]{:S(2)}, u32[]{:S(2)}) %collective-permute-start.6) | collective-permute-done | bytes 393248 | tf_op jit(solution)/shard_map/ppermute | solution.py:50
  60.7 0.0 collective-permute-done.5.refs_2_
  60.7 0.7 %score.1 = bf16[16,32,128]{2,1,0:T(8,128)(2,1)S(1)} custom-call(bf16[160,2048]{1,0:T(8,128)(2,1)S(1)} %pad_maximum_fusion.refs_0_, bf16[96,2048]{1,0:T(8,128)(2,1)S(1)} %constant_dynamic-update-slice_fusion.refs_1_, bf16[160,2048]{1,0:T(8,128)(2,1)S(1)} %collective-permute-done.5.refs_2_, bf16[96,2048]{1,0:T(8,128)(2,1)S(1)} %collective-permute-done.6.refs_3_, ...), custom_call_target="tpu_custom_call" | custom-call | tf_op jit(solution)/shard_map/score/pallas_call | solution.py:247
  61.4 10.5 %all_to_all.15.parts_ref = bf16[16,32,128]{2,1,0:T(8,128)(2,1)S(1)} all-to-all(bf16[16,32,128]{2,1,0:T(8,128)(2,1)S(1)} %score.1), channel_id=1, replica_groups={{0,1,8,9,128,129,136,137,256,257,264,265,384,385,392,393},{16,17,24,25,..., dimensions={0} | all-to-all | bytes 262144 | tf_op jit(solution)/shard_map/all_to_all | solution.py:266
  71.9 0.0 copy-done.1
  71.9 1.1 %finish.1 = (f32[32,256]{1,0:T(8,128)}, f32[8,32]{1,0:T(8,128)}) custom-call(bf16[16,32,128]{2,1,0:T(8,128)(2,1)S(1)} %all_to_all.15.parts_ref, s32[1,256]{1,0:T(1,128)S(1)} %bitcast.8), custom_call_target="tpu_custom_call" | custom-call | tf_op jit(solution)/shard_map/finish/pallas_call | solution.py:207
  (12 shorter events, 0.3 us)
Async XLA Ops:
  0.6 13.6 %copy-start.3 = (bf16[32,16384]{1,0:T(8,128)(2,1)S(1)}, bf16[32,16384]{1,0:T(8,128)(2,1)}, u32[]{:S(2)}) copy-start(bf16[32,16384]{1,0:T(8,128)(2,1)} %param.12) | copy-start | bytes 3145732
  4.1 19.2 %all-to-all-start = ((f32[8,64,128]{2,1,0:T(8,128)}), f32[8,64,128]{2,1,0:T(8,128)S(1)}, u32[]{:S(2)}, u32[]{:S(2)}) async-start(f32[8,64,128]{2,1,0:T(8,128)} %bitcast.9), calls=%async_computation | async-start | bytes 524288 | tf_op jit(solution)/shard_map/all_to_all | solution.py:300
  14.3 26.9 %collective-permute-start.1 = (bf16[32,4096]{1,0:T(8,128)(2,1)S(1)}, bf16[32,4096]{1,0:T(8,128)(2,1)S(1)}, u32[]{:S(2)}, u32[]{:S(2)}) collective-permute-start(bf16[32,4096]{1,0:T(8,128)(2,1)S(1)} %constant_dynamic-slice_fusion.6), channel_id=1, source_target_pairs={{256,0},{257,1},{264,8},{265,9},{272,16},{273,17},{280,24},{281,25... | collective-permute-start | bytes 786440 | tf_op jit(solution)/shard_map/ppermute | solution.py:50
  16.4 6.9 %copy-start = (s32[4,32]{1,0:T(4,128)S(1)}, s32[4,32]{1,0:T(4,128)}, u32[]{:S(2)}) copy-start(s32[4,32]{1,0:T(4,128)} %mask_ref.1) | copy-start | bytes 1540
  16.4 6.9 %copy-start.2 = (s32[4]{0:T(128)S(1)}, s32[4]{0:T(128)}, u32[]{:S(2)}) copy-start(s32[4]{0:T(128)} %lengths_ref.1) | copy-start | bytes 52
  16.4 20.6 %collective-permute-start = (bf16[32,8192]{1,0:T(8,128)(2,1)S(1)}, bf16[32,8192]{1,0:T(8,128)(2,1)S(1)}, u32[]{:S(2)}, u32[]{:S(2)}) collective-permute-start(bf16[32,8192]{1,0:T(8,128)(2,1)S(1)} %pad_maximum_fusion.2), channel_id=1, source_target_pairs={{8,0},{9,1},{0,8},{1,9},{24,16},{25,17},{16,24},{17,25},{40,32},{4... | collective-permute-start | bytes 1572872 | tf_op jit(solution)/shard_map/ppermute | solution.py:50
  25.5 33.8 %all-to-all-start.1 = ((bf16[64,32,128]{2,1,0:T(8,128)(2,1)}), bf16[64,32,128]{2,1,0:T(8,128)(2,1)S(1)}, u32[]{:S(2)}, u32[]{:S(2)}) async-start(bf16[64,32,128]{2,1,0:T(8,128)(2,1)} %bitcast.1), calls=%async_computation.1 | async-start | bytes 1048576 | tf_op jit(solution)/shard_map/all_to_all | solution.py:266
  37.1 13.5 %collective-permute-start.2 = (bf16[64,2048]{1,0:T(8,128)(2,1)S(1)}, bf16[64,2048]{1,0:T(8,128)(2,1)S(1)}, u32[]{:S(2)}, u32[]{:S(2)}) collective-permute-start(bf16[64,2048]{1,0:T(8,128)(2,1)S(1)} %pad_maximum_fusion.3), channel_id=1, source_target_pairs={{128,0},{129,1},{136,8},{137,9},{144,16},{145,17},{152,24},{153,25... | collective-permute-start | bytes 786440 | tf_op jit(solution)/shard_map/ppermute | solution.py:50
  41.2 14.1 %collective-permute-start.3 = (bf16[64,2048]{1,0:T(8,128)(2,1)S(1)}, bf16[64,2048]{1,0:T(8,128)(2,1)S(1)}, u32[]{:S(2)}, u32[]{:S(2)}) collective-permute-start(bf16[64,2048]{1,0:T(8,128)(2,1)S(1)} %pad_maximum_fusion.4), channel_id=1, source_target_pairs={{384,0},{385,1},{392,8},{393,9},{400,16},{401,17},{408,24},{409,25... | collective-permute-start | bytes 786440 | tf_op jit(solution)/shard_map/ppermute | solution.py:50
  45.8 10.5 %collective-permute-start.4 = (bf16[32,2048]{1,0:T(8,128)(2,1)S(1)}, bf16[32,2048]{1,0:T(8,128)(2,1)S(1)}, u32[]{:S(2)}, u32[]{:S(2)}) collective-permute-start(bf16[32,2048]{1,0:T(8,128)(2,1)S(1)} %get-tuple-element.22), channel_id=1, source_target_pairs={{8,0},{9,1},{0,8},{1,9},{24,16},{25,17},{16,24},{17,25},{40,32},{4... | collective-permute-start | bytes 393224 | tf_op jit(solution)/shard_map/ppermute | solution.py:50
  50.6 10.1 %collective-permute-start.5 = (bf16[160,2048]{1,0:T(8,128)(2,1)S(1)}, bf16[160,2048]{1,0:T(8,128)(2,1)S(1)}, u32[]{:S(2)}, u32[]{:S(2)}) collective-permute-start(bf16[160,2048]{1,0:T(8,128)(2,1)S(1)} %pad_maximum_fusion.refs_0_), channel_id=1, source_target_pairs={{1,0},{0,1},{9,8},{8,9},{17,16},{16,17},{25,24},{24,25},{33,32},{3... | collective-permute-start | bytes 1966088 | tf_op jit(solution)/shard_map/ppermute | solution.py:50
  56.3 4.3 %collective-permute-start.6 = (bf16[96,2048]{1,0:T(8,128)(2,1)S(1)}, bf16[96,2048]{1,0:T(8,128)(2,1)S(1)}, u32[]{:S(2)}, u32[]{:S(2)}) collective-permute-start(bf16[96,2048]{1,0:T(8,128)(2,1)S(1)} %constant_dynamic-update-slice_fusion.refs_1_), channel_id=1, source_target_pairs={{1,0},{0,1},{9,8},{8,9},{17,16},{16,17},{25,24},{24,25},{33,32},{3... | collective-permute-start | bytes 1179656 | tf_op jit(solution)/shard_map/ppermute | solution.py:50
  60.7 11.2 %copy-start.1 = (s32[256,1]{0,1:T(1,128)S(1)}, s32[256,1]{0,1:T(1,128)}, u32[]{:S(2)}) copy-start(s32[256,1]{0,1:T(1,128)} %param.15) | copy-start | bytes 3076

commit v9 on v7

--- a/solution.py
+++ b/solution.py
@@ -209,26 +209,22 @@
 
 
 def score_kernel(*refs):
-    *rows_refs, blocks_ref, out_ref, rows_buf, queries_buf = refs
+    *rows_refs, blocks_ref, out_ref, queries_buf = refs
     x, _, z_low, core = here()
     lines, sources, lanes = blocks_ref.shape
     for line in range(lines):
         pair, query = line // 2, line % 2
         queries_buf[query * sources : (query + 1) * sources, pair * lanes : (pair + 1) * lanes] = blocks_ref[line]
-    at = 0
+    places = [(other_core, *place) for other_core in range(NC) for place in ORDER]
+    rows = out_ref.shape[1]
     for ref in rows_refs:
-        rows_buf[at : at + ref.shape[0], :] = ref[...]
-        at += ref.shape[0]
-    result = lax.dot_general(
-        rows_buf[...], queries_buf[...], (((1,), (1,)), ((), ())), preferred_element_type=jnp.float32
-    )
-    rows = out_ref.shape[1]
-    at = 0
-    for other_core in range(NC):
-        for step, other_z in ORDER:
+        result = lax.dot_general(
+            ref[...], queries_buf[...], (((1,), (1,)), ((), ())), preferred_element_type=jnp.float32
+        )
+        for n in range(ref.shape[0] // rows):
+            other_core, step, other_z = places.pop(0)
             member = ((x ^ step) * 2 + (z_low ^ other_z)) * NC + (core ^ other_core)
-            out_ref[pl.ds(member, 1)] = result[at : at + rows].astype(out_ref.dtype)[None]
-            at += rows
+            out_ref[pl.ds(member, 1)] = result[n * rows : (n + 1) * rows].astype(out_ref.dtype)[None]
 
 
 def score(rows, blocks):
@@ -243,7 +239,6 @@
         in_specs=[vmem] * (len(rows) + 1),
         out_specs=vmem,
         scratch_shapes=[
-            pltpu.VMEM((count, width), jnp.bfloat16),
             pltpu.VMEM((queries, width), jnp.bfloat16),
         ],
         compiler_params=pltpu.CompilerParams(vmem_limit_bytes=24 * 1024 * 1024),

time: 73.5 us -> 73.6 us (level)
  no operation moved by 1% of the time
where the time goes in v9:
time: 73.6 us; the launch traced here: 73.1 us
  starting transfers between devices  45.2 us (61%)
  blocking collectives  10.4 us (14%)
  waiting for transfers between devices  8.35 us (11%)
  Pallas kernels  7.55 us (10%)
  between operations  0.89 us (1%)
    ppermute x7, starting transfers between devices, swapped(): lax.ppermute(block, AXES, [(flat(*change(*p)), flat(*p)) for p in places()])  23.6 us
    all_to_all x1, starting transfers between devices, exchange(): lax.all_to_all(blocks, AXES, 0, 0, axis_index_groups=partition(members))  11.4 us
    all_to_all x1, blocking collectives, exchange(): lax.all_to_all(blocks, AXES, 0, 0, axis_index_groups=partition(members))  10.4 us
    all_to_all x1, starting transfers between devices, body(): parts = lax.all_to_all(parts, 'tensor', 0, 0)  10.2 us
    ppermute x7, waiting for transfers between devices, swapped(): lax.ppermute(block, AXES, [(flat(*change(*p)), flat(*p)) for p in places()])  4.49 us
    all_to_all x1, waiting for transfers between devices, body(): parts = lax.all_to_all(parts, 'tensor', 0, 0)  3.87 us
    pallas_call x1, Pallas kernels, project(): pl.pallas_call(project_kernel, out_shape=jax.ShapeDtypeStruct((LAYERS, qu...  3.44 us
    pallas_call x1, Pallas kernels, outer(): pl.pallas_call(outer_kernel, out_shape=jax.ShapeDtypeStruct((members // 2...  2.24 us
  transfers between devices with their start and end apart: 9, of which 5 were waited for; matrix products, arithmetic and copies ran while one was open for 1% of the time, Pallas kernels for 3%

profile of v9, /device:TPU:1, one launch (start us, length us, event | category | flops | bytes accessed | tf_op | source)
XLA Modules:
  0.0 73.1 jit_solution(9500781883329582438)
XLA Ops:
  0.6 0.0 copy-start.3
  0.6 3.4 %project.1 = f32[4,128,128]{2,1,0:T(8,128)} custom-call(bf16[4,4,32,1024]{3,2,1,0:T(8,128)(2,1)} %in_ref.1, bf16[4,4,32,1024]{3,2,1,0:T(8,128)(2,1)} %grad_ref.1, bf16[4,64,1024]{2,1,0:T(8,128)(2,1)} %in_proj_ref.1, bf16[4,64,1024]{2,1,0:T(8,128)(2,1)} %out_proj_ref.1), custom_call_target="tpu_custom_call" | custom-call | tf_op jit(solution)/shard_map/project/pallas_call | solution.py:100
  4.1 10.2 %all-to-all-start = ((f32[8,64,128]{2,1,0:T(8,128)}), f32[8,64,128]{2,1,0:T(8,128)S(1)}, u32[]{:S(2)}, u32[]{:S(2)}) async-start(f32[8,64,128]{2,1,0:T(8,128)} %bitcast.9), calls=%async_computation | async-start | bytes 524288 | tf_op jit(solution)/shard_map/all_to_all | solution.py:288
  14.3 0.0 copy-done.3
  14.3 1.9 %collective-permute-start.1 = (bf16[32,4096]{1,0:T(8,128)(2,1)S(1)}, bf16[32,4096]{1,0:T(8,128)(2,1)S(1)}, u32[]{:S(2)}, u32[]{:S(2)}) collective-permute-start(bf16[32,4096]{1,0:T(8,128)(2,1)S(1)} %constant_dynamic-slice_fusion.6), channel_id=1, source_target_pairs={{256,0},{257,1},{264,8},{265,9},{272,16},{273,17},{280,24},{281,25... | collective-permute-start | bytes 786440 | tf_op jit(solution)/shard_map/ppermute | solution.py:50
  16.3 0.1 constant_dynamic-slice_fusion.16
  16.4 0.0 copy-start
  16.4 0.0 copy-start.2
  16.4 2.9 %collective-permute-start = (bf16[32,8192]{1,0:T(8,128)(2,1)S(1)}, bf16[32,8192]{1,0:T(8,128)(2,1)S(1)}, u32[]{:S(2)}, u32[]{:S(2)}) collective-permute-start(bf16[32,8192]{1,0:T(8,128)(2,1)S(1)} %pad_maximum_fusion.2), channel_id=1, source_target_pairs={{8,0},{9,1},{0,8},{1,9},{24,16},{25,17},{16,24},{17,25},{40,32},{4... | collective-permute-start | bytes 1572872 | tf_op jit(solution)/shard_map/ppermute | solution.py:50
  19.5 3.9 %all-to-all-done.parts_ref = f32[8,64,128]{2,1,0:T(8,128)S(1)} async-done(((f32[8,64,128]{2,1,0:T(8,128)}), f32[8,64,128]{2,1,0:T(8,128)S(1)}, u32[]{:S(2)}, u32[]{:S(2)}) %all-to-all-start) | async-done | bytes 262176 | tf_op jit(solution)/shard_map/all_to_all | solution.py:288
  23.3 0.0 copy-done
  23.3 0.0 copy-done.2
  23.3 2.2 %outer.1 = bf16[32,2,32,128]{3,2,1,0:T(8,128)(2,1)} custom-call(s32[4]{0:T(128)S(1)} %copy-done.2, s32[4,32]{1,0:T(4,128)S(1)} %copy-done, f32[8,64,128]{2,1,0:T(8,128)S(1)} %all-to-all-done.parts_ref), custom_call_target="tpu_custom_call" | custom-call | bytes 62914560 | tf_op jit(solution)/shard_map/outer/pallas_call | solution.py:153
  25.6 11.4 %all-to-all-start.1 = ((bf16[64,32,128]{2,1,0:T(8,128)(2,1)}), bf16[64,32,128]{2,1,0:T(8,128)(2,1)S(1)}, u32[]{:S(2)}, u32[]{:S(2)}) async-start(bf16[64,32,128]{2,1,0:T(8,128)(2,1)} %bitcast.1), calls=%async_computation.1 | async-start | bytes 1048576 | tf_op jit(solution)/shard_map/all_to_all | solution.py:254
  37.0 0.0 collective-permute-done
  37.1 4.1 %collective-permute-start.2 = (bf16[64,2048]{1,0:T(8,128)(2,1)S(1)}, bf16[64,2048]{1,0:T(8,128)(2,1)S(1)}, u32[]{:S(2)}, u32[]{:S(2)}) collective-permute-start(bf16[64,2048]{1,0:T(8,128)(2,1)S(1)} %pad_maximum_fusion.3), channel_id=1, source_target_pairs={{128,0},{129,1},{136,8},{137,9},{144,16},{145,17},{152,24},{153,25... | collective-permute-start | bytes 786440 | tf_op jit(solution)/shard_map/ppermute | solution.py:50
  41.2 0.0 collective-permute-done.1
  41.2 4.6 %collective-permute-start.3 = (bf16[64,2048]{1,0:T(8,128)(2,1)S(1)}, bf16[64,2048]{1,0:T(8,128)(2,1)S(1)}, u32[]{:S(2)}, u32[]{:S(2)}) collective-permute-start(bf16[64,2048]{1,0:T(8,128)(2,1)S(1)} %pad_maximum_fusion.4), channel_id=1, source_target_pairs={{384,0},{385,1},{392,8},{393,9},{400,16},{401,17},{408,24},{409,25... | collective-permute-start | bytes 786440 | tf_op jit(solution)/shard_map/ppermute | solution.py:50
  45.9 3.1 %collective-permute-start.4 = (bf16[32,2048]{1,0:T(8,128)(2,1)S(1)}, bf16[32,2048]{1,0:T(8,128)(2,1)S(1)}, u32[]{:S(2)}, u32[]{:S(2)}) collective-permute-start(bf16[32,2048]{1,0:T(8,128)(2,1)S(1)} %get-tuple-element.22), channel_id=1, source_target_pairs={{8,0},{9,1},{0,8},{1,9},{24,16},{25,17},{16,24},{17,25},{40,32},{4... | collective-permute-start | bytes 393224 | tf_op jit(solution)/shard_map/ppermute | solution.py:50
  49.0 1.8 %collective-permute-done.2 = bf16[64,2048]{1,0:T(8,128)(2,1)S(1)} collective-permute-done((bf16[64,2048]{1,0:T(8,128)(2,1)S(1)}, bf16[64,2048]{1,0:T(8,128)(2,1)S(1)}, u32[]{:S(2)}, u32[]{:S(2)}) %collective-permute-start.2) | collective-permute-done | bytes 262176 | tf_op jit(solution)/shard_map/ppermute | solution.py:50
  50.9 3.9 %collective-permute-start.5 = (bf16[160,2048]{1,0:T(8,128)(2,1)S(1)}, bf16[160,2048]{1,0:T(8,128)(2,1)S(1)}, u32[]{:S(2)}, u32[]{:S(2)}) collective-permute-start(bf16[160,2048]{1,0:T(8,128)(2,1)S(1)} %pad_maximum_fusion.refs_0_), channel_id=1, source_target_pairs={{1,0},{0,1},{9,8},{8,9},{17,16},{16,17},{25,24},{24,25},{33,32},{3... | collective-permute-start | bytes 1966088 | tf_op jit(solution)/shard_map/ppermute | solution.py:50
  54.8 0.6 collective-permute-done.3
  55.4 1.0 %collective-permute-done.4 = bf16[32,2048]{1,0:T(8,128)(2,1)S(1)} collective-permute-done((bf16[32,2048]{1,0:T(8,128)(2,1)S(1)}, bf16[32,2048]{1,0:T(8,128)(2,1)S(1)}, u32[]{:S(2)}, u32[]{:S(2)}) %collective-permute-start.4) | collective-permute-done | bytes 131104 | tf_op jit(solution)/shard_map/ppermute | solution.py:50
  56.4 3.1 %collective-permute-start.6 = (bf16[96,2048]{1,0:T(8,128)(2,1)S(1)}, bf16[96,2048]{1,0:T(8,128)(2,1)S(1)}, u32[]{:S(2)}, u32[]{:S(2)}) collective-permute-start(bf16[96,2048]{1,0:T(8,128)(2,1)S(1)} %constant_dynamic-update-slice_fusion.refs_1_), channel_id=1, source_target_pairs={{1,0},{0,1},{9,8},{8,9},{17,16},{16,17},{25,24},{24,25},{33,32},{3... | collective-permute-start | bytes 1179656 | tf_op jit(solution)/shard_map/ppermute | solution.py:50
  59.5 0.0 all-to-all-done.1
  59.5 0.2 copy.13
  59.7 1.1 %collective-permute-done.6.refs_3_ = bf16[96,2048]{1,0:T(8,128)(2,1)S(1)} collective-permute-done((bf16[96,2048]{1,0:T(8,128)(2,1)S(1)}, bf16[96,2048]{1,0:T(8,128)(2,1)S(1)}, u32[]{:S(2)}, u32[]{:S(2)}) %collective-permute-start.6) | collective-permute-done | bytes 393248 | tf_op jit(solution)/shard_map/ppermute | solution.py:50
  60.8 0.0 collective-permute-done.5.refs_2_
  60.8 0.8 %score.1 = bf16[16,32,128]{2,1,0:T(8,128)(2,1)S(1)} custom-call(bf16[160,2048]{1,0:T(8,128)(2,1)S(1)} %pad_maximum_fusion.refs_0_, bf16[96,2048]{1,0:T(8,128)(2,1)S(1)} %constant_dynamic-update-slice_fusion.refs_1_, bf16[160,2048]{1,0:T(8,128)(2,1)S(1)} %collective-permute-done.5.refs_2_, bf16[96,2048]{1,0:T(8,128)(2,1)S(1)} %collective-permute-done.6.refs_3_, ...), custom_call_target="tpu_custom_call" | custom-call | tf_op jit(solution)/shard_map/score/pallas_call | solution.py:236
  61.6 10.4 %all_to_all.15.parts_ref = bf16[16,32,128]{2,1,0:T(8,128)(2,1)S(1)} all-to-all(bf16[16,32,128]{2,1,0:T(8,128)(2,1)S(1)} %score.1), channel_id=1, replica_groups={{0,1,8,9,128,129,136,137,256,257,264,265,384,385,392,393},{16,17,24,25,..., dimensions={0} | all-to-all | bytes 262144 | tf_op jit(solution)/shard_map/all_to_all | solution.py:254
  72.0 0.0 copy-done.1
  72.0 1.1 %finish.1 = (f32[32,256]{1,0:T(8,128)}, f32[8,32]{1,0:T(8,128)}) custom-call(bf16[16,32,128]{2,1,0:T(8,128)(2,1)S(1)} %all_to_all.15.parts_ref, s32[1,256]{1,0:T(1,128)S(1)} %bitcast.8), custom_call_target="tpu_custom_call" | custom-call | tf_op jit(solution)/shard_map/finish/pallas_call | solution.py:200
  (12 shorter events, 0.3 us)
Async XLA Ops:
  0.6 13.7 %copy-start.3 = (bf16[32,16384]{1,0:T(8,128)(2,1)S(1)}, bf16[32,16384]{1,0:T(8,128)(2,1)}, u32[]{:S(2)}) copy-start(bf16[32,16384]{1,0:T(8,128)(2,1)} %param.12) | copy-start | bytes 3145732
  4.1 19.2 %all-to-all-start = ((f32[8,64,128]{2,1,0:T(8,128)}), f32[8,64,128]{2,1,0:T(8,128)S(1)}, u32[]{:S(2)}, u32[]{:S(2)}) async-start(f32[8,64,128]{2,1,0:T(8,128)} %bitcast.9), calls=%async_computation | async-start | bytes 524288 | tf_op jit(solution)/shard_map/all_to_all | solution.py:288
  14.3 26.9 %collective-permute-start.1 = (bf16[32,4096]{1,0:T(8,128)(2,1)S(1)}, bf16[32,4096]{1,0:T(8,128)(2,1)S(1)}, u32[]{:S(2)}, u32[]{:S(2)}) collective-permute-start(bf16[32,4096]{1,0:T(8,128)(2,1)S(1)} %constant_dynamic-slice_fusion.6), channel_id=1, source_target_pairs={{256,0},{257,1},{264,8},{265,9},{272,16},{273,17},{280,24},{281,25... | collective-permute-start | bytes 786440 | tf_op jit(solution)/shard_map/ppermute | solution.py:50
  16.4 6.9 %copy-start = (s32[4,32]{1,0:T(4,128)S(1)}, s32[4,32]{1,0:T(4,128)}, u32[]{:S(2)}) copy-start(s32[4,32]{1,0:T(4,128)} %mask_ref.1) | copy-start | bytes 1540
  16.4 6.9 %copy-start.2 = (s32[4]{0:T(128)S(1)}, s32[4]{0:T(128)}, u32[]{:S(2)}) copy-start(s32[4]{0:T(128)} %lengths_ref.1) | copy-start | bytes 52
  16.4 20.6 %collective-permute-start = (bf16[32,8192]{1,0:T(8,128)(2,1)S(1)}, bf16[32,8192]{1,0:T(8,128)(2,1)S(1)}, u32[]{:S(2)}, u32[]{:S(2)}) collective-permute-start(bf16[32,8192]{1,0:T(8,128)(2,1)S(1)} %pad_maximum_fusion.2), channel_id=1, source_target_pairs={{8,0},{9,1},{0,8},{1,9},{24,16},{25,17},{16,24},{17,25},{40,32},{4... | collective-permute-start | bytes 1572872 | tf_op jit(solution)/shard_map/ppermute | solution.py:50
  25.6 33.9 %all-to-all-start.1 = ((bf16[64,32,128]{2,1,0:T(8,128)(2,1)}), bf16[64,32,128]{2,1,0:T(8,128)(2,1)S(1)}, u32[]{:S(2)}, u32[]{:S(2)}) async-start(bf16[64,32,128]{2,1,0:T(8,128)(2,1)} %bitcast.1), calls=%async_computation.1 | async-start | bytes 1048576 | tf_op jit(solution)/shard_map/all_to_all | solution.py:254
  37.1 13.7 %collective-permute-start.2 = (bf16[64,2048]{1,0:T(8,128)(2,1)S(1)}, bf16[64,2048]{1,0:T(8,128)(2,1)S(1)}, u32[]{:S(2)}, u32[]{:S(2)}) collective-permute-start(bf16[64,2048]{1,0:T(8,128)(2,1)S(1)} %pad_maximum_fusion.3), channel_id=1, source_target_pairs={{128,0},{129,1},{136,8},{137,9},{144,16},{145,17},{152,24},{153,25... | collective-permute-start | bytes 786440 | tf_op jit(solution)/shard_map/ppermute | solution.py:50
  41.2 14.1 %collective-permute-start.3 = (bf16[64,2048]{1,0:T(8,128)(2,1)S(1)}, bf16[64,2048]{1,0:T(8,128)(2,1)S(1)}, u32[]{:S(2)}, u32[]{:S(2)}) collective-permute-start(bf16[64,2048]{1,0:T(8,128)(2,1)S(1)} %pad_maximum_fusion.4), channel_id=1, source_target_pairs={{384,0},{385,1},{392,8},{393,9},{400,16},{401,17},{408,24},{409,25... | collective-permute-start | bytes 786440 | tf_op jit(solution)/shard_map/ppermute | solution.py:50
  45.9 10.5 %collective-permute-start.4 = (bf16[32,2048]{1,0:T(8,128)(2,1)S(1)}, bf16[32,2048]{1,0:T(8,128)(2,1)S(1)}, u32[]{:S(2)}, u32[]{:S(2)}) collective-permute-start(bf16[32,2048]{1,0:T(8,128)(2,1)S(1)} %get-tuple-element.22), channel_id=1, source_target_pairs={{8,0},{9,1},{0,8},{1,9},{24,16},{25,17},{16,24},{17,25},{40,32},{4... | collective-permute-start | bytes 393224 | tf_op jit(solution)/shard_map/ppermute | solution.py:50
  50.9 9.9 %collective-permute-start.5 = (bf16[160,2048]{1,0:T(8,128)(2,1)S(1)}, bf16[160,2048]{1,0:T(8,128)(2,1)S(1)}, u32[]{:S(2)}, u32[]{:S(2)}) collective-permute-start(bf16[160,2048]{1,0:T(8,128)(2,1)S(1)} %pad_maximum_fusion.refs_0_), channel_id=1, source_target_pairs={{1,0},{0,1},{9,8},{8,9},{17,16},{16,17},{25,24},{24,25},{33,32},{3... | collective-permute-start | bytes 1966088 | tf_op jit(solution)/shard_map/ppermute | solution.py:50
  56.4 4.4 %collective-permute-start.6 = (bf16[96,2048]{1,0:T(8,128)(2,1)S(1)}, bf16[96,2048]{1,0:T(8,128)(2,1)S(1)}, u32[]{:S(2)}, u32[]{:S(2)}) collective-permute-start(bf16[96,2048]{1,0:T(8,128)(2,1)S(1)} %constant_dynamic-update-slice_fusion.refs_1_), channel_id=1, source_target_pairs={{1,0},{0,1},{9,8},{8,9},{17,16},{16,17},{25,24},{24,25},{33,32},{3... | collective-permute-start | bytes 1179656 | tf_op jit(solution)/shard_map/ppermute | solution.py:50
  60.8 11.2 %copy-start.1 = (s32[256,1]{0,1:T(1,128)S(1)}, s32[256,1]{0,1:T(1,128)}, u32[]{:S(2)}) copy-start(s32[256,1]{0,1:T(1,128)} %param.15) | copy-start | bytes 3076
